TPU v7x, 32 devices: a whole 2x2x4 slice. The times are simulated.
32 devices in a mesh: seq: 16 (over z, y, x), head: 2 (over core).
Axes of the slice: x: 2, y: 2, z: 4, core: 2. Of those that a mesh axis runs over, the one named last changes fastest.
Arguments:
- query_rows: bfloat16 [16384, 1536], P(('seq', 'head')), may hold values from -150 to 150
- key_rows: bfloat16 [16384, 1536], P(('seq', 'head')), may hold values from -4 to 4
- value_rows: bfloat16 [16384, 1536], P(('seq', 'head')), may hold values from -6 to 6
- out_grad: bfloat16 [16384, 1536], P(('seq', 'head')), may hold values from -180 to 180
- key_blocks: int32 [32, 3], replicated, may hold values from 0 to 31, as said below
- block_counts: int32 [32], replicated, may hold values from 1 to 3
Outputs:
- query_grad: bfloat16 [16384, 1536], P(('seq', 'head'))
- key_grad: bfloat16 [16384, 1536], P(('seq', 'head'))
- value_grad: bfloat16 [16384, 1536], P(('seq', 'head'))
Inputs may be any that keep to these rules, and one draw needn't show every extreme that they name: `key_blocks`: row b lists 3 different key blocks; its first entry is b itself and the others lie within 2 blocks of b.
All inputs are finite; a program needn't handle non-finite values.
Results may differ from a plain program's by a relative error of at most 0.0051.
Values may be sent and summed in bfloat16 or wider, within the bound.
No kernel may reach another device: no remote copies, remote signals or barrier semaphores. Data moves between devices by JAX's collectives and lax.ppermute only.
A program may use at most 192 MiB of HBM per device.

v0:
```python
from functools import reduce

import jax
import jax.numpy as jnp
from jax import lax
from jax.sharding import PartitionSpec as P

HEADS = 12
HEAD_DIM = 128
BLOCK = 512
RADIUS = 2
MAXK = 3


def from_behind(shard, axis, by):
    count = lax.axis_size(axis)
    pairs = [(i, i + by) for i in range(count) if 0 <= i + by < count]
    return lax.ppermute(shard, axis, pairs)


def pair_scores(left, right):
    return lax.dot_general(
        left, right, (((1,), (1,)), ((), ())), preferred_element_type=jnp.float32
    )


def column_sums(left, right):
    return lax.dot_general(
        left, right, (((0,), (0,)), ((), ())), preferred_element_type=jnp.float32
    )


def owner_pair(
    query_window,
    grad_window,
    log_window,
    delta_window,
    query_start,
    key_block,
    value_block,
    score_scale,
):
    query_block = lax.dynamic_slice_in_dim(query_window, query_start, BLOCK, 0)
    grad_block = lax.dynamic_slice_in_dim(grad_window, query_start, BLOCK, 0)
    log_part = lax.dynamic_slice_in_dim(log_window, query_start, BLOCK, 0)
    delta_part = lax.dynamic_slice_in_dim(delta_window, query_start, BLOCK, 0)
    scores = pair_scores(query_block, key_block) * score_scale
    weights = jnp.exp(scores - log_part[:, None])
    weight_grads = pair_scores(grad_block, value_block)
    score_low = (weights * (weight_grads - delta_part[:, None])).astype(jnp.bfloat16)
    return (
        column_sums(score_low, query_block) * score_scale,
        column_sums(weights.astype(jnp.bfloat16), grad_block),
    )


def shards(query_rows, key_rows, value_rows, out_grad, key_blocks, block_counts):
    shard_rows = query_rows.shape[0]
    score_scale = HEAD_DIM ** (-0.5)

    def by_heads(matrix):
        return matrix.reshape(shard_rows, HEADS, HEAD_DIM)

    regrouped = (
        lax.all_to_all(by_heads(query_rows), "head", split_axis=1, concat_axis=0, tiled=True),
        lax.all_to_all(by_heads(key_rows), "head", split_axis=1, concat_axis=0, tiled=True),
        lax.all_to_all(by_heads(value_rows), "head", split_axis=1, concat_axis=0, tiled=True),
        lax.all_to_all(by_heads(out_grad), "head", split_axis=1, concat_axis=0, tiled=True),
    )
    query_heads, key_heads, value_heads, grad_heads = [
        jnp.transpose(member, (1, 0, 2)) for member in regrouped
    ]
    span_rows = query_heads.shape[1]
    blocks_here = span_rows // BLOCK
    block_total = key_blocks.shape[0]
    seq_index = lax.axis_index("seq")
    window_first = (seq_index - 1) * blocks_here
    slot_range = jnp.arange(MAXK, dtype=jnp.int32)
    fetched = {}
    for shift_step in (1, -1):
        fetched[shift_step] = from_behind((key_heads, value_heads), "seq", shift_step)
    key_window = jnp.concatenate([fetched[1][0], key_heads, fetched[-1][0]], axis=1)
    value_window = jnp.concatenate([fetched[1][1], value_heads, fetched[-1][1]], axis=1)
    plans = []
    for block_index in range(blocks_here):
        global_block = seq_index * blocks_here + block_index
        listed_blocks = lax.dynamic_index_in_dim(key_blocks, global_block, 0, keepdims=False)
        live_count = lax.dynamic_index_in_dim(block_counts, global_block, 0, keepdims=False)
        plans.append(((listed_blocks - window_first) * BLOCK, slot_range < live_count))

    def query_side(members):
        query_one, grad_one, key_one, value_one = members
        window_rows = key_one.shape[0]
        key_acc = jnp.zeros((window_rows, HEAD_DIM), jnp.float32)
        value_acc = jnp.zeros((window_rows, HEAD_DIM), jnp.float32)
        query_parts = []
        log_parts = []
        delta_parts = []
        for block_index in range(blocks_here):
            starts, live_slots = plans[block_index]
            query_block = query_one[block_index * BLOCK : (block_index + 1) * BLOCK]
            grad_block = grad_one[block_index * BLOCK : (block_index + 1) * BLOCK]
            key_list = [
                lax.dynamic_slice_in_dim(key_one, starts[slot_index], BLOCK, 0)
                for slot_index in range(MAXK)
            ]
            value_list = [
                lax.dynamic_slice_in_dim(value_one, starts[slot_index], BLOCK, 0)
                for slot_index in range(MAXK)
            ]
            scores = [pair_scores(query_block, member) * score_scale for member in key_list]
            row_peak = reduce(
                jnp.maximum,
                [
                    jnp.where(live_slots[slot_index], jnp.max(scores[slot_index], axis=1), -jnp.inf)
                    for slot_index in range(MAXK)
                ],
            )
            row_total = reduce(
                jnp.add,
                [
                    jnp.where(
                        live_slots[slot_index],
                        jnp.sum(jnp.exp(scores[slot_index] - row_peak[:, None]), axis=1),
                        0.0,
                    )
                    for slot_index in range(MAXK)
                ],
            )
            log_total = row_peak + jnp.log(row_total)
            weights = [
                jnp.exp(scores[slot_index] - log_total[:, None])
                * live_slots[slot_index].astype(jnp.float32)
                for slot_index in range(MAXK)
            ]
            weight_grads = [pair_scores(grad_block, member) for member in value_list]
            row_delta = reduce(
                jnp.add,
                [
                    jnp.sum(weights[slot_index] * weight_grads[slot_index], axis=1)
                    for slot_index in range(MAXK)
                ],
            )
            query_acc = jnp.zeros((BLOCK, HEAD_DIM), jnp.float32)
            for slot_index in range(MAXK):
                score_low = (
                    weights[slot_index] * (weight_grads[slot_index] - row_delta[:, None])
                ).astype(jnp.bfloat16)
                query_acc = query_acc + jnp.dot(
                    score_low, key_list[slot_index], preferred_element_type=jnp.float32
                )
            query_parts.append(query_acc * score_scale)
            log_parts.append(log_total)
            delta_parts.append(row_delta)
        return (
            jnp.concatenate(query_parts, axis=0),
            key_acc,
            value_acc,
            jnp.concatenate(log_parts),
            jnp.concatenate(delta_parts),
        )

    query_heads_grad, key_window_grad, value_window_grad, log_all, delta_all = lax.map(
        query_side, (query_heads, grad_heads, key_window, value_window)
    )
    sent_rows = {}
    sent_stats = {}
    for shift_step in (1, -1):
        sent_rows[shift_step] = from_behind((query_heads, grad_heads), "seq", shift_step)
        sent_stats[shift_step] = from_behind((log_all, delta_all), "seq", shift_step)
    query_window = jnp.concatenate([sent_rows[1][0], query_heads, sent_rows[-1][0]], axis=1)
    grad_window = jnp.concatenate([sent_rows[1][1], grad_heads, sent_rows[-1][1]], axis=1)
    log_window = jnp.concatenate([sent_stats[1][0], log_all, sent_stats[-1][0]], axis=1)
    delta_window = jnp.concatenate([sent_stats[1][1], delta_all, sent_stats[-1][1]], axis=1)
    owner_plans = []
    for block_index in range(blocks_here):
        key_global = seq_index * blocks_here + block_index
        entries_here = []
        for relative in range(-RADIUS, RADIUS + 1):
            query_global = key_global + relative
            inside = (query_global >= 0) & (query_global < block_total)
            clipped = jnp.clip(query_global, 0, block_total - 1)
            entries = lax.dynamic_index_in_dim(key_blocks, clipped, 0, keepdims=False)
            live_slots = slot_range < lax.dynamic_index_in_dim(
                block_counts, clipped, 0, keepdims=False
            )
            listed = jnp.any((entries == key_global) & live_slots) & inside
            query_start = jnp.clip(clipped - window_first, 0, 3 * blocks_here - 1) * BLOCK
            entries_here.append((query_start, listed))
        owner_plans.append(entries_here)

    def owner_side(members):
        key_one, value_one, query_win, grad_win, log_win, delta_win = members
        key_parts = []
        value_parts = []
        for block_index in range(blocks_here):
            key_block = key_one[block_index * BLOCK : (block_index + 1) * BLOCK]
            value_block = value_one[block_index * BLOCK : (block_index + 1) * BLOCK]
            key_acc = jnp.zeros((BLOCK, HEAD_DIM), jnp.float32)
            value_acc = jnp.zeros((BLOCK, HEAD_DIM), jnp.float32)
            for query_start, listed in owner_plans[block_index]:
                add_key, add_value = lax.cond(
                    listed,
                    lambda unused, start_row=query_start, key_here=key_block, value_here=value_block: owner_pair(
                        query_win,
                        grad_win,
                        log_win,
                        delta_win,
                        start_row,
                        key_here,
                        value_here,
                        score_scale,
                    ),
                    lambda unused: (
                        jnp.zeros((BLOCK, HEAD_DIM), jnp.float32),
                        jnp.zeros((BLOCK, HEAD_DIM), jnp.float32),
                    ),
                    0,
                )
                key_acc = key_acc + add_key
                value_acc = value_acc + add_value
            key_parts.append(key_acc)
            value_parts.append(value_acc)
        return (jnp.concatenate(key_parts, axis=0), jnp.concatenate(value_parts, axis=0))

    key_heads_grad, value_heads_grad = lax.map(
        owner_side, (key_heads, value_heads, query_window, grad_window, log_window, delta_window)
    )

    def token_major(stacked):
        return jnp.transpose(stacked, (1, 0, 2)).astype(jnp.bfloat16)

    returned = (
        lax.all_to_all(
            token_major(query_heads_grad), "head", split_axis=0, concat_axis=1, tiled=True
        ),
        lax.all_to_all(
            token_major(key_heads_grad), "head", split_axis=0, concat_axis=1, tiled=True
        ),
        lax.all_to_all(
            token_major(value_heads_grad), "head", split_axis=0, concat_axis=1, tiled=True
        ),
    )
    query_grad, key_grad, value_grad = [
        member.reshape(shard_rows, HEADS * HEAD_DIM) for member in returned
    ]
    return (query_grad, key_grad, value_grad)


def solution(mesh):
    return jax.shard_map(
        shards,
        mesh=mesh,
        in_specs=(
            P(("seq", "head"), None),
            P(("seq", "head"), None),
            P(("seq", "head"), None),
            P(("seq", "head"), None),
            P(),
            P(),
        ),
        out_specs=(P(("seq", "head"), None), P(("seq", "head"), None), P(("seq", "head"), None)),
        check_vma=False,
    )
```

profile of v0, /device:TPU:9, one launch (start us, length us, event | category | flops | bytes accessed | tf_op | source)
XLA Modules:
  0.0 770.6 jit_solution(12870564413274391583)
XLA Ops:
  2.4 5.3 all_to_all.117
  8.6 4.0 collective-permute-start.1
  16.2 6.2 all_to_all.118
  24.3 5.4 collective-permute-start.3
  34.3 5.3 all-to-all-start
  42.1 4.7 all-to-all-start.2
  49.4 5.4 collective-permute-start.5
  89.8 59.0 %collective-permute-done = bf16[6,1024,128]{2,1,0:T(8,128)(2,1)} collective-permute-done((bf16[6,1024,128]{2,1,0:T(8,128)(2,1)S(1)}, bf16[6,1024,128]{2,1,0:T(8,128)(2,1)}, u32[]{:S(2)}, u32[]{:S(2)}) %collective-permute-start) | collective-permute-done | bytes 1572896 | tf_op jit(solution)/shard_map/ppermute | solution.py:18
  154.4 4.9 collective-permute-start.6
  159.3 23.2 %collective-permute-done.2 = bf16[6,1024,128]{2,1,0:T(8,128)(2,1)} collective-permute-done((bf16[6,1024,128]{2,1,0:T(8,128)(2,1)S(1)}, bf16[6,1024,128]{2,1,0:T(8,128)(2,1)}, u32[]{:S(2)}, u32[]{:S(2)}) %collective-permute-start.2) | collective-permute-done | bytes 1572896 | tf_op jit(solution)/shard_map/ppermute | solution.py:18
  182.5 3.7 pad_maximum_fusion.3
  187.5 265.3 %while.32 = (s32[]{:T(128)}, bf16[6,1024,128]{2,1,0:T(8,128)(2,1)}, f32[6,1024]{1,0:T(8,128)S(1)}, f32[6,1024]{1,0:T(8,128)S(1)}, bf16[6,1024,128]{2,1,0:T(8,128...) while((s32[]{:T(128)}, bf16[6,1024,128]{2,1,0:T(8,128)(2,1)}, ...), condition=%wide.region_19.20_spmd, body=%wide.region_0.19_spmd.sunk | while | flops 1229461504 | bytes 65701448 | solution.py:163
  452.9 3.8 copy.77
  456.7 4.3 all-to-all-start.4
  462.9 40.4 %collective-permute-start.8 = (f32[6,1024]{1,0:T(8,128)S(1)}, f32[6,1024]{1,0:T(8,128)S(1)}, u32[]{:S(2)}, u32[]{:S(2)}) collective-permute-start(f32[6,1024]{1,0:T(8,128)S(1)} %get-tuple-element.866), channel_id=1, source_target_pairs={{0,2},{2,4},{4,6},{6,8},{8,10},{10,12},{12,14},{14,16},{16,18},{18... | collective-permute-start | bytes 73736 | tf_op jit(solution)/shard_map/ppermute | solution.py:18
  505.3 3.9 pad_maximum_fusion.4
  509.2 4.2 collective-permute-start.10
  513.5 4.0 pad_maximum_fusion.5
  525.1 220.5 %while.33 = (s32[]{:T(128)}, bf16[6,1024,128]{2,1,0:T(8,128)(2,1)}, bf16[6,1024,128]{2,1,0:T(8,128)(2,1)}, pred[]{:T(512)}, bf16[6,3072,128]{2,1,0:T(8,128)(2,1)...) while((s32[]{:T(128)}, bf16[6,1024,128]{2,1,0:T(8,128)(2,1)}, ...), condition=%wide.region_51.52_spmd, body=%wide.region_30.51_spmd.sunk | while | flops 2703097856 | bytes 56987304 | solution.py:226
  545.5 3.7 conditional.27
  552.9 3.7 conditional.29
  582.3 3.7 conditional.27
  589.6 3.7 conditional.29
  622.7 3.7 conditional.28
  626.4 3.7 conditional.29
  655.8 3.7 conditional.27
  663.1 3.7 conditional.29
  699.9 3.7 conditional.29
  729.3 3.7 conditional.27
  736.6 3.7 conditional.29
  748.1 5.9 all_to_all.119
  760.2 5.4 all_to_all.120
  (730 shorter events, 651.6 us)
Async XLA Ops:
  8.6 142.1 %copy-start.4 = (bf16[2,512,6,128]{3,1,0,2:T(8,128)(2,1)}, bf16[2,512,6,128]{3,1,0,2:T(8,128)(2,1)S(1)}, u32[]{:S(2)}) copy-start(bf16[2,512,6,128]{3,1,0,2:T(8,128)(2,1)S(1)} %copy.70) | copy-start | bytes 4718596
  8.6 79.3 %collective-permute-start.1 = (bf16[6,1024,128]{2,1,0:T(8,128)(2,1)S(1)}, bf16[6,1024,128]{2,1,0:T(8,128)(2,1)}, u32[]{:S(2)}, u32[]{:S(2)}) collective-permute-start(bf16[6,1024,128]{2,1,0:T(8,128)(2,1)S(1)} %bitcast.307), channel_id=1, source_target_pairs={{2,0},{4,2},{6,4},{8,6},{10,8},{12,10},{14,12},{16,14},{18,16},{20... | collective-permute-start | bytes 4718600 | tf_op jit(solution)/shard_map/ppermute | solution.py:18
  12.5 136.2 %collective-permute-start = (bf16[6,1024,128]{2,1,0:T(8,128)(2,1)S(1)}, bf16[6,1024,128]{2,1,0:T(8,128)(2,1)}, u32[]{:S(2)}, u32[]{:S(2)}) collective-permute-start(bf16[6,1024,128]{2,1,0:T(8,128)(2,1)S(1)} %bitcast.308), channel_id=1, source_target_pairs={{0,2},{2,4},{4,6},{6,8},{8,10},{10,12},{12,14},{14,16},{16,18},{18... | collective-permute-start | bytes 4718600 | tf_op jit(solution)/shard_map/ppermute | solution.py:18
  24.3 158.2 %copy-start.5 = (bf16[2,512,6,128]{3,1,0,2:T(8,128)(2,1)}, bf16[2,512,6,128]{3,1,0,2:T(8,128)(2,1)S(1)}, u32[]{:S(2)}) copy-start(bf16[2,512,6,128]{3,1,0,2:T(8,128)(2,1)S(1)} %copy.76) | copy-start | bytes 4718596
  24.3 130.1 %collective-permute-start.3 = (bf16[6,1024,128]{2,1,0:T(8,128)(2,1)S(1)}, bf16[6,1024,128]{2,1,0:T(8,128)(2,1)}, u32[]{:S(2)}, u32[]{:S(2)}) collective-permute-start(bf16[6,1024,128]{2,1,0:T(8,128)(2,1)S(1)} %bitcast.311), channel_id=1, source_target_pairs={{2,0},{4,2},{6,4},{8,6},{10,8},{12,10},{14,12},{16,14},{18,16},{20... | collective-permute-start | bytes 4718600 | tf_op jit(solution)/shard_map/ppermute | solution.py:18
  29.7 152.7 %collective-permute-start.2 = (bf16[6,1024,128]{2,1,0:T(8,128)(2,1)S(1)}, bf16[6,1024,128]{2,1,0:T(8,128)(2,1)}, u32[]{:S(2)}, u32[]{:S(2)}) collective-permute-start(bf16[6,1024,128]{2,1,0:T(8,128)(2,1)S(1)} %bitcast.312), channel_id=1, source_target_pairs={{0,2},{2,4},{4,6},{6,8},{8,10},{10,12},{12,14},{14,16},{16,18},{18... | collective-permute-start | bytes 4718600 | tf_op jit(solution)/shard_map/ppermute | solution.py:18
  34.3 7.8 %all-to-all-start = ((bf16[512,12,128]{0,2,1:T(8,128)(2,1)}), bf16[512,12,128]{0,2,1:T(8,128)(2,1)}, u32[]{:S(2)}, u32[]{:S(2)}) async-start(bf16[512,12,128]{0,2,1:T(8,128)(2,1)} %bitcast.322), calls=%async_computation | async-start | bytes 3145728 | tf_op jit(solution)/shard_map/all_to_all | solution.py:65
  42.1 22.8 %all-to-all-start.2 = ((bf16[512,12,128]{0,2,1:T(8,128)(2,1)}), bf16[512,12,128]{0,2,1:T(8,128)(2,1)}, u32[]{:S(2)}, u32[]{:S(2)}) async-start(bf16[512,12,128]{0,2,1:T(8,128)(2,1)} %bitcast.318), calls=%async_computation.2 | async-start | bytes 3145728 | tf_op jit(solution)/shard_map/all_to_all | solution.py:68
  46.8 8.1 %copy-start.12 = (s32[32,3]{0,1:T(4,128)S(1)}, s32[32,3]{0,1:T(4,128)}, u32[]{:S(2)}) copy-start(s32[32,3]{0,1:T(4,128)} %param.34) | copy-start | bytes 1156
  49.4 413.5 %collective-permute-start.5 = (bf16[6,1024,128]{2,1,0:T(8,128)(2,1)}, bf16[6,1024,128]{2,1,0:T(8,128)(2,1)}, u32[]{:S(2)}, u32[]{:S(2)}) collective-permute-start(bf16[6,1024,128]{2,1,0:T(8,128)(2,1)} %bitcast.40), channel_id=1, source_target_pairs={{2,0},{4,2},{6,4},{8,6},{10,8},{12,10},{14,12},{16,14},{18,16},{20... | collective-permute-start | bytes 4718600 | tf_op jit(solution)/shard_map/ppermute | solution.py:18
  64.9 4.5 copy-start.13
  87.9 415.5 %collective-permute-start.4 = (bf16[6,1024,128]{2,1,0:T(8,128)(2,1)}, bf16[6,1024,128]{2,1,0:T(8,128)(2,1)}, u32[]{:S(2)}, u32[]{:S(2)}) collective-permute-start(bf16[6,1024,128]{2,1,0:T(8,128)(2,1)} %bitcast.40), channel_id=1, source_target_pairs={{0,2},{2,4},{4,6},{6,8},{8,10},{10,12},{12,14},{14,16},{16,18},{18... | collective-permute-start | bytes 4718600 | tf_op jit(solution)/shard_map/ppermute | solution.py:18
  148.8 360.4 %collective-permute-start.7 = (bf16[6,1024,128]{2,1,0:T(8,128)(2,1)}, bf16[6,1024,128]{2,1,0:T(8,128)(2,1)}, u32[]{:S(2)}, u32[]{:S(2)}) collective-permute-start(bf16[6,1024,128]{2,1,0:T(8,128)(2,1)} %bitcast.57), channel_id=1, source_target_pairs={{2,0},{4,2},{6,4},{8,6},{10,8},{12,10},{14,12},{16,14},{18,16},{20... | collective-permute-start | bytes 4718600 | tf_op jit(solution)/shard_map/ppermute | solution.py:18
  154.4 359.1 %collective-permute-start.6 = (bf16[6,1024,128]{2,1,0:T(8,128)(2,1)}, bf16[6,1024,128]{2,1,0:T(8,128)(2,1)}, u32[]{:S(2)}, u32[]{:S(2)}) collective-permute-start(bf16[6,1024,128]{2,1,0:T(8,128)(2,1)} %bitcast.57), channel_id=1, source_target_pairs={{0,2},{2,4},{4,6},{6,8},{8,10},{10,12},{12,14},{14,16},{16,18},{18... | collective-permute-start | bytes 4718600 | tf_op jit(solution)/shard_map/ppermute | solution.py:18
  456.7 60.7 %all-to-all-start.4 = ((bf16[1024,6,128]{2,1,0:T(8,128)(2,1)}), bf16[1024,6,128]{2,1,0:T(8,128)(2,1)S(1)}, u32[]{:S(2)}, u32[]{:S(2)}) async-start(bf16[1024,6,128]{2,1,0:T(8,128)(2,1)} %copy.77), calls=%async_computation.4 | async-start | bytes 4194304 | tf_op jit(solution)/shard_map/all_to_all | solution.py:234
  461.0 61.4 %collective-permute-start.9 = (f32[6,1024]{1,0:T(8,128)S(1)}, f32[6,1024]{1,0:T(8,128)S(1)}, u32[]{:S(2)}, u32[]{:S(2)}) collective-permute-start(f32[6,1024]{1,0:T(8,128)S(1)} %get-tuple-element.866), channel_id=1, source_target_pairs={{2,0},{4,2},{6,4},{8,6},{10,8},{12,10},{14,12},{16,14},{18,16},{20... | collective-permute-start | bytes 73736 | tf_op jit(solution)/shard_map/ppermute | solution.py:18
  462.9 59.5 %collective-permute-start.8 = (f32[6,1024]{1,0:T(8,128)S(1)}, f32[6,1024]{1,0:T(8,128)S(1)}, u32[]{:S(2)}, u32[]{:S(2)}) collective-permute-start(f32[6,1024]{1,0:T(8,128)S(1)} %get-tuple-element.866), channel_id=1, source_target_pairs={{0,2},{2,4},{4,6},{6,8},{8,10},{10,12},{12,14},{14,16},{16,18},{18... | collective-permute-start | bytes 73736 | tf_op jit(solution)/shard_map/ppermute | solution.py:18
  503.4 19.0 %collective-permute-start.11 = (f32[6,1024]{1,0:T(8,128)S(1)}, f32[6,1024]{1,0:T(8,128)S(1)}, u32[]{:S(2)}, u32[]{:S(2)}) collective-permute-start(f32[6,1024]{1,0:T(8,128)S(1)} %get-tuple-element.867), channel_id=1, source_target_pairs={{2,0},{4,2},{6,4},{8,6},{10,8},{12,10},{14,12},{16,14},{18,16},{20... | collective-permute-start | bytes 73736 | tf_op jit(solution)/shard_map/ppermute | solution.py:18
  509.2 13.2 %collective-permute-start.10 = (f32[6,1024]{1,0:T(8,128)S(1)}, f32[6,1024]{1,0:T(8,128)S(1)}, u32[]{:S(2)}, u32[]{:S(2)}) collective-permute-start(f32[6,1024]{1,0:T(8,128)S(1)} %get-tuple-element.867), channel_id=1, source_target_pairs={{0,2},{2,4},{4,6},{6,8},{8,10},{10,12},{12,14},{14,16},{16,18},{18... | collective-permute-start | bytes 73736 | tf_op jit(solution)/shard_map/ppermute | solution.py:18
  527.9 9.7 %copy-start.7 = (f32[1,3072]{1,0:T(1,128)}, f32[1,3072]{1,0:T(1,128)S(1)}, u32[]{:S(2)}) copy-start(f32[1,3072]{1,0:T(1,128)S(1)} %get-tuple-element.1392) | copy-start | bytes 36868 | tf_op jit(solution)/shard_map/while
  564.6 9.7 %copy-start.7 = (f32[1,3072]{1,0:T(1,128)}, f32[1,3072]{1,0:T(1,128)S(1)}, u32[]{:S(2)}) copy-start(f32[1,3072]{1,0:T(1,128)S(1)} %get-tuple-element.1392) | copy-start | bytes 36868 | tf_op jit(solution)/shard_map/while
  595.3 3.4 copy-start.9
  595.3 3.4 copy-start.11
  601.4 9.7 %copy-start.7 = (f32[1,3072]{1,0:T(1,128)}, f32[1,3072]{1,0:T(1,128)S(1)}, u32[]{:S(2)}) copy-start(f32[1,3072]{1,0:T(1,128)S(1)} %get-tuple-element.1392) | copy-start | bytes 36868 | tf_op jit(solution)/shard_map/while
  632.0 3.4 copy-start.11
  638.2 9.7 %copy-start.7 = (f32[1,3072]{1,0:T(1,128)}, f32[1,3072]{1,0:T(1,128)S(1)}, u32[]{:S(2)}) copy-start(f32[1,3072]{1,0:T(1,128)S(1)} %get-tuple-element.1392) | copy-start | bytes 36868 | tf_op jit(solution)/shard_map/while
  674.9 9.7 %copy-start.7 = (f32[1,3072]{1,0:T(1,128)}, f32[1,3072]{1,0:T(1,128)S(1)}, u32[]{:S(2)}) copy-start(f32[1,3072]{1,0:T(1,128)S(1)} %get-tuple-element.1392) | copy-start | bytes 36868 | tf_op jit(solution)/shard_map/while
  705.5 3.4 copy-start.9
  705.5 3.4 copy-start.11
  711.7 9.7 %copy-start.7 = (f32[1,3072]{1,0:T(1,128)}, f32[1,3072]{1,0:T(1,128)S(1)}, u32[]{:S(2)}) copy-start(f32[1,3072]{1,0:T(1,128)S(1)} %get-tuple-element.1392) | copy-start | bytes 36868 | tf_op jit(solution)/shard_map/while
  742.3 3.4 copy-start.9
  742.3 3.4 copy-start.11
  (42 other events, 100.2 us)
where the time goes:
time: 765 us; the launch traced here: 771 us
  matrix products  304 us (40%)
  other arithmetic  120 us (16%)
  local copies, waits for them, and re-layouts  107 us (14%)
  starting transfers between devices  90.2 us (12%)
  waiting for transfers between devices  82.1 us (11%)
  loops' own time  25 us (3%)
  blocking collectives  22.8 us (3%)
  between operations  18.8 us (2%)
    dot_general x120, matrix products, pair_scores(): lax.dot_general(left, right, (((1,), (1,)), ((), ())), preferred_element_...  146 us
    dot_general x96, matrix products, column_sums(): lax.dot_general(left, right, (((0,), (0,)), ((), ())), preferred_element_...  106 us
    ppermute x12, waiting for transfers between devices, from_behind(): return lax.ppermute(shard, axis, pairs)  82.1 us
    ppermute x12, starting transfers between devices, from_behind(): return lax.ppermute(shard, axis, pairs)  76 us
    dot_general x36, matrix products, query_side(): jnp.dot(score_low, key_list[slot_index], preferred_element_type=jnp.float32)  51.7 us
    another operation x1, loops' own time, shards(): lax.map(query_side, (query_heads, grad_heads, key_window, value_window))  23.6 us
    add x12, other arithmetic, query_side(): log_total = row_peak + jnp.log(row_total)  22.2 us
    max x12, other arithmetic, query_side(): reduce(jnp.maximum, [jnp.where(live_slots[slot_index], jnp.max(scores[slo...  22.1 us
  transfers between devices with their start and end apart: 15, of which 2 were waited for; matrix products, arithmetic and copies ran while one was open for 38% of the time, Pallas kernels for 0%

commit v1 on v0

v1 whole, which is shorter than its diff:
```python
import functools
import math

import jax
import jax.numpy as jnp
from jax import lax
from jax.experimental import pallas as pl
from jax.experimental.pallas import tpu as pltpu
from jax.sharding import PartitionSpec as P

HEADS = 12
HEAD_DIM = 128
BLOCK = 512
MAXK = 3
CHUNKS = (1, 1, 1, 1, 1, 1)
SCALE = HEAD_DIM ** -0.5
LOG_SCALE = SCALE * math.log2(math.e)
LOWEST = -1e30
VMEM_LIMIT = 40 * 1024 * 1024


def pair_rows(left, right):
    return lax.dot_general(
        left, right, (((1,), (1,)), ((), ())), preferred_element_type=jnp.float32
    )


def product(left, right):
    return jnp.dot(left, right, preferred_element_type=jnp.float32)


def is_live(place, lists, counts, query, key):
    chip, core, chips = place[0], place[1], place[2]
    odd = chip & 1
    origin, slot = query >> 1, query & 1
    step = jnp.where(origin == 1, 1 - 2 * odd, 2 * odd - 1)
    source = chip + jnp.where(origin == 0, 0, step)
    inside = (source >= 0) & (source < chips)
    query_block = 2 * jnp.clip(source, 0, chips - 1) + (core ^ slot)
    key_block = 2 * chip + (core ^ key)
    count = counts[query_block]
    found = lists[query_block * MAXK] == key_block
    for at in range(1, MAXK):
        found = found | ((lists[query_block * MAXK + at] == key_block) & (at < count))
    return found & inside


def for_live_pairs(scalars, first, last, step):
    place, lists, counts = scalars

    def candidate(index, carry):
        query, key = index >> 1, index & 1

        @pl.when(is_live(place, lists, counts, query, key))
        def _():
            step(query, key)

        return carry

    lax.fori_loop(2 * first, 2 * last, candidate, 0)


def fetch(copies, sem):
    started = [
        pltpu.make_async_copy(source, target, sem.at[at])
        for at, (source, target) in enumerate(copies)
    ]
    for copy in started:
        copy.start()
    for copy in started:
        copy.wait()


def key_copies(place, keys, lane, width, key_buf, value_buf):
    key_mine, key_other, value_mine, value_other = keys
    half = key_other.shape[1]
    own_columns = pl.ds(pl.multiple_of(place[1] * half + lane, HEAD_DIM), width)
    far_columns = pl.ds(lane, width)
    return [
        (key_mine.at[:, own_columns], key_buf.at[0]),
        (key_other.at[:, far_columns], key_buf.at[1]),
        (value_mine.at[:, own_columns], value_buf.at[0]),
        (value_other.at[:, far_columns], value_buf.at[1]),
    ]


def stats_step(heads, base, key_buf, value_buf, rows_buf, stats_ref):
    def step(query, key):
        for head in range(heads):
            lanes = slice(head * HEAD_DIM, (head + 1) * HEAD_DIM)
            at = query - base
            scores = pair_rows(key_buf[key, :, lanes], rows_buf[at, 0, :, lanes])
            weight_grads = pair_rows(value_buf[key, :, lanes], rows_buf[at, 1, :, lanes])
            peak_here = jnp.max(scores, axis=0, keepdims=True) * LOG_SCALE
            grown = jnp.exp2(scores * LOG_SCALE - peak_here)
            total_here = jnp.sum(grown, axis=0, keepdims=True)
            delta_here = jnp.sum(grown * weight_grads, axis=0, keepdims=True)
            row = 3 * head
            peak = stats_ref[at, row : row + 1, :]
            new_peak = jnp.maximum(peak, peak_here)
            keep = jnp.exp2(peak - new_peak)
            add = jnp.exp2(peak_here - new_peak)
            stats_ref[at, row : row + 1, :] = new_peak
            stats_ref[at, row + 1 : row + 2, :] = (
                stats_ref[at, row + 1 : row + 2, :] * keep + total_here * add
            )
            stats_ref[at, row + 2 : row + 3, :] = (
                stats_ref[at, row + 2 : row + 3, :] * keep + delta_here * add
            )

    return step


def clear_stats(heads, slots, stats_ref):
    stats_ref[slots] = jnp.zeros_like(stats_ref[slots])
    for head in range(heads):
        stats_ref[slots, 3 * head : 3 * head + 1, :] = jnp.full(
            (slots.stop - slots.start, 1, BLOCK), LOWEST, jnp.float32
        )


def near_stats_kernel(
    heads, lane, place, lists, counts, km, ko, vm, vo, pm, po, xm, xo, stats, key_buf, value_buf, rows_buf, sem
):
    width = heads * HEAD_DIM
    fetch(
        key_copies(place, (km, ko, vm, vo), lane, width, key_buf, value_buf)
        + [(member, rows_buf.at[at]) for at, member in enumerate((pm, po, xm, xo))],
        sem,
    )
    clear_stats(heads, slice(0, 4), stats)
    step = stats_step(heads, 0, key_buf, value_buf, rows_buf, stats)
    for_live_pairs((place, lists, counts), 0, 4, step)


def far_stats_kernel(
    heads, lane, place, lists, counts, km, ko, vm, vo, ym, yo, near, stats, key_buf, value_buf, rows_buf, sem
):
    width = heads * HEAD_DIM
    fetch(
        key_copies(place, (km, ko, vm, vo), lane, width, key_buf, value_buf)
        + [(member, rows_buf.at[at]) for at, member in enumerate((ym, yo))]
        + [(near.at[pl.ds(0, 2)], stats.at[pl.ds(2, 2)])],
        sem,
    )
    clear_stats(heads, slice(0, 2), stats)
    step = stats_step(heads, 4, key_buf, value_buf, rows_buf, stats)
    for_live_pairs((place, lists, counts), 4, 6, step)


def merged(parts, slot, head):
    row = 3 * head
    peaks, totals, deltas = [], [], []
    for ref, base in parts:
        total = ref[base + slot, row + 1 : row + 2, :]
        peaks.append(jnp.where(total > 0.0, ref[base + slot, row : row + 1, :], LOWEST))
        totals.append(total)
        deltas.append(ref[base + slot, row + 2 : row + 3, :])
    peak = functools.reduce(jnp.maximum, peaks)
    factors = [jnp.exp2(member - peak) for member in peaks]
    total = sum(factor * member for factor, member in zip(factors, totals))
    delta = sum(factor * member for factor, member in zip(factors, deltas))
    return peak + jnp.log2(total), delta / total


def grads_kernel(
    heads, lane, place, lists, counts, km, ko, vm, vo, pm, po, xm, xo, ym, yo,
    near, far, from_partner, from_relay, from_other, from_end,
    own_out, partner_out, relayed_out, key_out, value_out,
    key_buf, value_buf, rows_buf, near_buf, far_buf, partner_buf, relay_buf, other_buf, end_buf,
    log_buf, query_acc, key_acc, value_acc, sem,
):
    width = heads * HEAD_DIM
    fetch(
        key_copies(place, (km, ko, vm, vo), lane, width, key_buf, value_buf)
        + [(member, rows_buf.at[at]) for at, member in enumerate((pm, po, xm, xo, ym, yo))]
        + [
            (near, near_buf),
            (far, far_buf),
            (from_partner, partner_buf),
            (from_relay, relay_buf),
            (from_other, other_buf),
            (from_end, end_buf),
        ],
        sem,
    )
    groups = (
        ((near_buf, 0), (partner_buf, 2), (other_buf, 0)),
        ((near_buf, 2), (partner_buf, 0), (end_buf, 0)),
        ((far_buf, 0), (other_buf, 2), (relay_buf, 2)),
    )
    for origin, parts in enumerate(groups):
        for slot in range(2):
            for head in range(heads):
                log_total, delta = merged(parts, slot, head)
                log_buf[2 * origin + slot, 2 * head : 2 * head + 1, :] = log_total
                log_buf[2 * origin + slot, 2 * head + 1 : 2 * head + 2, :] = delta
    query_acc[...] = jnp.zeros_like(query_acc)
    key_acc[...] = jnp.zeros_like(key_acc)
    value_acc[...] = jnp.zeros_like(value_acc)

    def step(query, key):
        for head in range(heads):
            lanes = slice(head * HEAD_DIM, (head + 1) * HEAD_DIM)
            key_block = key_buf[key, :, lanes]
            query_block = rows_buf[query, 0, :, lanes]
            grad_block = rows_buf[query, 1, :, lanes]
            scores = pair_rows(key_block, query_block)
            weights = jnp.exp2(scores * LOG_SCALE - log_buf[query, 2 * head : 2 * head + 1, :])
            weight_grads = pair_rows(value_buf[key, :, lanes], grad_block)
            score_low = (
                weights * (weight_grads - log_buf[query, 2 * head + 1 : 2 * head + 2, :])
            ).astype(jnp.bfloat16)
            value_acc[key, :, lanes] += product(weights.astype(jnp.bfloat16), grad_block)
            key_acc[key, :, lanes] += product(score_low, query_block)
            query_acc[query, lanes, :] += product(key_block.T, score_low)

    for_live_pairs((place, lists, counts), 0, 6, step)
    for head in range(heads):
        lanes = slice(head * HEAD_DIM, (head + 1) * HEAD_DIM)
        for slot in range(2):
            own_out[slot, :, lanes] = query_acc[slot, lanes, :].T * SCALE
            partner_out[slot, :, lanes] = query_acc[2 + slot, lanes, :].T * SCALE
            relayed_out[slot, :, lanes] = (query_acc[4 + slot, lanes, :].T * SCALE).astype(jnp.bfloat16)
    key_out[...] = (key_acc[...] * SCALE).astype(jnp.bfloat16)
    value_out[...] = value_acc[...].astype(jnp.bfloat16)


ANYWHERE = pl.BlockSpec(memory_space=pl.ANY)
SCALARS = pl.BlockSpec(memory_space=pltpu.SMEM)
FAST = pl.BlockSpec(memory_space=pltpu.VMEM)


def call(kernel, name, outs, n_any, scratch, n_copies, matmuls):
    pairs = 3 * 512 * 512
    return pl.pallas_call(
        kernel,
        out_shape=outs,
        in_specs=[SCALARS] * 3 + [ANYWHERE] * n_any,
        out_specs=jax.tree.map(lambda _: FAST, outs),
        scratch_shapes=scratch + [pltpu.SemaphoreType.DMA((n_copies,))],
        compiler_params=pltpu.CompilerParams(vmem_limit_bytes=VMEM_LIMIT),
        cost_estimate=pl.CostEstimate(
            flops=matmuls * 2 * pairs * 128, bytes_accessed=2 << 20, transcendentals=pairs
        ),
        name=name,
    )


def shards(query_rows, key_rows, value_rows, out_grad, key_blocks, block_counts):
    chips = lax.axis_size("seq")
    chip = lax.axis_index("seq")
    core = lax.axis_index("head")
    half = HEADS * HEAD_DIM // 2
    place = jnp.stack([chip, core, jnp.int32(chips)]).astype(jnp.int32)
    lists = key_blocks.reshape(-1)

    swap_pairs = [(0, 1), (1, 0)]
    partner_pairs = [(c, c ^ 1) for c in range(chips)]
    relay_pairs = [(c, c + 2) for c in range(0, chips - 2, 2)]
    relay_pairs += [(c, c - 2) for c in range(3, chips, 2)]
    back_pairs = [(b, a) for a, b in relay_pairs]
    other_pairs = [(c, c + 1) for c in range(1, chips - 1, 2)]
    other_pairs += [(b, a) for a, b in other_pairs]

    def swap(member):
        return lax.ppermute(member, "head", swap_pairs)

    def over(member, pairs):
        return lax.ppermute(member, "seq", pairs)

    def columns(member, which, lane, width):
        return lax.dynamic_slice_in_dim(member, which * half + lane, width, 1)

    lanes = []
    lane = 0
    for heads in CHUNKS:
        lanes.append((lane, heads))
        lane += heads * HEAD_DIM

    mine, other = [], []
    for lane, heads in lanes:
        width = heads * HEAD_DIM
        mine.append(
            jnp.stack([columns(query_rows, core, lane, width), columns(out_grad, core, lane, width)])
        )
        away = jnp.stack(
            [columns(query_rows, 1 - core, lane, width), columns(out_grad, 1 - core, lane, width)]
        )
        other.append(swap(away))
    key_other = swap(columns(key_rows, 1 - core, 0, half))
    value_other = swap(columns(value_rows, 1 - core, 0, half))
    keys = (key_rows, key_other, value_rows, value_other)

    results = []
    for at, (lane, heads) in enumerate(lanes):
        width = heads * HEAD_DIM
        stat_rows = -(-3 * heads // 8) * 8
        pm, po = mine[at], other[at]
        xm, xo = over(pm, partner_pairs), over(po, partner_pairs)
        ym, yo = over(xm, relay_pairs), over(xo, relay_pairs)
        stats_shape = jax.ShapeDtypeStruct((4, stat_rows, BLOCK), jnp.float32)
        buf = lambda count: pltpu.VMEM((count, 2, BLOCK, width), jnp.bfloat16)
        key_buf = pltpu.VMEM((2, BLOCK, width), jnp.bfloat16)
        stat_buf = pltpu.VMEM((4, stat_rows, BLOCK), jnp.float32)
        near = call(
            functools.partial(near_stats_kernel, heads, lane),
            "near_stats", stats_shape, 8, [key_buf, key_buf, buf(4)], 8, 2 * heads,
        )(place, lists, block_counts, *keys, pm, po, xm, xo)
        from_partner = over(near, partner_pairs)
        from_relay = over(near, relay_pairs)
        far = call(
            functools.partial(far_stats_kernel, heads, lane),
            "far_stats", stats_shape, 7, [key_buf, key_buf, buf(2)], 7, heads,
        )(place, lists, block_counts, *keys, ym, yo, near)
        from_other = over(far, other_pairs)
        from_end = over(far, back_pairs)
        full = jax.ShapeDtypeStruct((2, BLOCK, width), jnp.float32)
        low = jax.ShapeDtypeStruct((2, BLOCK, width), jnp.bfloat16)
        own, partner, relayed, key_grad, value_grad = call(
            functools.partial(grads_kernel, heads, lane),
            "grads", (full, full, low, low, low), 16,
            [key_buf, key_buf, buf(6)] + [stat_buf] * 6
            + [
                pltpu.VMEM((6, -(-2 * heads // 8) * 8, BLOCK), jnp.float32),
                pltpu.VMEM((6, width, BLOCK), jnp.float32),
                pltpu.VMEM((2, BLOCK, width), jnp.float32),
                pltpu.VMEM((2, BLOCK, width), jnp.float32),
            ],
            16, 10 * heads,
        )(
            place, lists, block_counts, *keys, pm, po, xm, xo, ym, yo,
            near, far, from_partner, from_relay, from_other, from_end,
        )
        back = over(relayed, back_pairs)
        home = over((partner + back.astype(jnp.float32)).astype(jnp.bfloat16), partner_pairs)
        query_grad = (own + home.astype(jnp.float32)).astype(jnp.bfloat16)
        results.append(
            [(member[0], swap(member[1])) for member in (query_grad, key_grad, value_grad)]
        )

    def assembled(parts):
        near_half = jnp.concatenate([part[0] for part in parts], axis=1)
        far_half = jnp.concatenate([part[1] for part in parts], axis=1)
        first = jnp.where(core == 0, near_half, far_half)
        second = jnp.where(core == 0, far_half, near_half)
        return jnp.concatenate([first, second], axis=1)

    return tuple(assembled([chunk[at] for chunk in results]) for at in range(3))


def solution(mesh):
    rows = P(("seq", "head"), None)
    return jax.shard_map(
        shards,
        mesh=mesh,
        in_specs=(rows, rows, rows, rows, P(), P()),
        out_specs=(rows, rows, rows),
        check_vma=False,
    )
```

time: 765 us -> 314 us (0.41)
  the two profiles are of different devices: /device:TPU:9 before, /device:TPU:0 now
where the time goes in v1:
time: 314 us; the launch traced here: 309 us
  starting transfers between devices  171 us (54%)
  Pallas kernels  63.6 us (20%)
  waiting for transfers between devices  51.1 us (16%)
  local copies, waits for them, and re-layouts  14.7 us (5%)
  other arithmetic  5.41 us (2%)
    ppermute x60, starting transfers between devices, over(): return lax.ppermute(member, 'seq', pairs)  166 us
    ppermute x60, waiting for transfers between devices, over(): return lax.ppermute(member, 'seq', pairs)  46.7 us
    pallas_call x6, Pallas kernels, shards(): call(functools.partial(grads_kernel, heads, lane), 'grads', (full, full,...  31.5 us
    pallas_call x6, Pallas kernels, shards(): call(functools.partial(near_stats_kernel, heads, lane), 'near_stats', sta...  21.8 us
    pallas_call x6, Pallas kernels, shards(): call(functools.partial(far_stats_kernel, heads, lane), 'far_stats', stats...  10.3 us
    unnamed x137, local copies, waits for them, and re-layouts  9.64 us
  transfers between devices with their start and end apart: 86, of which 28 were waited for; matrix products, arithmetic and copies ran while one was open for 2% of the time, Pallas kernels for 21%

profile of v1, /device:TPU:0, one launch (start us, length us, event | category | flops | bytes accessed | tf_op | source)
XLA Modules:
  0.0 308.6 jit_solution(9691425413510795083)
XLA Ops:
  9.3 4.4 %collective-permute-done.3.xm = bf16[2,512,128]{2,1,0:T(8,128)(2,1)S(1)} collective-permute-done((bf16[2,512,128]{2,1,0:T(8,128)(2,1)S(1)}, bf16[2,512,128]{2,1,0:T(8,128)(2,1)S(1)}, u32[]{:S(2)}, u32[]{:S(2)}) %collective-permute-start.3) | collective-permute-done | bytes 262176 | tf_op jit(solution)/shard_map/ppermute | solution.py:270
  43.7 3.8 %collective-permute-done.4.xo = bf16[2,512,128]{2,1,0:T(8,128)(2,1)} collective-permute-done((bf16[2,512,128]{2,1,0:T(8,128)(2,1)S(1)}, bf16[2,512,128]{2,1,0:T(8,128)(2,1)}, u32[]{:S(2)}, u32[]{:S(2)}) %collective-permute-start.4) | collective-permute-done | bytes 262176 | tf_op jit(solution)/shard_map/ppermute | solution.py:270
  47.5 3.9 %collective-permute-start.27 = (bf16[2,512,128]{2,1,0:T(8,128)(2,1)S(1)}, bf16[2,512,128]{2,1,0:T(8,128)(2,1)S(1)}, u32[]{:S(2)}, u32[]{:S(2)}) collective-permute-start(bf16[2,512,128]{2,1,0:T(8,128)(2,1)S(1)} %collective-permute-done.25.xm), channel_id=1, source_target_pairs={{0,4},{4,8},{8,12},{12,16},{16,20},{20,24},{24,28},{6,2},{10,6},{1... | collective-permute-start | bytes 786440 | tf_op jit(solution)/shard_map/ppermute | solution.py:270
  58.7 3.9 %collective-permute-start.38 = (bf16[2,512,128]{2,1,0:T(8,128)(2,1)S(1)}, bf16[2,512,128]{2,1,0:T(8,128)(2,1)S(1)}, u32[]{:S(2)}, u32[]{:S(2)}) collective-permute-start(bf16[2,512,128]{2,1,0:T(8,128)(2,1)S(1)} %collective-permute-done.36.xm), channel_id=1, source_target_pairs={{0,4},{4,8},{8,12},{12,16},{16,20},{20,24},{24,28},{6,2},{10,6},{1... | collective-permute-start | bytes 786440 | tf_op jit(solution)/shard_map/ppermute | solution.py:270
  68.3 5.1 %collective-permute-start.6 = (bf16[2,512,128]{2,1,0:T(8,128)(2,1)}, bf16[2,512,128]{2,1,0:T(8,128)(2,1)}, u32[]{:S(2)}, u32[]{:S(2)}) collective-permute-start(bf16[2,512,128]{2,1,0:T(8,128)(2,1)} %collective-permute-done.4.xo), channel_id=1, source_target_pairs={{0,4},{4,8},{8,12},{12,16},{16,20},{20,24},{24,28},{6,2},{10,6},{1... | collective-permute-start | bytes 786440 | tf_op jit(solution)/shard_map/ppermute | solution.py:270
  73.4 4.3 %collective-permute-start.17 = (bf16[2,512,128]{2,1,0:T(8,128)(2,1)}, bf16[2,512,128]{2,1,0:T(8,128)(2,1)}, u32[]{:S(2)}, u32[]{:S(2)}) collective-permute-start(bf16[2,512,128]{2,1,0:T(8,128)(2,1)} %collective-permute-done.15.xo), channel_id=1, source_target_pairs={{0,4},{4,8},{8,12},{12,16},{16,20},{20,24},{24,28},{6,2},{10,6},{1... | collective-permute-start | bytes 786440 | tf_op jit(solution)/shard_map/ppermute | solution.py:270
  85.7 4.0 %collective-permute-start.49 = (bf16[2,512,128]{2,1,0:T(8,128)(2,1)}, bf16[2,512,128]{2,1,0:T(8,128)(2,1)S(1)}, u32[]{:S(2)}, u32[]{:S(2)}) collective-permute-start(bf16[2,512,128]{2,1,0:T(8,128)(2,1)} %copy-done.19), channel_id=1, source_target_pairs={{0,4},{4,8},{8,12},{12,16},{16,20},{20,24},{24,28},{6,2},{10,6},{1... | collective-permute-start | bytes 786440 | tf_op jit(solution)/shard_map/ppermute | solution.py:270
  89.7 5.3 %collective-permute-start.60 = (bf16[2,512,128]{2,1,0:T(8,128)(2,1)}, bf16[2,512,128]{2,1,0:T(8,128)(2,1)S(1)}, u32[]{:S(2)}, u32[]{:S(2)}) collective-permute-start(bf16[2,512,128]{2,1,0:T(8,128)(2,1)} %copy-done.15), channel_id=1, source_target_pairs={{0,4},{4,8},{8,12},{12,16},{16,20},{20,24},{24,28},{6,2},{10,6},{1... | collective-permute-start | bytes 786440 | tf_op jit(solution)/shard_map/ppermute | solution.py:270
  99.8 3.7 %near_stats.6.near = f32[4,8,512]{2,1,0:T(8,128)S(1)} custom-call(s32[3]{0:T(128)S(1)} %pad_add_fusion.place, s32[96]{0:T(128)S(1)} %reshape.9.lists, s32[32]{0:T(128)S(1)} %copy-done.51, bf16[512,1536]{1,0:T(8,128)(2,1)S(1)} %copy-done, bf16[512,768]{1,0:T(8,128)(2,1)} %collective-permute-done.ko, bf16[512,1536]{1,0:T(8,128)(2,1)S(1)} %copy-done.1, ...), custom_call_target="tpu_custom_call" | custom-call | flops 402653184 | bytes 2097152 | tf_op jit(solution)/shard_map/near_stats/pallas_call | solution.py:306
  105.3 6.2 %collective-permute-start.61 = (bf16[2,512,128]{2,1,0:T(8,128)(2,1)S(1)}, bf16[2,512,128]{2,1,0:T(8,128)(2,1)S(1)}, u32[]{:S(2)}, u32[]{:S(2)}) collective-permute-start(bf16[2,512,128]{2,1,0:T(8,128)(2,1)S(1)} %copy-done.30), channel_id=1, source_target_pairs={{0,4},{4,8},{8,12},{12,16},{16,20},{20,24},{24,28},{6,2},{10,6},{1... | collective-permute-start | bytes 786440 | tf_op jit(solution)/shard_map/ppermute | solution.py:270
  111.6 3.7 %near_stats.7.near = f32[4,8,512]{2,1,0:T(8,128)S(1)} custom-call(s32[3]{0:T(128)S(1)} %pad_add_fusion.place, s32[96]{0:T(128)S(1)} %reshape.9.lists, s32[32]{0:T(128)S(1)} %copy-done.51, bf16[512,1536]{1,0:T(8,128)(2,1)S(1)} %copy-done, bf16[512,768]{1,0:T(8,128)(2,1)} %collective-permute-done.ko, bf16[512,1536]{1,0:T(8,128)(2,1)S(1)} %copy-done.1, ...), custom_call_target="tpu_custom_call" | custom-call | flops 402653184 | bytes 2097152 | tf_op jit(solution)/shard_map/near_stats/pallas_call | solution.py:306
  117.1 3.7 %near_stats.8.near = f32[4,8,512]{2,1,0:T(8,128)S(1)} custom-call(s32[3]{0:T(128)S(1)} %pad_add_fusion.place, s32[96]{0:T(128)S(1)} %reshape.9.lists, s32[32]{0:T(128)S(1)} %copy-done.51, bf16[512,1536]{1,0:T(8,128)(2,1)S(1)} %copy-done, bf16[512,768]{1,0:T(8,128)(2,1)} %collective-permute-done.ko, bf16[512,1536]{1,0:T(8,128)(2,1)S(1)} %copy-done.1, ...), custom_call_target="tpu_custom_call" | custom-call | flops 402653184 | bytes 2097152 | tf_op jit(solution)/shard_map/near_stats/pallas_call | solution.py:306
  122.6 3.7 %near_stats.9.near = f32[4,8,512]{2,1,0:T(8,128)S(1)} custom-call(s32[3]{0:T(128)S(1)} %pad_add_fusion.place, s32[96]{0:T(128)S(1)} %reshape.9.lists, s32[32]{0:T(128)S(1)} %copy-done.51, bf16[512,1536]{1,0:T(8,128)(2,1)S(1)} %copy-done, bf16[512,768]{1,0:T(8,128)(2,1)} %collective-permute-done.ko, bf16[512,1536]{1,0:T(8,128)(2,1)S(1)} %copy-done.1, ...), custom_call_target="tpu_custom_call" | custom-call | flops 402653184 | bytes 2097152 | tf_op jit(solution)/shard_map/near_stats/pallas_call | solution.py:306
  131.9 5.6 %collective-permute-start.8 = (f32[4,8,512]{2,1,0:T(8,128)S(1)}, f32[4,8,512]{2,1,0:T(8,128)S(1)}, u32[]{:S(2)}, u32[]{:S(2)}) collective-permute-start(f32[4,8,512]{2,1,0:T(8,128)S(1)} %near_stats.6.near), channel_id=1, source_target_pairs={{0,4},{4,8},{8,12},{12,16},{16,20},{20,24},{24,28},{6,2},{10,6},{1... | collective-permute-start | bytes 196616 | tf_op jit(solution)/shard_map/ppermute | solution.py:270
  144.9 4.4 %collective-permute-start.18 = (f32[4,8,512]{2,1,0:T(8,128)S(1)}, f32[4,8,512]{2,1,0:T(8,128)S(1)}, u32[]{:S(2)}, u32[]{:S(2)}) collective-permute-start(f32[4,8,512]{2,1,0:T(8,128)S(1)} %near_stats.7.near), channel_id=1, source_target_pairs={{0,2},{2,0},{4,6},{6,4},{8,10},{10,8},{12,14},{14,12},{16,18},{18,... | collective-permute-start | bytes 196616 | tf_op jit(solution)/shard_map/ppermute | solution.py:270
  150.9 5.7 %collective-permute-start.19 = (f32[4,8,512]{2,1,0:T(8,128)S(1)}, f32[4,8,512]{2,1,0:T(8,128)S(1)}, u32[]{:S(2)}, u32[]{:S(2)}) collective-permute-start(f32[4,8,512]{2,1,0:T(8,128)S(1)} %near_stats.7.near), channel_id=1, source_target_pairs={{0,4},{4,8},{8,12},{12,16},{16,20},{20,24},{24,28},{6,2},{10,6},{1... | collective-permute-start | bytes 196616 | tf_op jit(solution)/shard_map/ppermute | solution.py:270
  158.7 6.3 %collective-permute-start.29 = (f32[4,8,512]{2,1,0:T(8,128)S(1)}, f32[4,8,512]{2,1,0:T(8,128)S(1)}, u32[]{:S(2)}, u32[]{:S(2)}) collective-permute-start(f32[4,8,512]{2,1,0:T(8,128)S(1)} %near_stats.8.near), channel_id=1, source_target_pairs={{0,2},{2,0},{4,6},{6,4},{8,10},{10,8},{12,14},{14,12},{16,18},{18,... | collective-permute-start | bytes 196616 | tf_op jit(solution)/shard_map/ppermute | solution.py:270
  165.0 5.3 %grads.6 = (f32[2,512,128]{2,1,0:T(8,128)S(1)}, f32[2,512,128]{2,1,0:T(8,128)S(1)}, bf16[2,512,128]{2,1,0:T(8,128)(2,1)S(1)}, bf16[2,512,128]{2,1,0:T(8,128)(2,1)S(1)}, bf16[2,512,128]{2,1,0:T(8,128)(2,1)S(1)}) custom-call(s32[3]{0:T(128)S(1)} %pad_add_fusion.place, s32[96]{0:T(128)S(1)} %reshape.9.lists, s32[32]{0:T(128)S(1)} %copy-done.51, ...), custom_call_target="tpu_custom_call" | custom-call | flops 2013265920 | bytes 2097152 | tf_op jit(solution)/shard_map/grads/pallas_call | solution.py:320
  175.9 5.3 %collective-permute-start.40 = (f32[4,8,512]{2,1,0:T(8,128)S(1)}, f32[4,8,512]{2,1,0:T(8,128)S(1)}, u32[]{:S(2)}, u32[]{:S(2)}) collective-permute-start(f32[4,8,512]{2,1,0:T(8,128)S(1)} %near_stats.9.near), channel_id=1, source_target_pairs={{0,2},{2,0},{4,6},{6,4},{8,10},{10,8},{12,14},{14,12},{16,18},{18,... | collective-permute-start | bytes 196616 | tf_op jit(solution)/shard_map/ppermute | solution.py:270
  181.2 5.3 %grads.7 = (f32[2,512,128]{2,1,0:T(8,128)S(1)}, f32[2,512,128]{2,1,0:T(8,128)S(1)}, bf16[2,512,128]{2,1,0:T(8,128)(2,1)S(1)}, bf16[2,512,128]{2,1,0:T(8,128)(2,1)S(1)}, bf16[2,512,128]{2,1,0:T(8,128)(2,1)S(1)}) custom-call(s32[3]{0:T(128)S(1)} %pad_add_fusion.place, s32[96]{0:T(128)S(1)} %reshape.9.lists, s32[32]{0:T(128)S(1)} %copy-done.51, ...), custom_call_target="tpu_custom_call" | custom-call | flops 2013265920 | bytes 2097152 | tf_op jit(solution)/shard_map/grads/pallas_call | solution.py:320
  192.1 5.9 %collective-permute-start.51 = (f32[4,8,512]{2,1,0:T(8,128)S(1)}, f32[4,8,512]{2,1,0:T(8,128)S(1)}, u32[]{:S(2)}, u32[]{:S(2)}) collective-permute-start(f32[4,8,512]{2,1,0:T(8,128)S(1)} %near_stats.10.near), channel_id=1, source_target_pairs={{0,2},{2,0},{4,6},{6,4},{8,10},{10,8},{12,14},{14,12},{16,18},{18,... | collective-permute-start | bytes 196616 | tf_op jit(solution)/shard_map/ppermute | solution.py:270
  198.0 5.3 %grads.8 = (f32[2,512,128]{2,1,0:T(8,128)S(1)}, f32[2,512,128]{2,1,0:T(8,128)S(1)}, bf16[2,512,128]{2,1,0:T(8,128)(2,1)S(1)}, bf16[2,512,128]{2,1,0:T(8,128)(2,1)S(1)}, bf16[2,512,128]{2,1,0:T(8,128)(2,1)S(1)}) custom-call(s32[3]{0:T(128)S(1)} %pad_add_fusion.place, s32[96]{0:T(128)S(1)} %reshape.9.lists, s32[32]{0:T(128)S(1)} %copy-done.51, ...), custom_call_target="tpu_custom_call" | custom-call | flops 2013265920 | bytes 2097152 | tf_op jit(solution)/shard_map/grads/pallas_call | solution.py:320
  208.9 6.0 %collective-permute-start.62 = (f32[4,8,512]{2,1,0:T(8,128)S(1)}, f32[4,8,512]{2,1,0:T(8,128)S(1)}, u32[]{:S(2)}, u32[]{:S(2)}) collective-permute-start(f32[4,8,512]{2,1,0:T(8,128)S(1)} %near_stats.11.near), channel_id=1, source_target_pairs={{0,2},{2,0},{4,6},{6,4},{8,10},{10,8},{12,14},{14,12},{16,18},{18,... | collective-permute-start | bytes 196616 | tf_op jit(solution)/shard_map/ppermute | solution.py:270
  214.9 5.3 %grads.9 = (f32[2,512,128]{2,1,0:T(8,128)S(1)}, f32[2,512,128]{2,1,0:T(8,128)S(1)}, bf16[2,512,128]{2,1,0:T(8,128)(2,1)S(1)}, bf16[2,512,128]{2,1,0:T(8,128)(2,1)S(1)}, bf16[2,512,128]{2,1,0:T(8,128)(2,1)S(1)}) custom-call(s32[3]{0:T(128)S(1)} %pad_add_fusion.place, s32[96]{0:T(128)S(1)} %reshape.9.lists, s32[32]{0:T(128)S(1)} %copy-done.51, ...), custom_call_target="tpu_custom_call" | custom-call | flops 2013265920 | bytes 2097152 | tf_op jit(solution)/shard_map/grads/pallas_call | solution.py:320
  227.1 5.1 %grads.10 = (f32[2,512,128]{2,1,0:T(8,128)S(1)}, f32[2,512,128]{2,1,0:T(8,128)S(1)}, bf16[2,512,128]{2,1,0:T(8,128)(2,1)S(1)}, bf16[2,512,128]{2,1,0:T(8,128)(2,1)S(1)}, bf16[2,512,128]{2,1,0:T(8,128)(2,1)S(1)}) custom-call(s32[3]{0:T(128)S(1)} %pad_add_fusion.place, s32[96]{0:T(128)S(1)} %reshape.9.lists, s32[32]{0:T(128)S(1)} %copy-done.51, ...), custom_call_target="tpu_custom_call" | custom-call | flops 2013265920 | bytes 2097152 | tf_op jit(solution)/shard_map/grads/pallas_call | solution.py:320
  235.2 5.1 %grads.11 = (f32[2,512,128]{2,1,0:T(8,128)S(1)}, f32[2,512,128]{2,1,0:T(8,128)S(1)}, bf16[2,512,128]{2,1,0:T(8,128)(2,1)S(1)}, bf16[2,512,128]{2,1,0:T(8,128)(2,1)S(1)}, bf16[2,512,128]{2,1,0:T(8,128)(2,1)S(1)}) custom-call(s32[3]{0:T(128)S(1)} %pad_add_fusion.place, s32[96]{0:T(128)S(1)} %reshape.9.lists, s32[32]{0:T(128)S(1)} %copy-done.51, ...), custom_call_target="tpu_custom_call" | custom-call | flops 2013265920 | bytes 2097152 | tf_op jit(solution)/shard_map/grads/pallas_call | solution.py:320
  254.8 16.3 %collective-permute-start.12 = (bf16[2,512,128]{2,1,0:T(8,128)(2,1)S(1)}, bf16[2,512,128]{2,1,0:T(8,128)(2,1)S(1)}, u32[]{:S(2)}, u32[]{:S(2)}) collective-permute-start(bf16[2,512,128]{2,1,0:T(8,128)(2,1)S(1)} %add_convert_fusion.11), channel_id=1, source_target_pairs={{0,2},{2,0},{4,6},{6,4},{8,10},{10,8},{12,14},{14,12},{16,18},{18,... | collective-permute-start | bytes 786440 | tf_op jit(solution)/shard_map/ppermute | solution.py:270
  276.7 4.3 %collective-permute-start.56 = (bf16[2,512,128]{2,1,0:T(8,128)(2,1)S(1)}, bf16[2,512,128]{2,1,0:T(8,128)(2,1)S(1)}, u32[]{:S(2)}, u32[]{:S(2)}) collective-permute-start(bf16[2,512,128]{2,1,0:T(8,128)(2,1)S(1)} %add_convert_fusion.3), channel_id=1, source_target_pairs={{0,2},{2,0},{4,6},{6,4},{8,10},{10,8},{12,14},{14,12},{16,18},{18,... | collective-permute-start | bytes 786440 | tf_op jit(solution)/shard_map/ppermute | solution.py:270
  284.0 5.5 %collective-permute-done.34 = bf16[2,512,128]{2,1,0:T(8,128)(2,1)S(1)} collective-permute-done((bf16[2,512,128]{2,1,0:T(8,128)(2,1)S(1)}, bf16[2,512,128]{2,1,0:T(8,128)(2,1)S(1)}, u32[]{:S(2)}, u32[]{:S(2)}) %collective-permute-start.34) | collective-permute-done | bytes 262176 | tf_op jit(solution)/shard_map/ppermute | solution.py:270
  289.6 5.5 %collective-permute-done.45 = bf16[2,512,128]{2,1,0:T(8,128)(2,1)S(1)} collective-permute-done((bf16[2,512,128]{2,1,0:T(8,128)(2,1)S(1)}, bf16[2,512,128]{2,1,0:T(8,128)(2,1)S(1)}, u32[]{:S(2)}, u32[]{:S(2)}) %collective-permute-start.45) | collective-permute-done | bytes 262176 | tf_op jit(solution)/shard_map/ppermute | solution.py:270
  295.3 5.5 %collective-permute-done.56 = bf16[2,512,128]{2,1,0:T(8,128)(2,1)S(1)} collective-permute-done((bf16[2,512,128]{2,1,0:T(8,128)(2,1)S(1)}, bf16[2,512,128]{2,1,0:T(8,128)(2,1)S(1)}, u32[]{:S(2)}, u32[]{:S(2)}) %collective-permute-start.56) | collective-permute-done | bytes 262176 | tf_op jit(solution)/shard_map/ppermute | solution.py:270
  300.9 4.1 %collective-permute-done.67 = bf16[2,512,128]{2,1,0:T(8,128)(2,1)S(1)} collective-permute-done((bf16[2,512,128]{2,1,0:T(8,128)(2,1)S(1)}, bf16[2,512,128]{2,1,0:T(8,128)(2,1)S(1)}, u32[]{:S(2)}, u32[]{:S(2)}) %collective-permute-start.67) | collective-permute-done | bytes 262176 | tf_op jit(solution)/shard_map/ppermute | solution.py:270
  (354 shorter events, 138.7 us)
Async XLA Ops:
  32.5 19.9 %collective-permute-start.5 = (bf16[2,512,128]{2,1,0:T(8,128)(2,1)S(1)}, bf16[2,512,128]{2,1,0:T(8,128)(2,1)S(1)}, u32[]{:S(2)}, u32[]{:S(2)}) collective-permute-start(bf16[2,512,128]{2,1,0:T(8,128)(2,1)S(1)} %collective-permute-done.3.xm), channel_id=1, source_target_pairs={{0,4},{4,8},{8,12},{12,16},{16,20},{20,24},{24,28},{6,2},{10,6},{1... | collective-permute-start | bytes 786440 | tf_op jit(solution)/shard_map/ppermute | solution.py:270
  53.0 36.7 %collective-permute-start = (bf16[512,768]{1,0:T(8,128)(2,1)}, bf16[512,768]{1,0:T(8,128)(2,1)}, u32[]{:S(2)}, u32[]{:S(2)}) collective-permute-start(bf16[512,768]{1,0:T(8,128)(2,1)} %constant_dynamic-slice_fusion.1), channel_id=1, source_target_pairs={{0,1},{1,0},{2,3},{3,2},{4,5},{5,4},{6,7},{7,6},{8,9},{9,8},{10,11... | collective-permute-start | bytes 2359304 | tf_op jit(solution)/shard_map/ppermute | solution.py:267
  53.1 41.9 %collective-permute-start.1 = (bf16[512,768]{1,0:T(8,128)(2,1)}, bf16[512,768]{1,0:T(8,128)(2,1)}, u32[]{:S(2)}, u32[]{:S(2)}) collective-permute-start(bf16[512,768]{1,0:T(8,128)(2,1)} %constant_dynamic-slice_fusion), channel_id=1, source_target_pairs={{0,1},{1,0},{2,3},{3,2},{4,5},{5,4},{6,7},{7,6},{8,9},{9,8},{10,11... | collective-permute-start | bytes 2359304 | tf_op jit(solution)/shard_map/ppermute | solution.py:267
  78.5 26.8 %collective-permute-start.28 = (bf16[2,512,128]{2,1,0:T(8,128)(2,1)}, bf16[2,512,128]{2,1,0:T(8,128)(2,1)}, u32[]{:S(2)}, u32[]{:S(2)}) collective-permute-start(bf16[2,512,128]{2,1,0:T(8,128)(2,1)} %collective-permute-done.26.xo), channel_id=1, source_target_pairs={{0,4},{4,8},{8,12},{12,16},{16,20},{20,24},{24,28},{6,2},{10,6},{1... | collective-permute-start | bytes 786440 | tf_op jit(solution)/shard_map/ppermute | solution.py:270
  81.7 44.6 %collective-permute-start.39 = (bf16[2,512,128]{2,1,0:T(8,128)(2,1)}, bf16[2,512,128]{2,1,0:T(8,128)(2,1)}, u32[]{:S(2)}, u32[]{:S(2)}) collective-permute-start(bf16[2,512,128]{2,1,0:T(8,128)(2,1)} %collective-permute-done.37.xo), channel_id=1, source_target_pairs={{0,4},{4,8},{8,12},{12,16},{16,20},{20,24},{24,28},{6,2},{10,6},{1... | collective-permute-start | bytes 786440 | tf_op jit(solution)/shard_map/ppermute | solution.py:270
  85.7 46.2 %collective-permute-start.49 = (bf16[2,512,128]{2,1,0:T(8,128)(2,1)}, bf16[2,512,128]{2,1,0:T(8,128)(2,1)S(1)}, u32[]{:S(2)}, u32[]{:S(2)}) collective-permute-start(bf16[2,512,128]{2,1,0:T(8,128)(2,1)} %copy-done.19), channel_id=1, source_target_pairs={{0,4},{4,8},{8,12},{12,16},{16,20},{20,24},{24,28},{6,2},{10,6},{1... | collective-permute-start | bytes 786440 | tf_op jit(solution)/shard_map/ppermute | solution.py:270
  89.7 47.7 %collective-permute-start.60 = (bf16[2,512,128]{2,1,0:T(8,128)(2,1)}, bf16[2,512,128]{2,1,0:T(8,128)(2,1)S(1)}, u32[]{:S(2)}, u32[]{:S(2)}) collective-permute-start(bf16[2,512,128]{2,1,0:T(8,128)(2,1)} %copy-done.15), channel_id=1, source_target_pairs={{0,4},{4,8},{8,12},{12,16},{16,20},{20,24},{24,28},{6,2},{10,6},{1... | collective-permute-start | bytes 786440 | tf_op jit(solution)/shard_map/ppermute | solution.py:270
  95.0 43.1 %collective-permute-start.50 = (bf16[2,512,128]{2,1,0:T(8,128)(2,1)}, bf16[2,512,128]{2,1,0:T(8,128)(2,1)S(1)}, u32[]{:S(2)}, u32[]{:S(2)}) collective-permute-start(bf16[2,512,128]{2,1,0:T(8,128)(2,1)} %copy-done.35), channel_id=1, source_target_pairs={{0,4},{4,8},{8,12},{12,16},{16,20},{20,24},{24,28},{6,2},{10,6},{1... | collective-permute-start | bytes 786440 | tf_op jit(solution)/shard_map/ppermute | solution.py:270
  105.3 39.6 %collective-permute-start.61 = (bf16[2,512,128]{2,1,0:T(8,128)(2,1)S(1)}, bf16[2,512,128]{2,1,0:T(8,128)(2,1)S(1)}, u32[]{:S(2)}, u32[]{:S(2)}) collective-permute-start(bf16[2,512,128]{2,1,0:T(8,128)(2,1)S(1)} %copy-done.30), channel_id=1, source_target_pairs={{0,4},{4,8},{8,12},{12,16},{16,20},{20,24},{24,28},{6,2},{10,6},{1... | collective-permute-start | bytes 786440 | tf_op jit(solution)/shard_map/ppermute | solution.py:270
  126.4 24.6 %collective-permute-start.7 = (f32[4,8,512]{2,1,0:T(8,128)S(1)}, f32[4,8,512]{2,1,0:T(8,128)S(1)}, u32[]{:S(2)}, u32[]{:S(2)}) collective-permute-start(f32[4,8,512]{2,1,0:T(8,128)S(1)} %near_stats.6.near), channel_id=1, source_target_pairs={{0,2},{2,0},{4,6},{6,4},{8,10},{10,8},{12,14},{14,12},{16,18},{18,... | collective-permute-start | bytes 196616 | tf_op jit(solution)/shard_map/ppermute | solution.py:270
  131.9 24.8 %collective-permute-start.8 = (f32[4,8,512]{2,1,0:T(8,128)S(1)}, f32[4,8,512]{2,1,0:T(8,128)S(1)}, u32[]{:S(2)}, u32[]{:S(2)}) collective-permute-start(f32[4,8,512]{2,1,0:T(8,128)S(1)} %near_stats.6.near), channel_id=1, source_target_pairs={{0,4},{4,8},{8,12},{12,16},{16,20},{20,24},{24,28},{6,2},{10,6},{1... | collective-permute-start | bytes 196616 | tf_op jit(solution)/shard_map/ppermute | solution.py:270
  137.4 19.9 %collective-permute-start.9 = (f32[4,8,512]{2,1,0:T(8,128)S(1)}, f32[4,8,512]{2,1,0:T(8,128)S(1)}, u32[]{:S(2)}, u32[]{:S(2)}) collective-permute-start(f32[4,8,512]{2,1,0:T(8,128)S(1)} %far_stats.6.far), channel_id=1, source_target_pairs={{2,4},{6,8},{10,12},{14,16},{18,20},{22,24},{26,28},{4,2},{8,6},{1... | collective-permute-start | bytes 196616 | tf_op jit(solution)/shard_map/ppermute | solution.py:270
  138.1 20.6 %collective-permute-start.10 = (f32[4,8,512]{2,1,0:T(8,128)S(1)}, f32[4,8,512]{2,1,0:T(8,128)S(1)}, u32[]{:S(2)}, u32[]{:S(2)}) collective-permute-start(f32[4,8,512]{2,1,0:T(8,128)S(1)} %far_stats.6.far), channel_id=1, source_target_pairs={{4,0},{8,4},{12,8},{16,12},{20,16},{24,20},{28,24},{2,6},{6,10},{1... | collective-permute-start | bytes 196616 | tf_op jit(solution)/shard_map/ppermute | solution.py:270
  144.9 25.5 %collective-permute-start.18 = (f32[4,8,512]{2,1,0:T(8,128)S(1)}, f32[4,8,512]{2,1,0:T(8,128)S(1)}, u32[]{:S(2)}, u32[]{:S(2)}) collective-permute-start(f32[4,8,512]{2,1,0:T(8,128)S(1)} %near_stats.7.near), channel_id=1, source_target_pairs={{0,2},{2,0},{4,6},{6,4},{8,10},{10,8},{12,14},{14,12},{16,18},{18,... | collective-permute-start | bytes 196616 | tf_op jit(solution)/shard_map/ppermute | solution.py:270
  150.9 23.0 %collective-permute-start.19 = (f32[4,8,512]{2,1,0:T(8,128)S(1)}, f32[4,8,512]{2,1,0:T(8,128)S(1)}, u32[]{:S(2)}, u32[]{:S(2)}) collective-permute-start(f32[4,8,512]{2,1,0:T(8,128)S(1)} %near_stats.7.near), channel_id=1, source_target_pairs={{0,4},{4,8},{8,12},{12,16},{16,20},{20,24},{24,28},{6,2},{10,6},{1... | collective-permute-start | bytes 196616 | tf_op jit(solution)/shard_map/ppermute | solution.py:270
  158.7 27.9 %collective-permute-start.29 = (f32[4,8,512]{2,1,0:T(8,128)S(1)}, f32[4,8,512]{2,1,0:T(8,128)S(1)}, u32[]{:S(2)}, u32[]{:S(2)}) collective-permute-start(f32[4,8,512]{2,1,0:T(8,128)S(1)} %near_stats.8.near), channel_id=1, source_target_pairs={{0,2},{2,0},{4,6},{6,4},{8,10},{10,8},{12,14},{14,12},{16,18},{18,... | collective-permute-start | bytes 196616 | tf_op jit(solution)/shard_map/ppermute | solution.py:270
  175.9 27.5 %collective-permute-start.40 = (f32[4,8,512]{2,1,0:T(8,128)S(1)}, f32[4,8,512]{2,1,0:T(8,128)S(1)}, u32[]{:S(2)}, u32[]{:S(2)}) collective-permute-start(f32[4,8,512]{2,1,0:T(8,128)S(1)} %near_stats.9.near), channel_id=1, source_target_pairs={{0,2},{2,0},{4,6},{6,4},{8,10},{10,8},{12,14},{14,12},{16,18},{18,... | collective-permute-start | bytes 196616 | tf_op jit(solution)/shard_map/ppermute | solution.py:270
  186.6 20.3 %collective-permute-start.41 = (f32[4,8,512]{2,1,0:T(8,128)S(1)}, f32[4,8,512]{2,1,0:T(8,128)S(1)}, u32[]{:S(2)}, u32[]{:S(2)}) collective-permute-start(f32[4,8,512]{2,1,0:T(8,128)S(1)} %near_stats.9.near), channel_id=1, source_target_pairs={{0,4},{4,8},{8,12},{12,16},{16,20},{20,24},{24,28},{6,2},{10,6},{1... | collective-permute-start | bytes 196616 | tf_op jit(solution)/shard_map/ppermute | solution.py:270
  192.1 28.2 %collective-permute-start.51 = (f32[4,8,512]{2,1,0:T(8,128)S(1)}, f32[4,8,512]{2,1,0:T(8,128)S(1)}, u32[]{:S(2)}, u32[]{:S(2)}) collective-permute-start(f32[4,8,512]{2,1,0:T(8,128)S(1)} %near_stats.10.near), channel_id=1, source_target_pairs={{0,2},{2,0},{4,6},{6,4},{8,10},{10,8},{12,14},{14,12},{16,18},{18,... | collective-permute-start | bytes 196616 | tf_op jit(solution)/shard_map/ppermute | solution.py:270
  203.4 20.4 %collective-permute-start.52 = (f32[4,8,512]{2,1,0:T(8,128)S(1)}, f32[4,8,512]{2,1,0:T(8,128)S(1)}, u32[]{:S(2)}, u32[]{:S(2)}) collective-permute-start(f32[4,8,512]{2,1,0:T(8,128)S(1)} %near_stats.10.near), channel_id=1, source_target_pairs={{0,4},{4,8},{8,12},{12,16},{16,20},{20,24},{24,28},{6,2},{10,6},{1... | collective-permute-start | bytes 196616 | tf_op jit(solution)/shard_map/ppermute | solution.py:270
  208.9 23.4 %collective-permute-start.62 = (f32[4,8,512]{2,1,0:T(8,128)S(1)}, f32[4,8,512]{2,1,0:T(8,128)S(1)}, u32[]{:S(2)}, u32[]{:S(2)}) collective-permute-start(f32[4,8,512]{2,1,0:T(8,128)S(1)} %near_stats.11.near), channel_id=1, source_target_pairs={{0,2},{2,0},{4,6},{6,4},{8,10},{10,8},{12,14},{14,12},{16,18},{18,... | collective-permute-start | bytes 196616 | tf_op jit(solution)/shard_map/ppermute | solution.py:270
  225.8 27.6 %collective-permute-start.11 = (bf16[2,512,128]{2,1,0:T(8,128)(2,1)S(1)}, bf16[2,512,128]{2,1,0:T(8,128)(2,1)S(1)}, u32[]{:S(2)}, u32[]{:S(2)}) collective-permute-start(bf16[2,512,128]{2,1,0:T(8,128)(2,1)S(1)} %get-tuple-element.35), channel_id=1, source_target_pairs={{4,0},{8,4},{12,8},{16,12},{20,16},{24,20},{28,24},{2,6},{6,10},{1... | collective-permute-start | bytes 786440 | tf_op jit(solution)/shard_map/ppermute | solution.py:270
  232.3 22.5 %collective-permute-start.22 = (bf16[2,512,128]{2,1,0:T(8,128)(2,1)S(1)}, bf16[2,512,128]{2,1,0:T(8,128)(2,1)S(1)}, u32[]{:S(2)}, u32[]{:S(2)}) collective-permute-start(bf16[2,512,128]{2,1,0:T(8,128)(2,1)S(1)} %get-tuple-element.38), channel_id=1, source_target_pairs={{4,0},{8,4},{12,8},{16,12},{20,16},{24,20},{28,24},{2,6},{6,10},{1... | collective-permute-start | bytes 786440 | tf_op jit(solution)/shard_map/ppermute | solution.py:270
  233.6 37.5 %collective-permute-start.33 = (bf16[2,512,128]{2,1,0:T(8,128)(2,1)S(1)}, bf16[2,512,128]{2,1,0:T(8,128)(2,1)S(1)}, u32[]{:S(2)}, u32[]{:S(2)}) collective-permute-start(bf16[2,512,128]{2,1,0:T(8,128)(2,1)S(1)} %get-tuple-element.41), channel_id=1, source_target_pairs={{4,0},{8,4},{12,8},{16,12},{20,16},{24,20},{28,24},{2,6},{6,10},{1... | collective-permute-start | bytes 786440 | tf_op jit(solution)/shard_map/ppermute | solution.py:270
  249.3 22.0 %collective-permute-start.44 = (bf16[2,512,128]{2,1,0:T(8,128)(2,1)S(1)}, bf16[2,512,128]{2,1,0:T(8,128)(2,1)S(1)}, u32[]{:S(2)}, u32[]{:S(2)}) collective-permute-start(bf16[2,512,128]{2,1,0:T(8,128)(2,1)S(1)} %get-tuple-element.44), channel_id=1, source_target_pairs={{4,0},{8,4},{12,8},{16,12},{20,16},{24,20},{28,24},{2,6},{6,10},{1... | collective-permute-start | bytes 786440 | tf_op jit(solution)/shard_map/ppermute | solution.py:270
  250.6 22.8 %collective-permute-start.55 = (bf16[2,512,128]{2,1,0:T(8,128)(2,1)S(1)}, bf16[2,512,128]{2,1,0:T(8,128)(2,1)S(1)}, u32[]{:S(2)}, u32[]{:S(2)}) collective-permute-start(bf16[2,512,128]{2,1,0:T(8,128)(2,1)S(1)} %get-tuple-element.47), channel_id=1, source_target_pairs={{4,0},{8,4},{12,8},{16,12},{20,16},{24,20},{28,24},{2,6},{6,10},{1... | collective-permute-start | bytes 786440 | tf_op jit(solution)/shard_map/ppermute | solution.py:270
  253.4 23.3 %collective-permute-start.66 = (bf16[2,512,128]{2,1,0:T(8,128)(2,1)S(1)}, bf16[2,512,128]{2,1,0:T(8,128)(2,1)S(1)}, u32[]{:S(2)}, u32[]{:S(2)}) collective-permute-start(bf16[2,512,128]{2,1,0:T(8,128)(2,1)S(1)} %get-tuple-element.50), channel_id=1, source_target_pairs={{4,0},{8,4},{12,8},{16,12},{20,16},{24,20},{28,24},{2,6},{6,10},{1... | collective-permute-start | bytes 786440 | tf_op jit(solution)/shard_map/ppermute | solution.py:270
  254.8 26.3 %collective-permute-start.12 = (bf16[2,512,128]{2,1,0:T(8,128)(2,1)S(1)}, bf16[2,512,128]{2,1,0:T(8,128)(2,1)S(1)}, u32[]{:S(2)}, u32[]{:S(2)}) collective-permute-start(bf16[2,512,128]{2,1,0:T(8,128)(2,1)S(1)} %add_convert_fusion.11), channel_id=1, source_target_pairs={{0,2},{2,0},{4,6},{6,4},{8,10},{10,8},{12,14},{14,12},{16,18},{18,... | collective-permute-start | bytes 786440 | tf_op jit(solution)/shard_map/ppermute | solution.py:270
  273.5 21.7 %collective-permute-start.45 = (bf16[2,512,128]{2,1,0:T(8,128)(2,1)S(1)}, bf16[2,512,128]{2,1,0:T(8,128)(2,1)S(1)}, u32[]{:S(2)}, u32[]{:S(2)}) collective-permute-start(bf16[2,512,128]{2,1,0:T(8,128)(2,1)S(1)} %add_convert_fusion.5), channel_id=1, source_target_pairs={{0,2},{2,0},{4,6},{6,4},{8,10},{10,8},{12,14},{14,12},{16,18},{18,... | collective-permute-start | bytes 786440 | tf_op jit(solution)/shard_map/ppermute | solution.py:270
  276.7 24.0 %collective-permute-start.56 = (bf16[2,512,128]{2,1,0:T(8,128)(2,1)S(1)}, bf16[2,512,128]{2,1,0:T(8,128)(2,1)S(1)}, u32[]{:S(2)}, u32[]{:S(2)}) collective-permute-start(bf16[2,512,128]{2,1,0:T(8,128)(2,1)S(1)} %add_convert_fusion.3), channel_id=1, source_target_pairs={{0,2},{2,0},{4,6},{6,4},{8,10},{10,8},{12,14},{14,12},{16,18},{18,... | collective-permute-start | bytes 786440 | tf_op jit(solution)/shard_map/ppermute | solution.py:270
  281.1 23.8 %collective-permute-start.67 = (bf16[2,512,128]{2,1,0:T(8,128)(2,1)S(1)}, bf16[2,512,128]{2,1,0:T(8,128)(2,1)S(1)}, u32[]{:S(2)}, u32[]{:S(2)}) collective-permute-start(bf16[2,512,128]{2,1,0:T(8,128)(2,1)S(1)} %add_convert_fusion.1), channel_id=1, source_target_pairs={{0,2},{2,0},{4,6},{6,4},{8,10},{10,8},{12,14},{14,12},{16,18},{18,... | collective-permute-start | bytes 786440 | tf_op jit(solution)/shard_map/ppermute | solution.py:270
  283.9 21.8 %collective-permute-start.68 = (bf16[512,128]{1,0:T(8,128)(2,1)S(1)}, bf16[512,128]{1,0:T(8,128)(2,1)S(1)}, u32[]{:S(2)}, u32[]{:S(2)}) collective-permute-start(bf16[512,128]{1,0:T(8,128)(2,1)S(1)} %slice_bitcast_fusion.5), channel_id=1, source_target_pairs={{0,1},{1,0},{2,3},{3,2},{4,5},{5,4},{6,7},{7,6},{8,9},{9,8},{10,11... | collective-permute-start | bytes 393224 | tf_op jit(solution)/shard_map/ppermute | solution.py:267
  (107 other events, 1273.0 us)

commit v2 on v0

v2 whole, which is shorter than its diff:
```python
import functools
import math

import jax
import jax.numpy as jnp
from jax import lax
from jax.experimental import pallas as pl
from jax.experimental.pallas import tpu as pltpu
from jax.sharding import PartitionSpec as P

HEADS = 12
HEAD_DIM = 128
BLOCK = 512
MAXK = 3
GROUP = 4
SHARE = HEADS // GROUP
WINDOW = 2 * GROUP + 4
KEY_GROUPS = ((0,), (1, 2))
SCALE = HEAD_DIM ** -0.5
LOG_SCALE = SCALE * math.log2(math.e)
VMEM_LIMIT = 48 * 1024 * 1024

ANYWHERE = pl.BlockSpec(memory_space=pl.ANY)
SCALARS = pl.BlockSpec(memory_space=pltpu.SMEM)
FAST = pl.BlockSpec(memory_space=pltpu.VMEM)


def pair_rows(left, right):
    return lax.dot_general(
        left, right, (((1,), (1,)), ((), ())), preferred_element_type=jnp.float32
    )


def product(left, right):
    return jnp.dot(left, right, preferred_element_type=jnp.float32)


def copy_all(copies, sem):
    started = [
        pltpu.make_async_copy(source, target, sem.at[at])
        for at, (source, target) in enumerate(copies)
    ]
    for copy in started:
        copy.start()
    for copy in started:
        copy.wait()


def head_columns(spot, head):
    return pl.ds(pl.multiple_of((spot * SHARE + head) * HEAD_DIM, HEAD_DIM), HEAD_DIM)


def pack_kernel(heads, place, first, second, *rest):
    outs, sem = rest[:-1], rest[-1]
    spot = place[0] & (GROUP - 1)
    copies = []
    for away, out in enumerate(outs):
        for at, head in enumerate(heads):
            columns = head_columns(spot ^ away, head)
            copies.append((first.at[:, columns], out.at[2 * at]))
            copies.append((second.at[:, columns], out.at[2 * at + 1]))
    copy_all(copies, sem)


def pack(place, first, second, heads):
    out = jax.ShapeDtypeStruct((2 * len(heads), BLOCK, HEAD_DIM), first.dtype)
    return pl.pallas_call(
        functools.partial(pack_kernel, heads),
        out_shape=[out] * GROUP,
        in_specs=[SCALARS, ANYWHERE, ANYWHERE],
        out_specs=[ANYWHERE] * GROUP,
        scratch_shapes=[pltpu.SemaphoreType.DMA((2 * GROUP * len(heads),))],
        name="pack",
    )(place, first, second)


def grads_kernel(
    at, place, lists, counts,
    k0, k1, k2, k3, s0, s1, s2, s3, below, above, swapped_edge, q0, q1, q2, q3,
    d0, d1, d2, d3, near_out, far_out,
    keys, rows, sums, query_out, low, sem,
):
    chip, core = place[0], place[1]
    spot = chip & (GROUP - 1)
    first = 2 * (chip - spot) - 2
    pair = pl.ds(2 * at, 2)
    copies = []
    for away, (mine, other, row) in enumerate(zip((k0, k1, k2, k3), (s0, s1, s2, s3), (q0, q1, q2, q3))):
        block = 2 + 2 * (spot ^ away)
        copies.append((mine.at[pair], keys.at[block + core]))
        copies.append((other.at[pair], keys.at[block + 1 - core]))
        copies.append((row, rows.at[away]))
    copies.append((below.at[pair], keys.at[core]))
    copies.append((above.at[pair], keys.at[WINDOW - 2 + core]))
    copies.append((swapped_edge.at[pair], keys.at[jnp.where(core == 0, 1, WINDOW - 2)]))
    started = [
        pltpu.make_async_copy(source, target, sem.at[index])
        for index, (source, target) in enumerate(copies)
    ]
    for copy in started:
        copy.start()
    sums[...] = jnp.zeros_like(sums)
    for copy in started:
        copy.wait()

    def query_step(away, carry):
        block = first + 2 + 2 * (spot ^ away) + core
        count = counts[block]

        def live(slots):
            query_block, grad_block = rows[away, 0], rows[away, 1]
            places = [lists[block * MAXK + slot] - first for slot in range(slots)]
            scores = [pair_rows(keys[spot_at, 0], query_block) for spot_at in places]
            peak = functools.reduce(
                jnp.maximum, [jnp.max(member, axis=0, keepdims=True) for member in scores]
            )
            grown = [jnp.exp2(member * LOG_SCALE - peak * LOG_SCALE) for member in scores]
            weight_grads = [pair_rows(keys[spot_at, 1], grad_block) for spot_at in places]
            total = sum(jnp.sum(member, axis=0, keepdims=True) for member in grown)
            share = 1.0 / total
            delta = share * sum(
                jnp.sum(member * other, axis=0, keepdims=True)
                for member, other in zip(grown, weight_grads)
            )
            query_sum = None
            for spot_at, member, other in zip(places, grown, weight_grads):
                weights = member * share
                score_low = (weights * (other - delta)).astype(jnp.bfloat16)
                sums[spot_at, 1] += product(weights.astype(jnp.bfloat16), grad_block)
                sums[spot_at, 0] += product(score_low, query_block) * SCALE
                term = product(keys[spot_at, 0].T, score_low)
                query_sum = term if query_sum is None else query_sum + term
            query_out[away] = (query_sum * SCALE).T.astype(jnp.bfloat16)

        for slots in range(1, MAXK + 1):
            pl.when(count == slots)(functools.partial(live, slots))
        return carry

    lax.fori_loop(0, GROUP, query_step, 0)
    for index in range(GROUP + 1):
        low[index] = sums[2 * index + jnp.where(core == 0, 1, 2)].astype(jnp.bfloat16)
    copies = [(query_out.at[away], out) for away, out in enumerate((d0, d1, d2, d3))]
    copies += [(sums.at[2 * index + core], near_out.at[index]) for index in range(GROUP + 2)]
    copies.append((low, far_out))
    copy_all(copies, sem)


def grads(at, place, lists, counts, keys, swapped, below, above, swapped_edge, rows):
    block = (BLOCK, HEAD_DIM)
    outs = [jax.ShapeDtypeStruct(block, jnp.bfloat16)] * GROUP
    outs.append(jax.ShapeDtypeStruct((GROUP + 2, 2) + block, jnp.float32))
    outs.append(jax.ShapeDtypeStruct((GROUP + 1, 2) + block, jnp.bfloat16))
    pairs = 8 * BLOCK * BLOCK
    return pl.pallas_call(
        functools.partial(grads_kernel, at),
        out_shape=outs,
        in_specs=[SCALARS] * 3 + [ANYWHERE] * (3 * GROUP + 3),
        out_specs=[ANYWHERE] * len(outs),
        scratch_shapes=[
            pltpu.VMEM((WINDOW, 2) + block, jnp.bfloat16),
            pltpu.VMEM((GROUP, 2) + block, jnp.bfloat16),
            pltpu.VMEM((WINDOW, 2) + block, jnp.float32),
            pltpu.VMEM((GROUP,) + block, jnp.bfloat16),
            pltpu.VMEM((GROUP + 1, 2) + block, jnp.bfloat16),
            pltpu.SemaphoreType.DMA((3 * GROUP + 3,)),
        ],
        compiler_params=pltpu.CompilerParams(vmem_limit_bytes=VMEM_LIMIT),
        cost_estimate=pl.CostEstimate(
            flops=10 * pairs * HEAD_DIM, bytes_accessed=8 << 20, transcendentals=pairs
        ),
        name="grads",
    )(place, lists, counts, *keys, *swapped, below, above, swapped_edge, *rows)


def settle_kernel(place, near, far, below, above, o0, o1, o2, o3):
    spot, core = place[0] & (GROUP - 1), place[1]
    for away, out in enumerate((o0, o1, o2, o3)):
        index = spot ^ away
        total = near[index + 1] + far[index + core].astype(jnp.float32)
        total += jnp.where(index == 0, below[...].astype(jnp.float32), 0.0)
        total += jnp.where(index == GROUP - 1, above[...].astype(jnp.float32), 0.0)
        out[...] = total.astype(jnp.bfloat16)


def settle(place, near, far, below, above):
    out = jax.ShapeDtypeStruct((2, BLOCK, HEAD_DIM), jnp.bfloat16)
    return pl.pallas_call(
        settle_kernel,
        out_shape=[out] * GROUP,
        in_specs=[SCALARS] + [FAST] * 4,
        out_specs=[FAST] * GROUP,
        compiler_params=pltpu.CompilerParams(vmem_limit_bytes=VMEM_LIMIT),
        cost_estimate=pl.CostEstimate(flops=4 << 20, bytes_accessed=6 << 20, transcendentals=0),
        name="settle",
    )(place, near, far, below, above)


def gather_kernel(head, kept, place, *refs):
    queries, others = refs[:GROUP], refs[GROUP : 2 * GROUP]
    query_out, key_out, value_out = refs[2 * GROUP + kept : 2 * GROUP + kept + 3]
    sem = refs[-1]
    spot = place[0] & (GROUP - 1)
    copies = []
    for away in range(GROUP):
        columns = head_columns(spot ^ away, head)
        copies.append((queries[away], query_out.at[:, columns]))
        copies.append((others[away].at[0], key_out.at[:, columns]))
        copies.append((others[away].at[1], value_out.at[:, columns]))
    copy_all(copies, sem)


def gather(head, place, queries, others, so_far):
    kept = len(so_far)
    out = jax.ShapeDtypeStruct((BLOCK, HEADS * HEAD_DIM), jnp.bfloat16)
    return pl.pallas_call(
        functools.partial(gather_kernel, head, kept),
        out_shape=[out] * 3,
        in_specs=[SCALARS] + [ANYWHERE] * (2 * GROUP + kept),
        out_specs=[ANYWHERE] * 3,
        scratch_shapes=[pltpu.SemaphoreType.DMA((3 * GROUP,))],
        input_output_aliases={1 + 2 * GROUP + at: at for at in range(kept)},
        name="gather",
    )(place, *queries, *others, *so_far)


def shards(query_rows, key_rows, value_rows, out_grad, key_blocks, block_counts):
    chips = lax.axis_size("seq")
    chip = lax.axis_index("seq")
    core = lax.axis_index("head")
    spot = chip & (GROUP - 1)
    place = jnp.stack([chip, core]).astype(jnp.int32)
    lists = key_blocks.reshape(-1)

    def swap(member):
        return lax.ppermute(member, "head", [(0, 1), (1, 0)])

    def across(members):
        return [members[0]] + [
            lax.ppermute(members[away], "seq", [(c, c ^ away) for c in range(chips)])
            for away in range(1, GROUP)
        ]

    def upward(member):
        return lax.ppermute(member, "seq", [(c, c + GROUP) for c in range(chips - GROUP)])

    def downward(member):
        return lax.ppermute(member, "seq", [(c + GROUP, c) for c in range(chips - GROUP)])

    def pick(members, which):
        return lax.select_n(which, *members)

    where = {}
    windows = []
    for group, heads in enumerate(KEY_GROUPS):
        keys = across(pack(place, key_rows, value_rows, heads))
        from_below = upward(pick(keys, spot ^ (GROUP - 1)))
        from_above = downward(pick(keys, spot))
        swapped = [swap(member) for member in keys]
        swapped_edge = swap(jnp.where(core == 1, from_below, from_above))
        windows.append((keys, swapped, from_below, from_above, swapped_edge))
        for at, head in enumerate(heads):
            where[head] = (group, at)

    results = ()
    for head in range(SHARE):
        rows = across(pack(place, query_rows, out_grad, (head,)))
        group, at = where[head]
        *query_grads, near, far = grads(at, place, lists, block_counts, *windows[group], rows)
        query_grads = across(query_grads)
        far = swap(far)
        edge_low = near[0] + jnp.where(core == 1, far[0].astype(jnp.float32), 0.0)
        edge_high = near[GROUP + 1] + jnp.where(core == 0, far[GROUP].astype(jnp.float32), 0.0)
        from_above = downward(edge_low.astype(jnp.bfloat16))
        from_below = upward(edge_high.astype(jnp.bfloat16))
        others = across(settle(place, near, far, from_below, from_above))
        results = gather(head, place, query_grads, others, results)
    return tuple(results)


def solution(mesh):
    rows = P(("seq", "head"), None)
    return jax.shard_map(
        shards,
        mesh=mesh,
        in_specs=(rows, rows, rows, rows, P(), P()),
        out_specs=(rows, rows, rows),
        check_vma=False,
    )
```

time: 765 us -> 549 us (0.72)
  the two profiles are of different devices: /device:TPU:9 before, /device:TPU:0 now
where the time goes in v2:
time: 549 us; the launch traced here: 548 us
  Pallas kernels  404 us (74%)
  starting transfers between devices  67.5 us (12%)
  waiting for transfers between devices  44.2 us (8%)
  local copies, waits for them, and re-layouts  21.6 us (4%)
  other arithmetic  8.64 us (2%)
    pallas_call x5, Pallas kernels, pack(): pl.pallas_call(functools.partial(pack_kernel, heads), out_shape=[out] * G...  200 us
    pallas_call x3, Pallas kernels, gather(): pl.pallas_call(functools.partial(gather_kernel, head, kept), out_shape=[o...  149 us
    pallas_call x3, Pallas kernels, grads(): pl.pallas_call(functools.partial(grads_kernel, at), out_shape=outs, in_sp...  49.7 us
    ppermute x33, starting transfers between devices, across(): lax.ppermute(members[away], 'seq', [(c, c ^ away) for c in range(chips)])  40.7 us
    ppermute x33, waiting for transfers between devices, across(): lax.ppermute(members[away], 'seq', [(c, c ^ away) for c in range(chips)])  35.5 us
    unnamed x153, local copies, waits for them, and re-layouts  21.5 us
    ppermute x5, starting transfers between devices, upward(): lax.ppermute(member, 'seq', [(c, c + GROUP) for c in range(chips - GROUP)])  18.5 us
  transfers between devices with their start and end apart: 56, of which 13 were waited for; matrix products, arithmetic and copies ran while one was open for 1% of the time, Pallas kernels for 59%

profile of v2, /device:TPU:0, one launch (start us, length us, event | category | flops | bytes accessed | tf_op | source)
XLA Modules:
  0.0 547.7 jit_solution(8119945360502055396)
XLA Ops:
  1.3 33.6 %pack.8 = (bf16[2,512,128]{2,1,0:T(8,128)(2,1)}, bf16[2,512,128]{2,1,0:T(8,128)(2,1)}, bf16[2,512,128]{2,1,0:T(8,128)(2,1)}, bf16[2,512,128]{2,1,0:T(8,128)(2,1)}) custom-call(s32[2]{0:T(128)} %pad_add_fusion.place, bf16[512,1536]{1,0:T(8,128)(2,1)} %first.8, bf16[512,1536]{1,0:T(8,128)(2,1)} %second.8), custom_call_target="tpu_custom_call" | custom-call | tf_op jit(solution)/shard_map/pack/pallas_call | solution.py:67
  34.9 3.0 collective-permute-start.34
  39.4 65.4 %pack.5 = (bf16[4,512,128]{2,1,0:T(8,128)(2,1)}, bf16[4,512,128]{2,1,0:T(8,128)(2,1)}, bf16[4,512,128]{2,1,0:T(8,128)(2,1)}, bf16[4,512,128]{2,1,0:T(8,128)(2,1)}) custom-call(s32[2]{0:T(128)} %pad_add_fusion.place, bf16[512,1536]{1,0:T(8,128)(2,1)} %first.8, bf16[512,1536]{1,0:T(8,128)(2,1)} %second.8), custom_call_target="tpu_custom_call" | custom-call | tf_op jit(solution)/shard_map/pack/pallas_call | solution.py:67
  104.9 2.0 collective-permute-start
  108.4 33.6 %pack.7 = (bf16[2,512,128]{2,1,0:T(8,128)(2,1)}, bf16[2,512,128]{2,1,0:T(8,128)(2,1)}, bf16[2,512,128]{2,1,0:T(8,128)(2,1)}, bf16[2,512,128]{2,1,0:T(8,128)(2,1)}) custom-call(s32[2]{0:T(128)} %pad_add_fusion.place, bf16[512,1536]{1,0:T(8,128)(2,1)} %first.9, bf16[512,1536]{1,0:T(8,128)(2,1)} %second.9), custom_call_target="tpu_custom_call" | custom-call | tf_op jit(solution)/shard_map/pack/pallas_call | solution.py:67
  142.1 33.7 %pack.9 = (bf16[2,512,128]{2,1,0:T(8,128)(2,1)}, bf16[2,512,128]{2,1,0:T(8,128)(2,1)}, bf16[2,512,128]{2,1,0:T(8,128)(2,1)}, bf16[2,512,128]{2,1,0:T(8,128)(2,1)}) custom-call(s32[2]{0:T(128)} %pad_add_fusion.place, bf16[512,1536]{1,0:T(8,128)(2,1)} %first.9, bf16[512,1536]{1,0:T(8,128)(2,1)} %second.9), custom_call_target="tpu_custom_call" | custom-call | tf_op jit(solution)/shard_map/pack/pallas_call | solution.py:67
  175.9 2.0 collective-permute-start.22
  178.0 4.6 collective-permute-done.22.q1
  189.8 6.9 %collective-permute-done.23.q2 = bf16[2,512,128]{2,1,0:T(8,128)(2,1)S(1)} collective-permute-done((bf16[2,512,128]{2,1,0:T(8,128)(2,1)S(1)}, bf16[2,512,128]{2,1,0:T(8,128)(2,1)S(1)}, u32[]{:S(2)}, u32[]{:S(2)}) %collective-permute-start.23) | collective-permute-done | bytes 262176 | tf_op jit(solution)/shard_map/ppermute | solution.py:239
  197.4 2.0 collective-permute-start.46
  200.1 2.9 collective-permute-start.41
  205.7 5.4 collective-permute-start.7
  216.3 2.1 collective-permute-done.7.below
  218.5 5.6 %collective-permute-done.8.above = bf16[4,512,128]{2,1,0:T(8,128)(2,1)} collective-permute-done((bf16[4,512,128]{2,1,0:T(8,128)(2,1)}, bf16[4,512,128]{2,1,0:T(8,128)(2,1)}, u32[]{:S(2)}, u32[]{:S(2)}) %collective-permute-start.8) | collective-permute-done | bytes 524320 | tf_op jit(solution)/shard_map/ppermute | solution.py:247
  233.1 16.4 %grads.5 = (bf16[512,128]{1,0:T(8,128)(2,1)S(1)}, bf16[512,128]{1,0:T(8,128)(2,1)S(1)}, bf16[512,128]{1,0:T(8,128)(2,1)S(1)}, bf16[512,128]{1,0:T(8,128)(2,1)S(1...) custom-call(s32[2]{0:T(128)S(1)} %copy-done.18, s32[96]{0:T(128)S(1)} %reshape.45.lists, ...), custom_call_target="tpu_custom_call" | custom-call | flops 2684354560 | bytes 8388608 | tf_op jit(solution)/shard_map/grads/pallas_call | solution.py:154
  252.2 33.7 %pack.6 = (bf16[2,512,128]{2,1,0:T(8,128)(2,1)}, bf16[2,512,128]{2,1,0:T(8,128)(2,1)}, bf16[2,512,128]{2,1,0:T(8,128)(2,1)}, bf16[2,512,128]{2,1,0:T(8,128)(2,1)}) custom-call(s32[2]{0:T(128)} %pad_add_fusion.place, bf16[512,1536]{1,0:T(8,128)(2,1)} %first.9, bf16[512,1536]{1,0:T(8,128)(2,1)} %second.9), custom_call_target="tpu_custom_call" | custom-call | tf_op jit(solution)/shard_map/pack/pallas_call | solution.py:67
  287.3 2.2 collective-permute-start.12
  289.6 16.6 %grads.4 = (bf16[512,128]{1,0:T(8,128)(2,1)S(1)}, bf16[512,128]{1,0:T(8,128)(2,1)S(1)}, bf16[512,128]{1,0:T(8,128)(2,1)S(1)}, bf16[512,128]{1,0:T(8,128)(2,1)S(1...) custom-call(s32[2]{0:T(128)S(1)} %copy-done.19, s32[96]{0:T(128)S(1)} %reshape.45.lists, ...), custom_call_target="tpu_custom_call" | custom-call | flops 2684354560 | bytes 8388608 | tf_op jit(solution)/shard_map/grads/pallas_call | solution.py:154
  310.0 16.8 %grads.3 = (bf16[512,128]{1,0:T(8,128)(2,1)S(1)}, bf16[512,128]{1,0:T(8,128)(2,1)S(1)}, bf16[512,128]{1,0:T(8,128)(2,1)S(1)}, bf16[512,128]{1,0:T(8,128)(2,1)S(1...) custom-call(s32[2]{0:T(128)S(1)} %copy-done.19, s32[96]{0:T(128)S(1)} %reshape.45.lists, ...), custom_call_target="tpu_custom_call" | custom-call | flops 2684354560 | bytes 8388608 | tf_op jit(solution)/shard_map/grads/pallas_call | solution.py:154
  338.1 4.4 collective-permute-start.29
  344.1 1.9 settle.5
  353.3 2.0 collective-permute-done.25.refs_1_
  355.3 2.0 collective-permute-start.27
  357.3 4.6 collective-permute-start.17
  363.2 1.9 settle.4
  371.1 1.9 settle.3
  373.8 6.9 %collective-permute-done.54.refs_6_ = bf16[2,512,128]{2,1,0:T(8,128)(2,1)S(1)} collective-permute-done((bf16[2,512,128]{2,1,0:T(8,128)(2,1)S(1)}, bf16[2,512,128]{2,1,0:T(8,128)(2,1)S(1)}, u32[]{:S(2)}, u32[]{:S(2)}) %collective-permute-start.54) | collective-permute-done | bytes 262176 | tf_op jit(solution)/shard_map/ppermute | solution.py:239
  382.2 2.0 collective-permute-start.21
  384.2 11.9 %collective-permute-done.32.refs_6_ = bf16[2,512,128]{2,1,0:T(8,128)(2,1)S(1)} collective-permute-done((bf16[2,512,128]{2,1,0:T(8,128)(2,1)S(1)}, bf16[2,512,128]{2,1,0:T(8,128)(2,1)S(1)}, u32[]{:S(2)}, u32[]{:S(2)}) %collective-permute-start.32) | collective-permute-done | bytes 262176 | tf_op jit(solution)/shard_map/ppermute | solution.py:239
  397.9 49.5 %gather.3 = (bf16[512,1536]{1,0:T(8,128)(2,1)}, bf16[512,1536]{1,0:T(8,128)(2,1)}, bf16[512,1536]{1,0:T(8,128)(2,1)}) custom-call(s32[2]{0:T(128)} %pad_add_fusion.place, bf16[512,128]{1,0:T(8,128)(2,1)} %copy-done.15, bf16[512,128]{1,0:T(8,128)(2,1)} %copy-done.60, bf16[512,128]{1,0:T(8,128)(2,1)} %copy-done.62, bf16[512,128]{1,0:T(8,128)(2,1)} %copy-done.63, ...), custom_call_target="tpu_custom_call" | custom-call | tf_op jit(solution)/shard_map/gather/pallas_call | solution.py:215
  447.5 49.5 %gather.4 = (bf16[512,1536]{1,0:T(8,128)(2,1)}, bf16[512,1536]{1,0:T(8,128)(2,1)}, bf16[512,1536]{1,0:T(8,128)(2,1)}) custom-call(s32[2]{0:T(128)} %pad_add_fusion.place, bf16[512,128]{1,0:T(8,128)(2,1)} %copy-done.17, bf16[512,128]{1,0:T(8,128)(2,1)} %copy-done.64, ...), custom_call_target="tpu_custom_call", output_to_operand_aliasing={{0}: (9, {}), {1}: (10, {}), {2}: (11, {})} | custom-call | tf_op jit(solution)/shard_map/gather/pallas_call | solution.py:215
  498.0 49.5 %gather.5 = (bf16[512,1536]{1,0:T(8,128)(2,1)}, bf16[512,1536]{1,0:T(8,128)(2,1)}, bf16[512,1536]{1,0:T(8,128)(2,1)}) custom-call(s32[2]{0:T(128)} %pad_add_fusion.place, bf16[512,128]{1,0:T(8,128)(2,1)} %copy-done.16, bf16[512,128]{1,0:T(8,128)(2,1)} %copy-done.61, ...), custom_call_target="tpu_custom_call", output_to_operand_aliasing={{0}: (9, {}), {1}: (10, {}), {2}: (11, {})} | custom-call | tf_op jit(solution)/shard_map/gather/pallas_call | solution.py:215
  (256 shorter events, 69.4 us)
Async XLA Ops:
  34.9 73.5 %collective-permute-start.34 = (bf16[2,512,128]{2,1,0:T(8,128)(2,1)}, bf16[2,512,128]{2,1,0:T(8,128)(2,1)S(1)}, u32[]{:S(2)}, u32[]{:S(2)}) collective-permute-start(bf16[2,512,128]{2,1,0:T(8,128)(2,1)} %get-tuple-element.92), channel_id=1, source_target_pairs={{0,2},{2,0},{4,6},{6,4},{8,10},{10,8},{12,14},{14,12},{16,18},{18,... | collective-permute-start | bytes 786440 | tf_op jit(solution)/shard_map/ppermute | solution.py:239
  37.9 138.0 %collective-permute-start.35 = (bf16[2,512,128]{2,1,0:T(8,128)(2,1)}, bf16[2,512,128]{2,1,0:T(8,128)(2,1)S(1)}, u32[]{:S(2)}, u32[]{:S(2)}) collective-permute-start(bf16[2,512,128]{2,1,0:T(8,128)(2,1)} %get-tuple-element.93), channel_id=1, source_target_pairs={{0,4},{2,6},{4,0},{6,2},{8,12},{10,14},{12,8},{14,10},{16,20},{18,... | collective-permute-start | bytes 786440 | tf_op jit(solution)/shard_map/ppermute | solution.py:239
  39.4 138.5 %collective-permute-start.36 = (bf16[2,512,128]{2,1,0:T(8,128)(2,1)}, bf16[2,512,128]{2,1,0:T(8,128)(2,1)S(1)}, u32[]{:S(2)}, u32[]{:S(2)}) collective-permute-start(bf16[2,512,128]{2,1,0:T(8,128)(2,1)} %get-tuple-element.94), channel_id=1, source_target_pairs={{0,6},{2,4},{4,2},{6,0},{8,14},{10,12},{12,10},{14,8},{16,22},{18,... | collective-permute-start | bytes 786440 | tf_op jit(solution)/shard_map/ppermute | solution.py:239
  104.9 80.1 %collective-permute-start = (bf16[4,512,128]{2,1,0:T(8,128)(2,1)}, bf16[4,512,128]{2,1,0:T(8,128)(2,1)S(1)}, u32[]{:S(2)}, u32[]{:S(2)}) collective-permute-start(bf16[4,512,128]{2,1,0:T(8,128)(2,1)} %get-tuple-element.60), channel_id=1, source_target_pairs={{0,2},{2,0},{4,6},{6,4},{8,10},{10,8},{12,14},{14,12},{16,18},{18,... | collective-permute-start | bytes 1572872 | tf_op jit(solution)/shard_map/ppermute | solution.py:239
  106.9 79.6 %collective-permute-start.1 = (bf16[4,512,128]{2,1,0:T(8,128)(2,1)}, bf16[4,512,128]{2,1,0:T(8,128)(2,1)S(1)}, u32[]{:S(2)}, u32[]{:S(2)}) collective-permute-start(bf16[4,512,128]{2,1,0:T(8,128)(2,1)} %get-tuple-element.61), channel_id=1, source_target_pairs={{0,4},{2,6},{4,0},{6,2},{8,12},{10,14},{12,8},{14,10},{16,20},{18,... | collective-permute-start | bytes 1572872 | tf_op jit(solution)/shard_map/ppermute | solution.py:239
  108.4 78.5 %collective-permute-start.2 = (bf16[4,512,128]{2,1,0:T(8,128)(2,1)}, bf16[4,512,128]{2,1,0:T(8,128)(2,1)S(1)}, u32[]{:S(2)}, u32[]{:S(2)}) collective-permute-start(bf16[4,512,128]{2,1,0:T(8,128)(2,1)} %get-tuple-element.62), channel_id=1, source_target_pairs={{0,6},{2,4},{4,2},{6,0},{8,14},{10,12},{12,10},{14,8},{16,22},{18,... | collective-permute-start | bytes 1572872 | tf_op jit(solution)/shard_map/ppermute | solution.py:239
  177.9 25.1 %collective-permute-start.37 = (bf16[2,512,128]{2,1,0:T(8,128)(2,1)S(1)}, bf16[2,512,128]{2,1,0:T(8,128)(2,1)S(1)}, u32[]{:S(2)}, u32[]{:S(2)}) collective-permute-start(bf16[2,512,128]{2,1,0:T(8,128)(2,1)S(1)} %copy-done.13), channel_id=1, source_target_pairs={{0,1},{1,0},{2,3},{3,2},{4,5},{5,4},{6,7},{7,6},{8,9},{9,8},{10,11... | collective-permute-start | bytes 786440 | tf_op jit(solution)/shard_map/ppermute | solution.py:235
  186.5 18.5 %collective-permute-start.44 = (bf16[2,512,128]{2,1,0:T(8,128)(2,1)S(1)}, bf16[2,512,128]{2,1,0:T(8,128)(2,1)S(1)}, u32[]{:S(2)}, u32[]{:S(2)}) collective-permute-start(bf16[2,512,128]{2,1,0:T(8,128)(2,1)S(1)} %copy-done.72), channel_id=1, source_target_pairs={{0,2},{2,0},{4,6},{6,4},{8,10},{10,8},{12,14},{14,12},{16,18},{18,... | collective-permute-start | bytes 786440 | tf_op jit(solution)/shard_map/ppermute | solution.py:239
  187.0 24.1 %collective-permute-start.45 = (bf16[2,512,128]{2,1,0:T(8,128)(2,1)S(1)}, bf16[2,512,128]{2,1,0:T(8,128)(2,1)S(1)}, u32[]{:S(2)}, u32[]{:S(2)}) collective-permute-start(bf16[2,512,128]{2,1,0:T(8,128)(2,1)S(1)} %copy-done.71), channel_id=1, source_target_pairs={{0,4},{2,6},{4,0},{6,2},{8,12},{10,14},{12,8},{14,10},{16,20},{18,... | collective-permute-start | bytes 786440 | tf_op jit(solution)/shard_map/ppermute | solution.py:239
  197.4 15.7 %collective-permute-start.46 = (bf16[2,512,128]{2,1,0:T(8,128)(2,1)S(1)}, bf16[2,512,128]{2,1,0:T(8,128)(2,1)S(1)}, u32[]{:S(2)}, u32[]{:S(2)}) collective-permute-start(bf16[2,512,128]{2,1,0:T(8,128)(2,1)S(1)} %copy-done.70), channel_id=1, source_target_pairs={{0,6},{2,4},{4,2},{6,0},{8,14},{10,12},{12,10},{14,8},{16,22},{18,... | collective-permute-start | bytes 786440 | tf_op jit(solution)/shard_map/ppermute | solution.py:239
  215.4 36.0 %collective-permute-start.3 = (bf16[4,512,128]{2,1,0:T(8,128)(2,1)S(1)}, bf16[4,512,128]{2,1,0:T(8,128)(2,1)}, u32[]{:S(2)}, u32[]{:S(2)}) collective-permute-start(bf16[4,512,128]{2,1,0:T(8,128)(2,1)S(1)} %copy-done.3), channel_id=1, source_target_pairs={{0,1},{1,0},{2,3},{3,2},{4,5},{5,4},{6,7},{7,6},{8,9},{9,8},{10,11... | collective-permute-start | bytes 1572872 | tf_op jit(solution)/shard_map/ppermute | solution.py:235
  216.2 69.7 %collective-permute-start.4 = (bf16[4,512,128]{2,1,0:T(8,128)(2,1)S(1)}, bf16[4,512,128]{2,1,0:T(8,128)(2,1)}, u32[]{:S(2)}, u32[]{:S(2)}) collective-permute-start(bf16[4,512,128]{2,1,0:T(8,128)(2,1)S(1)} %collective-permute-done.k1), channel_id=1, source_target_pairs={{0,1},{1,0},{2,3},{3,2},{4,5},{5,4},{6,7},{7,6},{8,9},{9,8},{10,11... | collective-permute-start | bytes 1572872 | tf_op jit(solution)/shard_map/ppermute | solution.py:235
  218.5 68.3 %collective-permute-start.5 = (bf16[4,512,128]{2,1,0:T(8,128)(2,1)S(1)}, bf16[4,512,128]{2,1,0:T(8,128)(2,1)}, u32[]{:S(2)}, u32[]{:S(2)}) collective-permute-start(bf16[4,512,128]{2,1,0:T(8,128)(2,1)S(1)} %collective-permute-done.1.k2), channel_id=1, source_target_pairs={{0,1},{1,0},{2,3},{3,2},{4,5},{5,4},{6,7},{7,6},{8,9},{9,8},{10,11... | collective-permute-start | bytes 1572872 | tf_op jit(solution)/shard_map/ppermute | solution.py:235
  224.1 63.2 %collective-permute-start.6 = (bf16[4,512,128]{2,1,0:T(8,128)(2,1)S(1)}, bf16[4,512,128]{2,1,0:T(8,128)(2,1)}, u32[]{:S(2)}, u32[]{:S(2)}) collective-permute-start(bf16[4,512,128]{2,1,0:T(8,128)(2,1)S(1)} %collective-permute-done.2.k3), channel_id=1, source_target_pairs={{0,1},{1,0},{2,3},{3,2},{4,5},{5,4},{6,7},{7,6},{8,9},{9,8},{10,11... | collective-permute-start | bytes 1572872 | tf_op jit(solution)/shard_map/ppermute | solution.py:235
  226.7 62.8 %collective-permute-start.9 = (bf16[4,512,128]{2,1,0:T(8,128)(2,1)}, bf16[4,512,128]{2,1,0:T(8,128)(2,1)}, u32[]{:S(2)}, u32[]{:S(2)}) collective-permute-start(bf16[4,512,128]{2,1,0:T(8,128)(2,1)} %broadcast_select_fusion), channel_id=1, source_target_pairs={{0,1},{1,0},{2,3},{3,2},{4,5},{5,4},{6,7},{7,6},{8,9},{9,8},{10,11... | collective-permute-start | bytes 1572872 | tf_op jit(solution)/shard_map/ppermute | solution.py:235
  252.1 76.8 %collective-permute-start.50 = (bf16[5,2,512,128]{3,2,1,0:T(8,128)(2,1)}, bf16[5,2,512,128]{3,2,1,0:T(8,128)(2,1)}, u32[]{:S(2)}, u32[]{:S(2)}) collective-permute-start(bf16[5,2,512,128]{3,2,1,0:T(8,128)(2,1)} %get-tuple-element.104), channel_id=1, source_target_pairs={{0,1},{1,0},{2,3},{3,2},{4,5},{5,4},{6,7},{7,6},{8,9},{9,8},{10,11... | collective-permute-start | bytes 3932168 | tf_op jit(solution)/shard_map/ppermute | solution.py:235
  285.9 20.9 %collective-permute-start.10 = (bf16[2,512,128]{2,1,0:T(8,128)(2,1)}, bf16[2,512,128]{2,1,0:T(8,128)(2,1)S(1)}, u32[]{:S(2)}, u32[]{:S(2)}) collective-permute-start(bf16[2,512,128]{2,1,0:T(8,128)(2,1)} %get-tuple-element.64), channel_id=1, source_target_pairs={{0,2},{2,0},{4,6},{6,4},{8,10},{10,8},{12,14},{14,12},{16,18},{18,... | collective-permute-start | bytes 786440 | tf_op jit(solution)/shard_map/ppermute | solution.py:239
  286.7 20.1 %collective-permute-start.11 = (bf16[2,512,128]{2,1,0:T(8,128)(2,1)}, bf16[2,512,128]{2,1,0:T(8,128)(2,1)S(1)}, u32[]{:S(2)}, u32[]{:S(2)}) collective-permute-start(bf16[2,512,128]{2,1,0:T(8,128)(2,1)} %get-tuple-element.65), channel_id=1, source_target_pairs={{0,4},{2,6},{4,0},{6,2},{8,12},{10,14},{12,8},{14,10},{16,20},{18,... | collective-permute-start | bytes 786440 | tf_op jit(solution)/shard_map/ppermute | solution.py:239
  287.3 19.5 %collective-permute-start.12 = (bf16[2,512,128]{2,1,0:T(8,128)(2,1)}, bf16[2,512,128]{2,1,0:T(8,128)(2,1)S(1)}, u32[]{:S(2)}, u32[]{:S(2)}) collective-permute-start(bf16[2,512,128]{2,1,0:T(8,128)(2,1)} %get-tuple-element.66), channel_id=1, source_target_pairs={{0,6},{2,4},{4,2},{6,0},{8,14},{10,12},{12,10},{14,8},{16,22},{18,... | collective-permute-start | bytes 786440 | tf_op jit(solution)/shard_map/ppermute | solution.py:239
  306.8 28.7 %collective-permute-start.28 = (bf16[5,2,512,128]{3,2,1,0:T(8,128)(2,1)}, bf16[5,2,512,128]{3,2,1,0:T(8,128)(2,1)}, u32[]{:S(2)}, u32[]{:S(2)}) collective-permute-start(bf16[5,2,512,128]{3,2,1,0:T(8,128)(2,1)} %get-tuple-element.86), channel_id=1, source_target_pairs={{0,1},{1,0},{2,3},{3,2},{4,5},{5,4},{6,7},{7,6},{8,9},{9,8},{10,11... | collective-permute-start | bytes 3932168 | tf_op jit(solution)/shard_map/ppermute | solution.py:235
  328.2 20.0 %collective-permute-start.16 = (bf16[5,2,512,128]{3,2,1,0:T(8,128)(2,1)}, bf16[5,2,512,128]{3,2,1,0:T(8,128)(2,1)}, u32[]{:S(2)}, u32[]{:S(2)}) collective-permute-start(bf16[5,2,512,128]{3,2,1,0:T(8,128)(2,1)} %get-tuple-element.72), channel_id=1, source_target_pairs={{0,1},{1,0},{2,3},{3,2},{4,5},{5,4},{6,7},{7,6},{8,9},{9,8},{10,11... | collective-permute-start | bytes 3932168 | tf_op jit(solution)/shard_map/ppermute | solution.py:235
  338.1 19.2 %collective-permute-start.29 = (bf16[2,512,128]{2,1,0:T(8,128)(2,1)S(1)}, bf16[2,512,128]{2,1,0:T(8,128)(2,1)S(1)}, u32[]{:S(2)}, u32[]{:S(2)}) collective-permute-start(bf16[2,512,128]{2,1,0:T(8,128)(2,1)S(1)} %get-tuple-element.118), channel_id=1, source_target_pairs={{0,8},{2,10},{4,12},{6,14},{8,16},{10,18},{12,20},{14,22},{16,24},... | collective-permute-start | bytes 786440 | tf_op jit(solution)/shard_map/ppermute | solution.py:244
  342.5 19.4 %collective-permute-start.30 = (bf16[2,512,128]{2,1,0:T(8,128)(2,1)S(1)}, bf16[2,512,128]{2,1,0:T(8,128)(2,1)S(1)}, u32[]{:S(2)}, u32[]{:S(2)}) collective-permute-start(bf16[2,512,128]{2,1,0:T(8,128)(2,1)S(1)} %get-tuple-element.117), channel_id=1, source_target_pairs={{8,0},{10,2},{12,4},{14,6},{16,8},{18,10},{20,12},{22,14},{24,16},... | collective-permute-start | bytes 786440 | tf_op jit(solution)/shard_map/ppermute | solution.py:247
  348.2 19.4 %collective-permute-start.53 = (bf16[2,512,128]{2,1,0:T(8,128)(2,1)S(1)}, bf16[2,512,128]{2,1,0:T(8,128)(2,1)S(1)}, u32[]{:S(2)}, u32[]{:S(2)}) collective-permute-start(bf16[2,512,128]{2,1,0:T(8,128)(2,1)S(1)} %get-tuple-element.106), channel_id=1, source_target_pairs={{0,2},{2,0},{4,6},{6,4},{8,10},{10,8},{12,14},{14,12},{16,18},{18,... | collective-permute-start | bytes 786440 | tf_op jit(solution)/shard_map/ppermute | solution.py:239
  365.8 14.9 %collective-permute-start.54 = (bf16[2,512,128]{2,1,0:T(8,128)(2,1)S(1)}, bf16[2,512,128]{2,1,0:T(8,128)(2,1)S(1)}, u32[]{:S(2)}, u32[]{:S(2)}) collective-permute-start(bf16[2,512,128]{2,1,0:T(8,128)(2,1)S(1)} %get-tuple-element.107), channel_id=1, source_target_pairs={{0,4},{2,6},{4,0},{6,2},{8,12},{10,14},{12,8},{14,10},{16,20},{18,... | collective-permute-start | bytes 786440 | tf_op jit(solution)/shard_map/ppermute | solution.py:239
  369.3 26.8 %collective-permute-start.32 = (bf16[2,512,128]{2,1,0:T(8,128)(2,1)S(1)}, bf16[2,512,128]{2,1,0:T(8,128)(2,1)S(1)}, u32[]{:S(2)}, u32[]{:S(2)}) collective-permute-start(bf16[2,512,128]{2,1,0:T(8,128)(2,1)S(1)} %get-tuple-element.89), channel_id=1, source_target_pairs={{0,4},{2,6},{4,0},{6,2},{8,12},{10,14},{12,8},{14,10},{16,20},{18,... | collective-permute-start | bytes 786440 | tf_op jit(solution)/shard_map/ppermute | solution.py:239
  370.2 26.8 %collective-permute-start.33 = (bf16[2,512,128]{2,1,0:T(8,128)(2,1)S(1)}, bf16[2,512,128]{2,1,0:T(8,128)(2,1)S(1)}, u32[]{:S(2)}, u32[]{:S(2)}) collective-permute-start(bf16[2,512,128]{2,1,0:T(8,128)(2,1)S(1)} %get-tuple-element.90), channel_id=1, source_target_pairs={{0,6},{2,4},{4,2},{6,0},{8,14},{10,12},{12,10},{14,8},{16,22},{18,... | collective-permute-start | bytes 786440 | tf_op jit(solution)/shard_map/ppermute | solution.py:239
  380.7 116.4 %collective-permute-start.19 = (bf16[2,512,128]{2,1,0:T(8,128)(2,1)S(1)}, bf16[2,512,128]{2,1,0:T(8,128)(2,1)S(1)}, u32[]{:S(2)}, u32[]{:S(2)}) collective-permute-start(bf16[2,512,128]{2,1,0:T(8,128)(2,1)S(1)} %get-tuple-element.74), channel_id=1, source_target_pairs={{0,2},{2,0},{4,6},{6,4},{8,10},{10,8},{12,14},{14,12},{16,18},{18,... | collective-permute-start | bytes 786440 | tf_op jit(solution)/shard_map/ppermute | solution.py:239
  381.0 116.1 %collective-permute-start.20 = (bf16[2,512,128]{2,1,0:T(8,128)(2,1)S(1)}, bf16[2,512,128]{2,1,0:T(8,128)(2,1)S(1)}, u32[]{:S(2)}, u32[]{:S(2)}) collective-permute-start(bf16[2,512,128]{2,1,0:T(8,128)(2,1)S(1)} %get-tuple-element.75), channel_id=1, source_target_pairs={{0,4},{2,6},{4,0},{6,2},{8,12},{10,14},{12,8},{14,10},{16,20},{18,... | collective-permute-start | bytes 786440 | tf_op jit(solution)/shard_map/ppermute | solution.py:239
  382.2 114.9 %collective-permute-start.21 = (bf16[2,512,128]{2,1,0:T(8,128)(2,1)S(1)}, bf16[2,512,128]{2,1,0:T(8,128)(2,1)S(1)}, u32[]{:S(2)}, u32[]{:S(2)}) collective-permute-start(bf16[2,512,128]{2,1,0:T(8,128)(2,1)S(1)} %get-tuple-element.76), channel_id=1, source_target_pairs={{0,6},{2,4},{4,2},{6,0},{8,14},{10,12},{12,10},{14,8},{16,22},{18,... | collective-permute-start | bytes 786440 | tf_op jit(solution)/shard_map/ppermute | solution.py:239
  396.2 100.9 %collective-permute-start.14 = (bf16[512,128]{1,0:T(8,128)(2,1)S(1)}, bf16[512,128]{1,0:T(8,128)(2,1)S(1)}, u32[]{:S(2)}, u32[]{:S(2)}) collective-permute-start(bf16[512,128]{1,0:T(8,128)(2,1)S(1)} %get-tuple-element.69), channel_id=1, source_target_pairs={{0,4},{2,6},{4,0},{6,2},{8,12},{10,14},{12,8},{14,10},{16,20},{18,... | collective-permute-start | bytes 393224 | tf_op jit(solution)/shard_map/ppermute | solution.py:239
  397.0 100.1 %collective-permute-start.15 = (bf16[512,128]{1,0:T(8,128)(2,1)S(1)}, bf16[512,128]{1,0:T(8,128)(2,1)S(1)}, u32[]{:S(2)}, u32[]{:S(2)}) collective-permute-start(bf16[512,128]{1,0:T(8,128)(2,1)S(1)} %get-tuple-element.70), channel_id=1, source_target_pairs={{0,6},{2,4},{4,2},{6,0},{8,14},{10,12},{12,10},{14,8},{16,22},{18,... | collective-permute-start | bytes 393224 | tf_op jit(solution)/shard_map/ppermute | solution.py:239
  (100 other events, 1447.3 us)

commit v3 on v2

v3 whole, which is shorter than its diff:
```python
import functools
import math

import jax
import jax.numpy as jnp
from jax import lax
from jax.experimental import pallas as pl
from jax.experimental.pallas import tpu as pltpu
from jax.sharding import PartitionSpec as P

HEADS = 12
HEAD_DIM = 128
BLOCK = 512
MAXK = 3
GROUP = 4
SHARE = HEADS // GROUP
OWN = GROUP + 2
SEEN = OWN + GROUP + 1
FIRST, LAST = (0, 1), (2,)
SCALE = HEAD_DIM ** -0.5
LOG_SCALE = SCALE * math.log2(math.e)
COST_FLOPS, COST_BYTES = 1.15e+09, 3.00e+06
VMEM_LIMIT = 60 * 1024 * 1024

ANYWHERE = pl.BlockSpec(memory_space=pl.ANY)
SCALARS = pl.BlockSpec(memory_space=pltpu.SMEM)
FAST = pl.BlockSpec(memory_space=pltpu.VMEM)


def pair_rows(left, right):
    return lax.dot_general(
        left, right, (((1,), (1,)), ((), ())), preferred_element_type=jnp.float32
    )


def product(left, right):
    return jnp.dot(left, right, preferred_element_type=jnp.float32)


def copy_all(copies, sem):
    started = [
        pltpu.make_async_copy(source, target, sem.at[at])
        for at, (source, target) in enumerate(copies)
    ]
    for copy in started:
        copy.start()
    for copy in started:
        copy.wait()


def head_columns(spot, head):
    return pl.ds((spot * SHARE + head) * HEAD_DIM, HEAD_DIM)


def cost(microseconds):
    return pl.CostEstimate(
        flops=int(microseconds * COST_FLOPS),
        bytes_accessed=int(microseconds * COST_BYTES),
        transcendentals=0,
    )


def pack_kernel(heads, count, *refs):
    sources, out, sem = refs[:count], refs[-2], refs[-1]
    copies = []
    for spot in range(GROUP):
        for at, head in enumerate(heads):
            for index, source in enumerate(sources):
                target = out.at[spot, len(sources) * at + index]
                copies.append((source.at[:, head_columns(spot, head)], target))
    copy_all(copies, sem)


def pack(sources, heads, after=()):
    parts = len(sources) * len(heads)
    return pl.pallas_call(
        functools.partial(pack_kernel, heads, len(sources)),
        out_shape=jax.ShapeDtypeStruct((GROUP, parts, BLOCK, HEAD_DIM), sources[0].dtype),
        in_specs=[ANYWHERE] * (len(sources) + len(after)),
        out_specs=FAST,
        scratch_shapes=[pltpu.SemaphoreType.DMA((GROUP * parts,))],
        compiler_params=pltpu.CompilerParams(vmem_limit_bytes=VMEM_LIMIT),
        cost_estimate=cost(4),
        name="pack",
    )(*sources, *after)


def grads_kernel(heads, key_at, waited, place, lists, counts, *refs):
    near_keys, far_keys, below, above, cross, rows_in = refs[:6]
    refs = refs[6 + waited :]
    query_out, near_out, far_out, low_out, high_out, cross_out = refs[:6]
    keys, rows, sums, queries, rounded, sem = refs[6:]
    chip, core = place[0], place[1]
    here = chip & (GROUP - 1)
    first = 2 * (chip - here) - 2
    copies = []
    for head in range(heads):
        pair = pl.ds(key_at + 2 * head, 2)
        copies += [
            (near_keys.at[:, pair], keys.at[head, pl.ds(1, GROUP)]),
            (rows_in.at[:, pl.ds(2 * head, 2)], rows.at[head]),
            (far_keys.at[:, pair], keys.at[head, pl.ds(OWN, GROUP)]),
            (below.at[pair], keys.at[head, 0]),
            (above.at[pair], keys.at[head, OWN - 1]),
            (cross.at[pair], keys.at[head, SEEN - 1]),
        ]
    started = [
        pltpu.make_async_copy(source, target, sem.at[index])
        for index, (source, target) in enumerate(copies)
    ]
    for copy in started:
        copy.start()
    sums[...] = jnp.zeros_like(sums)
    for copy in started:
        copy.wait()

    def place_of(block):
        offset = block - first
        half = offset >> 1
        other = jnp.where((half >= 1) & (half <= GROUP), OWN - 1 + half, SEEN - 1)
        return jnp.where((offset & 1) == core, half, other)

    def query_step(spot, carry):
        block = first + 2 + 2 * spot + core
        count = counts[block]

        def live(slots, head):
            query_block, grad_block = rows[head, spot, 0], rows[head, spot, 1]
            places = [place_of(lists[block * MAXK + slot]) for slot in range(slots)]
            scores = [pair_rows(keys[head, at, 0], query_block) for at in places]
            peak = functools.reduce(
                jnp.maximum, [jnp.max(member, axis=0, keepdims=True) for member in scores]
            )
            grown = [jnp.exp2(member * LOG_SCALE - peak * LOG_SCALE) for member in scores]
            weight_grads = [pair_rows(keys[head, at, 1], grad_block) for at in places]
            total = sum(jnp.sum(member, axis=0, keepdims=True) for member in grown)
            share = 1.0 / total
            delta = share * sum(
                jnp.sum(member * other, axis=0, keepdims=True)
                for member, other in zip(grown, weight_grads)
            )
            query_sum = None
            for at, member, other in zip(places, grown, weight_grads):
                weights = member * share
                score_low = (weights * (other - delta)).astype(jnp.bfloat16)
                sums[head, at, 1] += product(weights.astype(jnp.bfloat16), grad_block)
                sums[head, at, 0] += product(score_low, query_block) * SCALE
                term = product(keys[head, at, 0].T, score_low)
                query_sum = term if query_sum is None else query_sum + term
            queries[spot, head] = (query_sum * SCALE).T.astype(jnp.bfloat16)

        def all_heads(slots):
            for head in range(heads):
                live(slots, head)

        for slots in range(1, MAXK + 1):
            pl.when(count == slots)(functools.partial(all_heads, slots))
        return carry

    lax.fori_loop(0, GROUP, query_step, 0)
    copies = [(queries, query_out)]
    for head in range(heads):
        copies.append((sums.at[head, pl.ds(1, GROUP)], near_out.at[:, head]))
        for index, spot in enumerate((*range(OWN, OWN + GROUP), 0, OWN - 1, SEEN - 1)):
            rounded[head, index] = sums[head, spot].astype(jnp.bfloat16)
        copies.append((rounded.at[head, pl.ds(0, GROUP)], far_out.at[:, head]))
        for index, out in enumerate((low_out, high_out, cross_out)):
            copies.append((rounded.at[head, GROUP + index], out.at[head]))
    copy_all(copies, sem)


def grads(heads, key_at, place, lists, counts, window, rows, after):
    block = (BLOCK, HEAD_DIM)
    edge = jax.ShapeDtypeStruct((heads, 2) + block, jnp.bfloat16)
    outs = [
        jax.ShapeDtypeStruct((GROUP, heads) + block, jnp.bfloat16),
        jax.ShapeDtypeStruct((GROUP, heads, 2) + block, jnp.float32),
        jax.ShapeDtypeStruct((GROUP, heads, 2) + block, jnp.bfloat16),
        edge,
        edge,
        edge,
    ]
    return pl.pallas_call(
        functools.partial(grads_kernel, heads, key_at, len(after)),
        out_shape=outs,
        in_specs=[SCALARS] * 3 + [ANYWHERE] * (6 + len(after)),
        out_specs=[ANYWHERE] * len(outs),
        scratch_shapes=[
            pltpu.VMEM((heads, SEEN, 2) + block, jnp.bfloat16),
            pltpu.VMEM((heads, GROUP, 2) + block, jnp.bfloat16),
            pltpu.VMEM((heads, SEEN, 2) + block, jnp.float32),
            pltpu.VMEM((GROUP, heads) + block, jnp.bfloat16),
            pltpu.VMEM((heads, GROUP + 3, 2) + block, jnp.bfloat16),
            pltpu.SemaphoreType.DMA((6 * heads,)),
        ],
        compiler_params=pltpu.CompilerParams(vmem_limit_bytes=VMEM_LIMIT),
        cost_estimate=cost(2 + 11 * heads),
        name="grads",
    )(place, lists, counts, *window, rows, *after)


def settle_kernel(waited, held, place, near, far, below, above, cross, *refs):
    count = len(refs) - 1 - waited - 2 * held
    queries, out = refs[:count], refs[count + held + waited]
    for source, target in zip(refs[count : count + held], refs[len(refs) - held :]):
        target[...] = source[...]
    spot, core = pl.program_id(0), place[1]
    out[0, :, :2] = (near[0] + far[0].astype(jnp.float32)).astype(jnp.bfloat16)
    if queries:
        out[0, :, 2] = queries[0][0]

    def more(*edges):
        total = near[0] + far[0].astype(jnp.float32)
        for edge in edges:
            total += edge[...].astype(jnp.float32)
        out[0, :, :2] = total.astype(jnp.bfloat16)

    pl.when((spot == 0) & (core == 0))(lambda: more(below, cross))
    pl.when((spot == 0) & (core == 1))(lambda: more(below))
    pl.when((spot == GROUP - 1) & (core == 0))(lambda: more(above))
    pl.when((spot == GROUP - 1) & (core == 1))(lambda: more(above, cross))


def settle(place, near, far, edges, queries, after, held=()):
    heads = near.shape[1]
    block = (BLOCK, HEAD_DIM)
    parts = 3 if queries else 2
    by_spot = pl.BlockSpec((1, heads, 2) + block, lambda spot: (spot, 0, 0, 0, 0))
    whole = pl.BlockSpec((heads, 2) + block, lambda spot: (0, 0, 0, 0))
    kept = pl.BlockSpec((1, 2) + block, lambda spot: (0, 0, 0, 0))
    query = pl.BlockSpec((1, heads) + block, lambda spot: (spot, 0, 0, 0))
    return pl.pallas_call(
        functools.partial(settle_kernel, len(after), len(held)),
        grid=(GROUP,),
        out_shape=[jax.ShapeDtypeStruct((GROUP, heads, parts) + block, jnp.bfloat16)]
        + [jax.ShapeDtypeStruct(member.shape, member.dtype) for member in held],
        in_specs=[SCALARS, by_spot, by_spot]
        + [whole] * 3
        + [query] * len(queries)
        + [kept] * len(held)
        + [ANYWHERE] * len(after),
        out_specs=[pl.BlockSpec((1, heads, parts) + block, lambda spot: (spot, 0, 0, 0, 0))]
        + [kept] * len(held),
        compiler_params=pltpu.CompilerParams(vmem_limit_bytes=VMEM_LIMIT),
        cost_estimate=cost(2 + 2 * heads),
        name="settle",
    )(place, near, far, *edges, *queries, *held, *after)


def gather_kernel(heads, members, *refs):
    pieces, outs, sem = refs[:members], refs[-4:-1], refs[-1]
    key_out, value_out, query_out = outs
    copies = []
    for spot in range(GROUP):
        for at, head in enumerate(heads):
            columns = head_columns(spot, head)
            others = pieces[0].at[spot, at]
            query = pieces[1].at[spot, at] if members == 2 else others.at[2]
            copies.append((others.at[0], key_out.at[:, columns]))
            copies.append((others.at[1], value_out.at[:, columns]))
            copies.append((query, query_out.at[:, columns]))
    copy_all(copies, sem)


def gather(heads, pieces, so_far):
    kept = len(so_far)
    out = jax.ShapeDtypeStruct((BLOCK, HEADS * HEAD_DIM), jnp.bfloat16)
    return pl.pallas_call(
        functools.partial(gather_kernel, heads, len(pieces)),
        out_shape=[out] * 3,
        in_specs=[FAST] * len(pieces) + [ANYWHERE] * kept,
        out_specs=[ANYWHERE] * 3,
        scratch_shapes=[pltpu.SemaphoreType.DMA((3 * GROUP * len(heads),))],
        input_output_aliases={len(pieces) + at: at for at in range(kept)},
        compiler_params=pltpu.CompilerParams(vmem_limit_bytes=VMEM_LIMIT),
        cost_estimate=cost(1 + 2 * len(heads)),
        name="gather",
    )(*pieces, *so_far)


def shards(query_rows, key_rows, value_rows, out_grad, key_blocks, block_counts):
    chips = lax.axis_size("seq")
    chip = lax.axis_index("seq")
    core = lax.axis_index("head")
    place = jnp.stack([chip, core]).astype(jnp.int32)
    lists = key_blocks.reshape(-1)
    groups = [list(range(c, c + GROUP)) for c in range(0, chips, GROUP)]

    def regroup(member):
        return lax.all_to_all(
            member, "seq", split_axis=0, concat_axis=0, axis_index_groups=groups, tiled=True
        )

    def swap(member):
        return lax.ppermute(member, "head", [(0, 1), (1, 0)])

    def upward(member):
        return lax.ppermute(member, "seq", [(c, c + GROUP) for c in range(chips - GROUP)])

    def downward(member):
        return lax.ppermute(member, "seq", [(c + GROUP, c) for c in range(chips - GROUP)])

    def crosswise(member):
        pairs = [(2 * c + 1, 2 * (c + GROUP)) for c in range(chips - GROUP)]
        return lax.ppermute(member, ("seq", "head"), pairs + [(b, a) for a, b in pairs])

    def edges_of(low, high, cross):
        return [upward(high), downward(low), crosswise(cross)]

    def window_of(keys):
        below, above = upward(keys[GROUP - 1]), downward(keys[0])
        return [keys, swap(keys), below, above, swap(jnp.where(core == 1, below, above))]

    window = window_of(regroup(pack((key_rows, value_rows), FIRST + LAST)))
    rows = regroup(pack((query_rows, out_grad), FIRST))
    last_rows = regroup(pack((query_rows, out_grad), LAST, window[1:]))
    queries, near, far, *edges = grads(
        len(FIRST), 0, place, lists, block_counts, window, rows, []
    )
    queries = regroup(queries)
    edges, far = edges_of(*edges), swap(far)
    last_queries, last_near, last_far, *last_edges = grads(
        len(LAST), 2 * len(FIRST), place, lists, block_counts, window, last_rows, [near]
    )
    last_far = swap(last_far)
    others, *last_edges = settle(place, near, far, edges, [], [last_near, queries], last_edges)
    last_edges = edges_of(*last_edges)
    last_others = settle(place, last_near, last_far, last_edges, [last_queries], [])[0]
    results = gather(FIRST, (regroup(others), queries), ())
    key_grad, value_grad, query_grad = gather(LAST, (regroup(last_others),), results)
    return query_grad, key_grad, value_grad


def solution(mesh):
    rows = P(("seq", "head"), None)
    return jax.shard_map(
        shards,
        mesh=mesh,
        in_specs=(rows, rows, rows, rows, P(), P()),
        out_specs=(rows, rows, rows),
        check_vma=False,
    )
```

time: 549 us -> 208 us (0.38)
  Pallas kernels: 404 us -> 68.8 us
  blocking collectives: 0 us -> 41.8 us
  starting transfers between devices: 67.5 us -> 45.8 us
  local copies, waits for them, and re-layouts: 21.6 us -> 5.21 us
  other arithmetic: 8.64 us -> 2.65 us
    pallas_call x14 -> x9, Pallas kernels: 404 us -> 68.8 us  [the longest x2 42.5 us: grads(): pl.pallas_call(functools.partial(grads_kernel, heads, key_at, len(after))...]
    all_to_all x0 -> x1, blocking collectives: none -> 41.8 us  [regroup(): lax.all_to_all(member, 'seq', split_axis=0, concat_axis=0, axis_index_gro...]
    ppermute x33 -> x2, starting transfers between devices: 40.7 us -> 2.14 us  [crosswise(): lax.ppermute(member, ('seq', 'head'), pairs + [(b, a) for a, b in pairs])]
    ppermute x33 -> x2, waiting for transfers between devices: 35.5 us -> 0.01 us  [crosswise(): lax.ppermute(member, ('seq', 'head'), pairs + [(b, a) for a, b in pairs])]
    all_to_all x0 -> x5, waiting for transfers between devices: none -> 28.5 us  [regroup(): lax.all_to_all(member, 'seq', split_axis=0, concat_axis=0, axis_index_gro...]
    all_to_all x0 -> x5, starting transfers between devices: none -> 20.8 us  [regroup(): lax.all_to_all(member, 'seq', split_axis=0, concat_axis=0, axis_index_gro...]
    unnamed x153 -> x27, local copies, waits for them, and re-layouts: 21.5 us -> 3.12 us
    ppermute x5 -> x3, waiting for transfers between devices: 5.62 us -> 11.7 us  [downward(): lax.ppermute(member, 'seq', [(c + GROUP, c) for c in range(chips - GROUP)])]
  transfers between devices with their start and end apart: 56 -> 17, of which waited for: 13 -> 8; matrix products, arithmetic and copies ran while one was open for 1% -> 2% of each run, Pallas kernels for 59% -> 27%
where the time goes in v3:
time: 208 us; the launch traced here: 212 us
  Pallas kernels  68.8 us (33%)
  waiting for transfers between devices  46.2 us (22%)
  starting transfers between devices  45.8 us (22%)
  blocking collectives  41.8 us (20%)
  local copies, waits for them, and re-layouts  5.21 us (3%)
  other arithmetic  2.65 us (1%)
    pallas_call x2, Pallas kernels, grads(): pl.pallas_call(functools.partial(grads_kernel, heads, key_at, len(after))...  42.5 us
    all_to_all x1, blocking collectives, regroup(): lax.all_to_all(member, 'seq', split_axis=0, concat_axis=0, axis_index_gro...  41.8 us
    all_to_all x5, waiting for transfers between devices, regroup(): lax.all_to_all(member, 'seq', split_axis=0, concat_axis=0, axis_index_gro...  28.5 us
    all_to_all x5, starting transfers between devices, regroup(): lax.all_to_all(member, 'seq', split_axis=0, concat_axis=0, axis_index_gro...  20.8 us
    ppermute x3, starting transfers between devices, upward(): lax.ppermute(member, 'seq', [(c, c + GROUP) for c in range(chips - GROUP)])  18.4 us
    ppermute x3, waiting for transfers between devices, downward(): lax.ppermute(member, 'seq', [(c + GROUP, c) for c in range(chips - GROUP)])  11.7 us
    pallas_call x2, Pallas kernels, settle(): pl.pallas_call(functools.partial(settle_kernel, len(after), len(held)), g...  10.7 us
    pallas_call x3, Pallas kernels, pack(): pl.pallas_call(functools.partial(pack_kernel, heads, len(sources)), out_s...  9.35 us
  transfers between devices with their start and end apart: 17, of which 8 were waited for; matrix products, arithmetic and copies ran while one was open for 2% of the time, Pallas kernels for 27%

profile of v3, /device:TPU:0, one launch (start us, length us, event | category | flops | bytes accessed | tf_op | source)
XLA Modules:
  0.0 211.5 jit_solution(3358158075213292227)
XLA Ops:
  0.6 3.8 %pack.3 = bf16[4,6,512,128]{3,2,1,0:T(8,128)(2,1)} custom-call(bf16[512,1536]{1,0:T(8,128)(2,1)} %refs_0_.3, bf16[512,1536]{1,0:T(8,128)(2,1)} %refs_1_.3), custom_call_target="tpu_custom_call" | custom-call | flops 4600000000 | bytes 12000000 | tf_op jit(solution)/shard_map/pack/pallas_call | solution.py:76
  4.5 41.8 %all_to_all.30.refs_0_ = bf16[4,6,512,128]{3,2,1,0:T(8,128)(2,1)S(1)} all-to-all(bf16[4,6,512,128]{3,2,1,0:T(8,128)(2,1)} %pack.3), channel_id=1, replica_groups={{0,2,4,6},{8,10,12,14},{16,18,20,22},{24,26,28,30},{1,3,5,7},{9,11,13,1..., dimensions={0} | all-to-all | bytes 6291456 | tf_op jit(solution)/shard_map/all_to_all | solution.py:290
  46.3 1.4 slice_bitcast_fusion
  47.7 1.3 collective-permute-start.2
  49.0 5.4 %collective-permute-start.1 = (bf16[6,512,128]{2,1,0:T(8,128)(2,1)}, bf16[6,512,128]{2,1,0:T(8,128)(2,1)}, u32[]{:S(2)}, u32[]{:S(2)}) collective-permute-start(bf16[6,512,128]{2,1,0:T(8,128)(2,1)} %get-tuple-element.48), channel_id=1, source_target_pairs={{0,8},{2,10},{4,12},{6,14},{8,16},{10,18},{12,20},{14,22},{16,24},... | collective-permute-start | bytes 2359304 | tf_op jit(solution)/shard_map/ppermute | solution.py:298
  54.5 3.2 %pack.5 = bf16[4,4,512,128]{3,2,1,0:T(8,128)(2,1)} custom-call(bf16[512,1536]{1,0:T(8,128)(2,1)} %refs_0_.5, bf16[512,1536]{1,0:T(8,128)(2,1)} %refs_1_.5), custom_call_target="tpu_custom_call" | custom-call | flops 4600000000 | bytes 12000000 | tf_op jit(solution)/shard_map/pack/pallas_call | solution.py:76
  57.6 4.4 %all-to-all-start.2 = ((bf16[4,4,512,128]{3,2,1,0:T(8,128)(2,1)}), bf16[4,4,512,128]{3,2,1,0:T(8,128)(2,1)}, u32[]{:S(2)}, u32[]{:S(2)}) async-start(bf16[4,4,512,128]{3,2,1,0:T(8,128)(2,1)} %pack.5), calls=%async_computation.2 | async-start | bytes 4194304 | tf_op jit(solution)/shard_map/all_to_all | solution.py:290
  62.1 7.6 %collective-permute-done.2.refs_4_.refs_3_ = bf16[6,512,128]{2,1,0:T(8,128)(2,1)} collective-permute-done((bf16[6,512,128]{2,1,0:T(8,128)(2,1)}, bf16[6,512,128]{2,1,0:T(8,128)(2,1)}, u32[]{:S(2)}, u32[]{:S(2)}) %collective-permute-start.2) | collective-permute-done | bytes 786464 | tf_op jit(solution)/shard_map/ppermute | solution.py:301
  69.7 1.2 collective-permute-done.1.refs_3_.refs_2_
  70.9 2.1 broadcast_select_fusion
  74.3 1.3 collective-permute-done.3.refs_5_.refs_4_
  75.7 2.3 %pack.4 = bf16[4,2,512,128]{3,2,1,0:T(8,128)(2,1)} custom-call(bf16[512,1536]{1,0:T(8,128)(2,1)} %refs_0_.5, bf16[512,1536]{1,0:T(8,128)(2,1)} %refs_1_.5, bf16[4,6,512,128]{3,2,1,0:T(8,128)(2,1)} %collective-permute-done.refs_2_.refs_1_, bf16[6,512,128]{2,1,0:T(8,128)(2,1)} %collective-permute-done.1.refs_3_.refs_2_, ...), custom_call_target="tpu_custom_call" | custom-call | flops 4600000000 | bytes 12000000 | tf_op jit(solution)/shard_map/pack/pallas_call | solution.py:76
  78.0 9.3 %all-to-all-done.2.refs_5_ = bf16[4,4,512,128]{3,2,1,0:T(8,128)(2,1)} async-done(((bf16[4,4,512,128]{3,2,1,0:T(8,128)(2,1)}), bf16[4,4,512,128]{3,2,1,0:T(8,128)(2,1)}, u32[]{:S(2)}, u32[]{:S(2)}) %all-to-all-start.2) | async-done | bytes 2097184 | tf_op jit(solution)/shard_map/all_to_all | solution.py:290
  87.3 3.5 %all-to-all-start.1 = ((bf16[4,2,512,128]{3,2,1,0:T(8,128)(2,1)}), bf16[4,2,512,128]{3,2,1,0:T(8,128)(2,1)S(1)}, u32[]{:S(2)}, u32[]{:S(2)}) async-start(bf16[4,2,512,128]{3,2,1,0:T(8,128)(2,1)} %pack.4), calls=%async_computation.1 | async-start | bytes 2097152 | tf_op jit(solution)/shard_map/all_to_all | solution.py:290
  90.8 27.2 %grads.2 = (bf16[4,2,512,128]{3,2,1,0:T(8,128)(2,1)}, f32[4,2,2,512,128]{4,3,2,1,0:T(8,128)}, bf16[4,2,2,512,128]{4,3,2,1,0:T(8,128)(2,1)}, bf16[2,2,512,128]{3,...) custom-call(s32[2]{0:T(128)} %pad_add_fusion.place, s32[96]{0:T(128)} %reshape.9.lists, ...), custom_call_target="tpu_custom_call" | custom-call | flops 27599998976 | bytes 72000000 | tf_op jit(solution)/shard_map/grads/pallas_call | solution.py:183
  118.1 6.6 %collective-permute-start.6 = (bf16[2,2,512,128]{3,2,1,0:T(8,128)(2,1)}, bf16[2,2,512,128]{3,2,1,0:T(8,128)(2,1)S(1)}, u32[]{:S(2)}, u32[]{:S(2)}) collective-permute-start(bf16[2,2,512,128]{3,2,1,0:T(8,128)(2,1)} %get-tuple-element.29), channel_id=1, source_target_pairs={{0,8},{2,10},{4,12},{6,14},{8,16},{10,18},{12,20},{14,22},{16,24},... | collective-permute-start | bytes 1572872 | tf_op jit(solution)/shard_map/ppermute | solution.py:298
  124.7 1.3 collective-permute-start.7
  126.0 1.5 collective-permute-start.8
  127.4 4.2 %all-to-all-start.3 = ((bf16[4,2,512,128]{3,2,1,0:T(8,128)(2,1)}), bf16[4,2,512,128]{3,2,1,0:T(8,128)(2,1)S(1)}, u32[]{:S(2)}, u32[]{:S(2)}) async-start(bf16[4,2,512,128]{3,2,1,0:T(8,128)(2,1)} %get-tuple-element.35), calls=%async_computation.3 | async-start | bytes 2097152 | tf_op jit(solution)/shard_map/all_to_all | solution.py:290
  131.6 15.3 %grads.3 = (bf16[4,1,512,128]{3,2,1,0:T(8,128)(2,1)}, f32[4,1,2,512,128]{4,3,2,1,0:T(8,128)}, bf16[4,1,2,512,128]{4,3,2,1,0:T(8,128)(2,1)}, bf16[1,2,512,128]{3,...) custom-call(s32[2]{0:T(128)} %pad_add_fusion.place, s32[96]{0:T(128)} %reshape.9.lists, ...), custom_call_target="tpu_custom_call" | custom-call | flops 14949999616 | bytes 39000000 | tf_op jit(solution)/shard_map/grads/pallas_call | solution.py:183
  148.2 6.1 %settle.2 = (bf16[4,2,2,512,128]{4,3,2,1,0:T(8,128)(2,1)}, bf16[1,2,512,128]{3,2,1,0:T(8,128)(2,1)}, bf16[1,2,512,128]{3,2,1,0:T(8,128)(2,1)}, bf16[1,2,512,128]{3,2,1,0:T(8,128)(2,1)}) custom-call(s32[2]{0:T(128)} %pad_add_fusion.place, f32[4,2,2,512,128]{4,3,2,1,0:T(8,128)} %get-tuple-element.25.refs_6_.near, ...), custom_call_target="tpu_custom_call" | custom-call | flops 6899999744 | bytes 18000000 | tf_op jit(solution)/shard_map/settle/pallas_call | solution.py:232
  154.4 4.3 %all-to-all-start.5 = ((bf16[4,2,2,512,128]{4,3,2,1,0:T(8,128)(2,1)}), bf16[4,2,2,512,128]{4,3,2,1,0:T(8,128)(2,1)S(1)}, u32[]{:S(2)}, u32[]{:S(2)}) async-start(bf16[4,2,2,512,128]{4,3,2,1,0:T(8,128)(2,1)} %get-tuple-element.40), calls=%async_computation.5 | async-start | bytes 4194304 | tf_op jit(solution)/shard_map/all_to_all | solution.py:290
  159.3 6.3 %collective-permute-start.9 = (bf16[1,2,512,128]{3,2,1,0:T(8,128)(2,1)}, bf16[1,2,512,128]{3,2,1,0:T(8,128)(2,1)S(1)}, u32[]{:S(2)}, u32[]{:S(2)}) collective-permute-start(bf16[1,2,512,128]{3,2,1,0:T(8,128)(2,1)} %get-tuple-element.36), channel_id=1, source_target_pairs={{0,8},{2,10},{4,12},{6,14},{8,16},{10,18},{12,20},{14,22},{16,24},... | collective-permute-start | bytes 786440 | tf_op jit(solution)/shard_map/ppermute | solution.py:298
  165.6 1.3 collective-permute-start.10
  168.6 3.5 %collective-permute-done.9.below = bf16[1,2,512,128]{3,2,1,0:T(8,128)(2,1)S(1)} collective-permute-done((bf16[1,2,512,128]{3,2,1,0:T(8,128)(2,1)}, bf16[1,2,512,128]{3,2,1,0:T(8,128)(2,1)S(1)}, u32[]{:S(2)}, u32[]{:S(2)}) %collective-permute-start.9) | collective-permute-done | bytes 262176 | tf_op jit(solution)/shard_map/ppermute | solution.py:298
  172.1 4.0 %collective-permute-done.10.above = bf16[1,2,512,128]{3,2,1,0:T(8,128)(2,1)S(1)} collective-permute-done((bf16[1,2,512,128]{3,2,1,0:T(8,128)(2,1)}, bf16[1,2,512,128]{3,2,1,0:T(8,128)(2,1)S(1)}, u32[]{:S(2)}, u32[]{:S(2)}) %collective-permute-start.10) | collective-permute-done | bytes 262176 | tf_op jit(solution)/shard_map/ppermute | solution.py:301
  176.9 4.5 %settle.3 = bf16[4,1,3,512,128]{4,3,2,1,0:T(8,128)(2,1)} custom-call(s32[2]{0:T(128)} %pad_add_fusion.place, f32[4,1,2,512,128]{4,3,2,1,0:T(8,128)} %get-tuple-element.26.refs_3_.near, bf16[4,1,2,512,128]{4,3,2,1,0:T(8,128)(2,1)} %copy-done.6, bf16[1,2,512,128]{3,2,1,0:T(8,128)(2,1)} %copy-done.10, bf16[1,2,512,128]{3,2,1,0:T(8,128)(2,1)} %copy-done.11, ...), custom_call_target="tpu_custom_call" | custom-call | flops 4600000000 | bytes 12000000 | tf_op jit(solution)/shard_map/settle/pallas_call | solution.py:232
  181.4 3.1 %all-to-all-done.5.refs_0_ = bf16[4,2,2,512,128]{4,3,2,1,0:T(8,128)(2,1)S(1)} async-done(((bf16[4,2,2,512,128]{4,3,2,1,0:T(8,128)(2,1)}), bf16[4,2,2,512,128]{4,3,2,1,0:T(8,128)(2,1)S(1)}, u32[]{:S(2)}, u32[]{:S(2)}) %all-to-all-start.5) | async-done | bytes 2097184 | tf_op jit(solution)/shard_map/all_to_all | solution.py:290
  184.6 4.3 %all-to-all-start.4 = ((bf16[4,1,3,512,128]{4,3,2,1,0:T(8,128)(2,1)}), bf16[4,1,3,512,128]{4,3,2,1,0:T(8,128)(2,1)}, u32[]{:S(2)}, u32[]{:S(2)}) async-start(bf16[4,1,3,512,128]{4,3,2,1,0:T(8,128)(2,1)} %settle.3), calls=%async_computation.4 | async-start | bytes 3145728 | tf_op jit(solution)/shard_map/all_to_all | solution.py:290
  188.9 3.7 %gather.2 = (bf16[512,1536]{1,0:T(8,128)(2,1)}, bf16[512,1536]{1,0:T(8,128)(2,1)}, bf16[512,1536]{1,0:T(8,128)(2,1)}) custom-call(bf16[4,2,2,512,128]{4,3,2,1,0:T(8,128)(2,1)} %copy-done.1, bf16[4,2,512,128]{3,2,1,0:T(8,128)(2,1)} %copy-done.2), custom_call_target="tpu_custom_call" | custom-call | flops 5750000128 | bytes 15000000 | tf_op jit(solution)/shard_map/gather/pallas_call | solution.py:268
  192.6 16.1 %all-to-all-done.4.refs_0_ = bf16[4,1,3,512,128]{4,3,2,1,0:T(8,128)(2,1)} async-done(((bf16[4,1,3,512,128]{4,3,2,1,0:T(8,128)(2,1)}), bf16[4,1,3,512,128]{4,3,2,1,0:T(8,128)(2,1)}, u32[]{:S(2)}, u32[]{:S(2)}) %all-to-all-start.4) | async-done | bytes 1572896 | tf_op jit(solution)/shard_map/all_to_all | solution.py:290
  208.7 2.6 %gather.3 = (bf16[512,1536]{1,0:T(8,128)(2,1)}, bf16[512,1536]{1,0:T(8,128)(2,1)}, bf16[512,1536]{1,0:T(8,128)(2,1)}) custom-call(bf16[4,1,3,512,128]{4,3,2,1,0:T(8,128)(2,1)} %all-to-all-done.4.refs_0_, bf16[512,1536]{1,0:T(8,128)(2,1)} %get-tuple-element.41.refs_1_, ...), custom_call_target="tpu_custom_call", output_to_operand_aliasing={{0}: (1, {}), {1}: (2, {}), {2}: (3, {})} | custom-call | flops 3449999872 | bytes 9000000 | tf_op jit(solution)/shard_map/gather/pallas_call | solution.py:268
  (43 shorter events, 5.7 us)
Async XLA Ops:
  46.3 11.3 %copy-start = (bf16[4,6,512,128]{3,2,1,0:T(8,128)(2,1)}, bf16[4,6,512,128]{3,2,1,0:T(8,128)(2,1)S(1)}, u32[]{:S(2)}) copy-start(bf16[4,6,512,128]{3,2,1,0:T(8,128)(2,1)S(1)} %all_to_all.30.refs_0_) | copy-start | bytes 9437188
  46.3 29.3 %collective-permute-start = (bf16[4,6,512,128]{3,2,1,0:T(8,128)(2,1)S(1)}, bf16[4,6,512,128]{3,2,1,0:T(8,128)(2,1)}, u32[]{:S(2)}, u32[]{:S(2)}) collective-permute-start(bf16[4,6,512,128]{3,2,1,0:T(8,128)(2,1)S(1)} %all_to_all.30.refs_0_), channel_id=1, source_target_pairs={{0,1},{1,0},{2,3},{3,2},{4,5},{5,4},{6,7},{7,6},{8,9},{9,8},{10,11... | collective-permute-start | bytes 9437192 | tf_op jit(solution)/shard_map/ppermute | solution.py:295
  47.7 22.0 %collective-permute-start.2 = (bf16[6,512,128]{2,1,0:T(8,128)(2,1)}, bf16[6,512,128]{2,1,0:T(8,128)(2,1)}, u32[]{:S(2)}, u32[]{:S(2)}) collective-permute-start(bf16[6,512,128]{2,1,0:T(8,128)(2,1)} %get-tuple-element.47), channel_id=1, source_target_pairs={{8,0},{10,2},{12,4},{14,6},{16,8},{18,10},{20,12},{22,14},{24,16},... | collective-permute-start | bytes 2359304 | tf_op jit(solution)/shard_map/ppermute | solution.py:301
  49.0 21.9 %collective-permute-start.1 = (bf16[6,512,128]{2,1,0:T(8,128)(2,1)}, bf16[6,512,128]{2,1,0:T(8,128)(2,1)}, u32[]{:S(2)}, u32[]{:S(2)}) collective-permute-start(bf16[6,512,128]{2,1,0:T(8,128)(2,1)} %get-tuple-element.48), channel_id=1, source_target_pairs={{0,8},{2,10},{4,12},{6,14},{8,16},{10,18},{12,20},{14,22},{16,24},... | collective-permute-start | bytes 2359304 | tf_op jit(solution)/shard_map/ppermute | solution.py:298
  57.6 29.6 %all-to-all-start.2 = ((bf16[4,4,512,128]{3,2,1,0:T(8,128)(2,1)}), bf16[4,4,512,128]{3,2,1,0:T(8,128)(2,1)}, u32[]{:S(2)}, u32[]{:S(2)}) async-start(bf16[4,4,512,128]{3,2,1,0:T(8,128)(2,1)} %pack.5), calls=%async_computation.2 | async-start | bytes 4194304 | tf_op jit(solution)/shard_map/all_to_all | solution.py:290
  62.1 10.9 %copy-start.4 = (s32[32,3]{0,1:T(4,128)S(1)}, s32[32,3]{0,1:T(4,128)}, u32[]{:S(2)}) copy-start(s32[32,3]{0,1:T(4,128)} %param.10) | copy-start | bytes 1156
  73.0 2.6 %collective-permute-start.3 = (bf16[6,512,128]{2,1,0:T(8,128)(2,1)}, bf16[6,512,128]{2,1,0:T(8,128)(2,1)}, u32[]{:S(2)}, u32[]{:S(2)}) collective-permute-start(bf16[6,512,128]{2,1,0:T(8,128)(2,1)} %broadcast_select_fusion), channel_id=1, source_target_pairs={{0,1},{1,0},{2,3},{3,2},{4,5},{5,4},{6,7},{7,6},{8,9},{9,8},{10,11... | collective-permute-start | bytes 2359304 | tf_op jit(solution)/shard_map/ppermute | solution.py:295
  87.3 40.2 %all-to-all-start.1 = ((bf16[4,2,512,128]{3,2,1,0:T(8,128)(2,1)}), bf16[4,2,512,128]{3,2,1,0:T(8,128)(2,1)S(1)}, u32[]{:S(2)}, u32[]{:S(2)}) async-start(bf16[4,2,512,128]{3,2,1,0:T(8,128)(2,1)} %pack.4), calls=%async_computation.1 | async-start | bytes 2097152 | tf_op jit(solution)/shard_map/all_to_all | solution.py:290
  118.0 29.0 %collective-permute-start.5 = (bf16[4,2,2,512,128]{4,3,2,1,0:T(8,128)(2,1)}, bf16[4,2,2,512,128]{4,3,2,1,0:T(8,128)(2,1)}, u32[]{:S(2)}, u32[]{:S(2)}) collective-permute-start(bf16[4,2,2,512,128]{4,3,2,1,0:T(8,128)(2,1)} %get-tuple-element.28), channel_id=1, source_target_pairs={{0,1},{1,0},{2,3},{3,2},{4,5},{5,4},{6,7},{7,6},{8,9},{9,8},{10,11... | collective-permute-start | bytes 6291464 | tf_op jit(solution)/shard_map/ppermute | solution.py:295
  118.1 28.8 %collective-permute-start.6 = (bf16[2,2,512,128]{3,2,1,0:T(8,128)(2,1)}, bf16[2,2,512,128]{3,2,1,0:T(8,128)(2,1)S(1)}, u32[]{:S(2)}, u32[]{:S(2)}) collective-permute-start(bf16[2,2,512,128]{3,2,1,0:T(8,128)(2,1)} %get-tuple-element.29), channel_id=1, source_target_pairs={{0,8},{2,10},{4,12},{6,14},{8,16},{10,18},{12,20},{14,22},{16,24},... | collective-permute-start | bytes 1572872 | tf_op jit(solution)/shard_map/ppermute | solution.py:298
  124.7 22.2 %collective-permute-start.7 = (bf16[2,2,512,128]{3,2,1,0:T(8,128)(2,1)}, bf16[2,2,512,128]{3,2,1,0:T(8,128)(2,1)S(1)}, u32[]{:S(2)}, u32[]{:S(2)}) collective-permute-start(bf16[2,2,512,128]{3,2,1,0:T(8,128)(2,1)} %get-tuple-element.30), channel_id=1, source_target_pairs={{8,0},{10,2},{12,4},{14,6},{16,8},{18,10},{20,12},{22,14},{24,16},... | collective-permute-start | bytes 1572872 | tf_op jit(solution)/shard_map/ppermute | solution.py:301
  126.0 21.0 %collective-permute-start.8 = (bf16[2,2,512,128]{3,2,1,0:T(8,128)(2,1)}, bf16[2,2,512,128]{3,2,1,0:T(8,128)(2,1)}, u32[]{:S(2)}, u32[]{:S(2)}) collective-permute-start(bf16[2,2,512,128]{3,2,1,0:T(8,128)(2,1)} %get-tuple-element.31), channel_id=1, source_target_pairs={{1,8},{3,10},{5,12},{7,14},{9,16},{11,18},{13,20},{15,22},{17,24},... | collective-permute-start | bytes 1572872 | tf_op jit(solution)/shard_map/ppermute | solution.py:305
  127.4 4.2 %copy-start.3 = (bf16[4,2,512,128]{3,2,1,0:T(8,128)(2,1)}, bf16[4,2,512,128]{3,2,1,0:T(8,128)(2,1)S(1)}, u32[]{:S(2)}) copy-start(bf16[4,2,512,128]{3,2,1,0:T(8,128)(2,1)S(1)} %all-to-all-done.1.refs_5_) | copy-start | bytes 3145732
  127.4 19.5 %all-to-all-start.3 = ((bf16[4,2,512,128]{3,2,1,0:T(8,128)(2,1)}), bf16[4,2,512,128]{3,2,1,0:T(8,128)(2,1)S(1)}, u32[]{:S(2)}, u32[]{:S(2)}) async-start(bf16[4,2,512,128]{3,2,1,0:T(8,128)(2,1)} %get-tuple-element.35), calls=%async_computation.3 | async-start | bytes 2097152 | tf_op jit(solution)/shard_map/all_to_all | solution.py:290
  146.9 0.8 copy-start.7
  146.9 0.9 copy-start.8
  147.0 1.3 copy-start.2
  154.4 4.4 %copy-start.5 = (bf16[4,1,2,512,128]{4,3,2,1,0:T(8,128)(2,1)S(1)}, bf16[4,1,2,512,128]{4,3,2,1,0:T(8,128)(2,1)}, u32[]{:S(2)}) copy-start(bf16[4,1,2,512,128]{4,3,2,1,0:T(8,128)(2,1)} %get-tuple-element.27) | copy-start | bytes 3145732
  154.4 12.5 %copy-start.9 = (bf16[1,2,512,128]{3,2,1,0:T(8,128)(2,1)S(1)}, bf16[1,2,512,128]{3,2,1,0:T(8,128)(2,1)}, u32[]{:S(2)}) copy-start(bf16[1,2,512,128]{3,2,1,0:T(8,128)(2,1)} %get-tuple-element.38) | copy-start | bytes 786436
  154.4 30.2 %all-to-all-start.5 = ((bf16[4,2,2,512,128]{4,3,2,1,0:T(8,128)(2,1)}), bf16[4,2,2,512,128]{4,3,2,1,0:T(8,128)(2,1)S(1)}, u32[]{:S(2)}, u32[]{:S(2)}) async-start(bf16[4,2,2,512,128]{4,3,2,1,0:T(8,128)(2,1)} %get-tuple-element.40), calls=%async_computation.5 | async-start | bytes 4194304 | tf_op jit(solution)/shard_map/all_to_all | solution.py:290
  158.7 8.9 %collective-permute-start.4 = (bf16[4,1,2,512,128]{4,3,2,1,0:T(8,128)(2,1)S(1)}, bf16[4,1,2,512,128]{4,3,2,1,0:T(8,128)(2,1)S(1)}, u32[]{:S(2)}, u32[]{:S(2)}) collective-permute-start(bf16[4,1,2,512,128]{4,3,2,1,0:T(8,128)(2,1)S(1)} %copy-done.5), channel_id=1, source_target_pairs={{0,1},{1,0},{2,3},{3,2},{4,5},{5,4},{6,7},{7,6},{8,9},{9,8},{10,11... | collective-permute-start | bytes 3145736 | tf_op jit(solution)/shard_map/ppermute | solution.py:295
  159.3 12.8 %collective-permute-start.9 = (bf16[1,2,512,128]{3,2,1,0:T(8,128)(2,1)}, bf16[1,2,512,128]{3,2,1,0:T(8,128)(2,1)S(1)}, u32[]{:S(2)}, u32[]{:S(2)}) collective-permute-start(bf16[1,2,512,128]{3,2,1,0:T(8,128)(2,1)} %get-tuple-element.36), channel_id=1, source_target_pairs={{0,8},{2,10},{4,12},{6,14},{8,16},{10,18},{12,20},{14,22},{16,24},... | collective-permute-start | bytes 786440 | tf_op jit(solution)/shard_map/ppermute | solution.py:298
  165.6 10.5 %collective-permute-start.10 = (bf16[1,2,512,128]{3,2,1,0:T(8,128)(2,1)}, bf16[1,2,512,128]{3,2,1,0:T(8,128)(2,1)S(1)}, u32[]{:S(2)}, u32[]{:S(2)}) collective-permute-start(bf16[1,2,512,128]{3,2,1,0:T(8,128)(2,1)} %get-tuple-element.37), channel_id=1, source_target_pairs={{8,0},{10,2},{12,4},{14,6},{16,8},{18,10},{20,12},{22,14},{24,16},... | collective-permute-start | bytes 786440 | tf_op jit(solution)/shard_map/ppermute | solution.py:301
  166.9 9.2 %collective-permute-start.11 = (bf16[1,2,512,128]{3,2,1,0:T(8,128)(2,1)S(1)}, bf16[1,2,512,128]{3,2,1,0:T(8,128)(2,1)S(1)}, u32[]{:S(2)}, u32[]{:S(2)}) collective-permute-start(bf16[1,2,512,128]{3,2,1,0:T(8,128)(2,1)S(1)} %copy-done.9), channel_id=1, source_target_pairs={{1,8},{3,10},{5,12},{7,14},{9,16},{11,18},{13,20},{15,22},{17,24},... | collective-permute-start | bytes 786440 | tf_op jit(solution)/shard_map/ppermute | solution.py:305
  167.6 1.0 copy-start.6
  172.1 4.8 %copy-start.10 = (bf16[1,2,512,128]{3,2,1,0:T(8,128)(2,1)}, bf16[1,2,512,128]{3,2,1,0:T(8,128)(2,1)S(1)}, u32[]{:S(2)}) copy-start(bf16[1,2,512,128]{3,2,1,0:T(8,128)(2,1)S(1)} %collective-permute-done.9.below) | copy-start | bytes 786436
  176.1 0.8 copy-start.11
  176.2 0.7 copy-start.12
  184.6 4.4 %copy-start.1 = (bf16[4,2,2,512,128]{4,3,2,1,0:T(8,128)(2,1)}, bf16[4,2,2,512,128]{4,3,2,1,0:T(8,128)(2,1)S(1)}, u32[]{:S(2)}) copy-start(bf16[4,2,2,512,128]{4,3,2,1,0:T(8,128)(2,1)S(1)} %all-to-all-done.5.refs_0_) | copy-start | bytes 6291460
  184.6 24.2 %all-to-all-start.4 = ((bf16[4,1,3,512,128]{4,3,2,1,0:T(8,128)(2,1)}), bf16[4,1,3,512,128]{4,3,2,1,0:T(8,128)(2,1)}, u32[]{:S(2)}, u32[]{:S(2)}) async-start(bf16[4,1,3,512,128]{4,3,2,1,0:T(8,128)(2,1)} %settle.3), calls=%async_computation.4 | async-start | bytes 3145728 | tf_op jit(solution)/shard_map/all_to_all | solution.py:290

commit v4 on v3

v4 whole, which is shorter than its diff:
```python
import functools
import math

import jax
import jax.numpy as jnp
from jax import lax
from jax.experimental import pallas as pl
from jax.experimental.pallas import tpu as pltpu
from jax.sharding import PartitionSpec as P

HEADS = 12
HEAD_DIM = 128
BLOCK = 512
MAXK = 3
GROUP = 4
SHARE = HEADS // GROUP
OWN = GROUP + 2
SEEN = OWN + GROUP + 1
CORES = 2
MEMBERS = GROUP * CORES
SCALE = HEAD_DIM ** -0.5
LOG_SCALE = SCALE * math.log2(math.e)
COST_FLOPS, COST_BYTES = 3.45e+09, 9.00e+06
VMEM_LIMIT = 60 * 1024 * 1024

ANYWHERE = pl.BlockSpec(memory_space=pl.ANY)
SCALARS = pl.BlockSpec(memory_space=pltpu.SMEM)
FAST = pl.BlockSpec(memory_space=pltpu.VMEM)


def pair_rows(left, right):
    return lax.dot_general(
        left, right, (((1,), (1,)), ((), ())), preferred_element_type=jnp.float32
    )


def product(left, right):
    return jnp.dot(left, right, preferred_element_type=jnp.float32)


def copy_all(copies, sem):
    started = [
        pltpu.make_async_copy(source, target, sem.at[at])
        for at, (source, target) in enumerate(copies)
    ]
    for copy in started:
        copy.start()
    for copy in started:
        copy.wait()


def head_columns(head):
    return pl.ds(head * HEAD_DIM, HEAD_DIM)


def cost(microseconds):
    return pl.CostEstimate(
        flops=int(microseconds * COST_FLOPS),
        bytes_accessed=int(microseconds * COST_BYTES),
        transcendentals=0,
    )


def pack_split_kernel(place, key_rows, value_rows, query_rows, out_grad, *refs):
    outs, sem = refs[:-1], refs[-1]
    here = place[0] & (GROUP - 1)
    copies = []
    for away, out in enumerate(outs):
        start = (SHARE * (here ^ away) + CORES) * HEAD_DIM
        columns = pl.ds(pl.multiple_of(start, HEAD_DIM), HEAD_DIM)
        for index, source in enumerate((key_rows, value_rows, query_rows, out_grad)):
            copies.append((source.at[:, columns], out.at[index]))
    copy_all(copies, sem)


def pack_split(place, sources):
    out = jax.ShapeDtypeStruct((len(sources), BLOCK, HEAD_DIM), jnp.bfloat16)
    return pl.pallas_call(
        pack_split_kernel,
        out_shape=[out] * GROUP,
        in_specs=[SCALARS] + [ANYWHERE] * len(sources),
        out_specs=[FAST] * GROUP,
        scratch_shapes=[pltpu.SemaphoreType.DMA((GROUP * len(sources),))],
        compiler_params=pltpu.CompilerParams(vmem_limit_bytes=VMEM_LIMIT),
        cost_estimate=cost(4),
        name="pack_split",
    )(place, *sources)


def pack_kernel(heads, *refs):
    sources, outs, sem = refs[:4], refs[4:6], refs[6]
    copies = []
    for at, head in enumerate(heads):
        for index, source in enumerate(sources):
            target = outs[index // 2].at[at, index % 2]
            copies.append((source.at[:, pl.ds(head * HEAD_DIM, HEAD_DIM)], target))
    copy_all(copies, sem)


def pack(sources, heads):
    out = jax.ShapeDtypeStruct((len(heads), 2, BLOCK, HEAD_DIM), jnp.bfloat16)
    return pl.pallas_call(
        functools.partial(pack_kernel, heads),
        out_shape=[out] * 2,
        in_specs=[ANYWHERE] * 4,
        out_specs=[FAST] * 2,
        scratch_shapes=[pltpu.SemaphoreType.DMA((4 * len(heads),))],
        compiler_params=pltpu.CompilerParams(vmem_limit_bytes=VMEM_LIMIT),
        cost_estimate=cost(6),
        name="pack",
    )(*sources)


def arrange_kernel(waited, place, *refs):
    members = refs[:GROUP]
    ordered, low, high, cross, sem = refs[GROUP + waited :]
    here, core = place[0] & (GROUP - 1), place[1]
    pair = pl.ds(0, 2)
    copies = []
    for away, member in enumerate(members):
        copies.append(pltpu.make_async_copy(member.at[pair], ordered.at[here ^ away], sem.at[away]))
    for copy in copies:
        copy.start()
    for copy in copies:
        copy.wait()
    low[0] = ordered[0]
    high[0] = ordered[GROUP - 1]
    cross[0] = ordered[core * (GROUP - 1)]


def arrange(place, members, after=()):
    block = (2, BLOCK, HEAD_DIM)
    edge = jax.ShapeDtypeStruct((1,) + block, jnp.bfloat16)
    return pl.pallas_call(
        functools.partial(arrange_kernel, len(after)),
        out_shape=[jax.ShapeDtypeStruct((GROUP,) + block, jnp.bfloat16), edge, edge, edge],
        in_specs=[SCALARS] + [ANYWHERE] * (GROUP + len(after)),
        out_specs=[FAST] * 4,
        scratch_shapes=[pltpu.SemaphoreType.DMA((GROUP,))],
        compiler_params=pltpu.CompilerParams(vmem_limit_bytes=VMEM_LIMIT),
        cost_estimate=cost(2.5),
        name="arrange",
    )(place, *members, *after)


def cut_kernel(pieces, place, member, *refs):
    outs, sem = refs[-1 - len(pieces) : -1], refs[-1]
    copies = []
    for piece, out in zip(pieces, outs):
        start, rows, parts = piece(place[1])
        copies.append((member.at[pl.ds(start, rows), pl.ds(0, parts)], out))
    copy_all(copies, sem)


def cut(place, member, pieces, after=()):
    shapes = [piece(0)[1:] + member.shape[2:] for piece in pieces]
    return pl.pallas_call(
        functools.partial(cut_kernel, pieces),
        out_shape=[jax.ShapeDtypeStruct(shape, member.dtype) for shape in shapes],
        in_specs=[SCALARS] + [ANYWHERE] * (1 + len(after)),
        out_specs=[FAST] * len(pieces),
        scratch_shapes=[pltpu.SemaphoreType.DMA((len(pieces),))],
        compiler_params=pltpu.CompilerParams(vmem_limit_bytes=VMEM_LIMIT),
        cost_estimate=cost(1.5),
        name="cut",
    )(place, member, *after)


def grads_core(first, place_of, spots, block_of, keys, rows, sums, queries, lists, counts):
    def query_step(spot, carry):
        block = block_of(spot)
        count = counts[block]

        def live(slots):
            query_block, grad_block = rows[spot, 0], rows[spot, 1]
            places = [place_of(lists[block * MAXK + slot] - first) for slot in range(slots)]
            scores = [pair_rows(keys[at, 0], query_block) for at in places]
            peak = functools.reduce(
                jnp.maximum, [jnp.max(member, axis=0, keepdims=True) for member in scores]
            )
            grown = [jnp.exp2(member * LOG_SCALE - peak * LOG_SCALE) for member in scores]
            weight_grads = [pair_rows(keys[at, 1], grad_block) for at in places]
            total = sum(jnp.sum(member, axis=0, keepdims=True) for member in grown)
            share = 1.0 / total
            delta = share * sum(
                jnp.sum(member * other, axis=0, keepdims=True)
                for member, other in zip(grown, weight_grads)
            )
            query_sum = None
            for at, member, other in zip(places, grown, weight_grads):
                weights = member * share
                score_low = (weights * (other - delta)).astype(jnp.bfloat16)
                sums[at, 1] += product(weights.astype(jnp.bfloat16), grad_block)
                sums[at, 0] += product(score_low, query_block) * SCALE
                term = product(keys[at, 0].T, score_low)
                query_sum = term if query_sum is None else query_sum + term
            queries[spot] = (query_sum * SCALE).T.astype(jnp.bfloat16)

        for slots in range(1, MAXK + 1):
            pl.when(count == slots)(functools.partial(live, slots))
        return carry

    lax.fori_loop(0, spots, query_step, 0)


def begin(copies, sem):
    started = [
        pltpu.make_async_copy(source, target, sem.at[at])
        for at, (source, target) in enumerate(copies)
    ]
    for copy in started:
        copy.start()
    return started


def split_grads_kernel(waited, place, lists, counts, *refs):
    member, swapped, below, above, cross = refs[:5]
    rows_in = refs[5 : 5 + GROUP]
    refs = refs[5 + GROUP + waited :]
    query_out, near_out, far_out, low_out, high_out, cross_out = refs[:6]
    keys, rows, sums, queries, rounded, sem = refs[6:]
    chip, core = place[0], place[1]
    first = 2 * (chip & ~(GROUP - 1)) - 2
    here = chip & (GROUP - 1)
    copies = begin(
        [(part.at[pl.ds(2, 2)], rows.at[here ^ away]) for away, part in enumerate(rows_in)]
        + [
            (member, keys.at[pl.ds(1, GROUP)]),
            (swapped, keys.at[pl.ds(OWN, GROUP)]),
            (below.at[0], keys.at[0]),
            (above.at[0], keys.at[OWN - 1]),
            (cross.at[0], keys.at[SEEN - 1]),
        ],
        sem,
    )
    sums[...] = jnp.zeros_like(sums)
    for copy in copies:
        copy.wait()

    def place_of(offset):
        half = offset >> 1
        other = jnp.where((half >= 1) & (half <= GROUP), OWN - 1 + half, SEEN - 1)
        return jnp.where((offset & 1) == core, half, other)

    def block_of(spot):
        return first + 2 + 2 * spot + core

    grads_core(first, place_of, GROUP, block_of, keys, rows, sums, queries, lists, counts)
    copies = begin([(queries, query_out), (sums.at[pl.ds(1, GROUP)], near_out)], sem)
    for index, spot in enumerate((*range(OWN, OWN + GROUP), 0, OWN - 1, SEEN - 1)):
        rounded[index] = sums[spot].astype(jnp.bfloat16)
    more = begin(
        [
            (rounded.at[pl.ds(0, GROUP)], far_out),
            (rounded.at[pl.ds(GROUP, 1)], low_out),
            (rounded.at[pl.ds(GROUP + 1, 1)], high_out),
            (rounded.at[pl.ds(GROUP + 2, 1)], cross_out),
        ],
        sem.at[pl.ds(2, 4)],
    )
    for copy in copies + more:
        copy.wait()


def split_grads(place, lists, counts, member, swapped, edges, rows, after=()):
    block = (BLOCK, HEAD_DIM)
    edge = jax.ShapeDtypeStruct((1, 2) + block, jnp.bfloat16)
    outs = [
        jax.ShapeDtypeStruct((GROUP,) + block, jnp.bfloat16),
        jax.ShapeDtypeStruct((GROUP, 2) + block, jnp.float32),
        jax.ShapeDtypeStruct((GROUP, 2) + block, jnp.bfloat16),
        edge,
        edge,
        edge,
    ]
    return pl.pallas_call(
        functools.partial(split_grads_kernel, len(after)),
        out_shape=outs,
        in_specs=[SCALARS] * 3 + [ANYWHERE] * (5 + GROUP + len(after)),
        out_specs=[ANYWHERE] * len(outs),
        scratch_shapes=[
            pltpu.VMEM((SEEN, 2) + block, jnp.bfloat16),
            pltpu.VMEM((GROUP, 2) + block, jnp.bfloat16),
            pltpu.VMEM((SEEN, 2) + block, jnp.float32),
            pltpu.VMEM((GROUP,) + block, jnp.bfloat16),
            pltpu.VMEM((GROUP + 3, 2) + block, jnp.bfloat16),
            pltpu.SemaphoreType.DMA((GROUP + 5,)),
        ],
        compiler_params=pltpu.CompilerParams(vmem_limit_bytes=VMEM_LIMIT),
        cost_estimate=cost(13),
        name="split_grads",
    )(place, lists, counts, member, swapped, *edges, *rows, *after)


def whole_grads_kernel(waited, place, lists, counts, *refs):
    member, below, above, rows_in = refs[:4]
    refs = refs[4 + waited :]
    query_out, sum_out, edge_out, low_out, high_out = refs[:5]
    keys, rows, sums, queries, rounded, sem = refs[5:]
    first = 2 * (place[0] & ~(GROUP - 1)) - 2
    copies = begin(
        [
            (member, keys.at[pl.ds(2, MEMBERS)]),
            (below, keys.at[pl.ds(0, 2)]),
            (above, keys.at[pl.ds(MEMBERS + 2, 2)]),
            (rows_in, rows),
        ],
        sem,
    )
    sums[...] = jnp.zeros_like(sums)
    for copy in copies:
        copy.wait()
    grads_core(
        first, lambda offset: offset, MEMBERS, lambda spot: first + 2 + spot,
        keys, rows, sums, queries, lists, counts,
    )
    copies = begin(
        [
            (queries, query_out),
            (sums.at[pl.ds(2, 2)], edge_out.at[pl.ds(0, 2)]),
            (sums.at[pl.ds(MEMBERS, 2)], edge_out.at[pl.ds(2, 2)]),
        ],
        sem,
    )
    rounded[...] = sums[...].astype(jnp.bfloat16)
    more = begin(
        [
            (rounded.at[pl.ds(2, MEMBERS)], sum_out),
            (rounded.at[pl.ds(0, 2)], low_out),
            (rounded.at[pl.ds(MEMBERS + 2, 2)], high_out),
        ],
        sem.at[pl.ds(3, 3)],
    )
    for copy in copies + more:
        copy.wait()


def whole_grads(place, lists, counts, member, edges, rows, after=()):
    block = (BLOCK, HEAD_DIM)
    edge = jax.ShapeDtypeStruct((2, 2) + block, jnp.bfloat16)
    outs = [
        jax.ShapeDtypeStruct((MEMBERS,) + block, jnp.bfloat16),
        jax.ShapeDtypeStruct((MEMBERS, 2) + block, jnp.bfloat16),
        jax.ShapeDtypeStruct((4, 2) + block, jnp.float32),
        edge,
        edge,
    ]
    return pl.pallas_call(
        functools.partial(whole_grads_kernel, len(after)),
        out_shape=outs,
        in_specs=[SCALARS] * 3 + [ANYWHERE] * (4 + len(after)),
        out_specs=[ANYWHERE] * len(outs),
        scratch_shapes=[
            pltpu.VMEM((MEMBERS + 4, 2) + block, jnp.bfloat16),
            pltpu.VMEM((MEMBERS, 2) + block, jnp.bfloat16),
            pltpu.VMEM((MEMBERS + 4, 2) + block, jnp.float32),
            pltpu.VMEM((MEMBERS,) + block, jnp.bfloat16),
            pltpu.VMEM((MEMBERS + 4, 2) + block, jnp.bfloat16),
            pltpu.SemaphoreType.DMA((6,)),
        ],
        compiler_params=pltpu.CompilerParams(vmem_limit_bytes=VMEM_LIMIT),
        cost_estimate=cost(22),
        name="whole_grads",
    )(place, lists, counts, member, *edges, rows, *after)


def split_settle_kernel(waited, place, near, far, below, above, cross, queries, *refs):
    outs = refs[waited:]
    here, core = place[0] & (GROUP - 1), place[1]
    for away, out in enumerate(outs):
        spot = here ^ away
        out[:2] = (near[spot] + far[spot].astype(jnp.float32)).astype(jnp.bfloat16)
        out[2] = queries[spot]

        def more(out, spot, *edges):
            total = near[spot] + far[spot].astype(jnp.float32)
            for edge in edges:
                total += edge[0].astype(jnp.float32)
            out[:2] = total.astype(jnp.bfloat16)

        low, high = spot == 0, spot == GROUP - 1
        pl.when(low & (core == 0))(functools.partial(more, out, spot, below, cross))
        pl.when(low & (core == 1))(functools.partial(more, out, spot, below))
        pl.when(high & (core == 0))(functools.partial(more, out, spot, above))
        pl.when(high & (core == 1))(functools.partial(more, out, spot, above, cross))


def split_settle(place, near, far, edges, queries, after=()):
    out = jax.ShapeDtypeStruct((3, BLOCK, HEAD_DIM), jnp.bfloat16)
    return pl.pallas_call(
        functools.partial(split_settle_kernel, len(after)),
        out_shape=[out] * GROUP,
        in_specs=[SCALARS] + [FAST] * 6 + [ANYWHERE] * len(after),
        out_specs=[FAST] * GROUP,
        compiler_params=pltpu.CompilerParams(vmem_limit_bytes=VMEM_LIMIT),
        cost_estimate=cost(4),
        name="split_settle",
    )(place, near, far, *edges, queries, *after)


def whole_settle_kernel(near, below, above, summed, *refs):
    out = refs[-1]
    at = pl.program_id(0)

    @pl.when(at < 2)
    def _():
        out[...] = (near[...] + below[...].astype(jnp.float32)).astype(jnp.bfloat16)

    @pl.when(at >= 2)
    def _():
        out[...] = (near[...] + above[...].astype(jnp.float32)).astype(jnp.bfloat16)


def whole_settle(near, below, above, summed, after=()):
    one = (1, 2, BLOCK, HEAD_DIM)
    return pl.pallas_call(
        whole_settle_kernel,
        grid=(4,),
        out_shape=jax.ShapeDtypeStruct(summed.shape, summed.dtype),
        in_specs=[
            pl.BlockSpec(one, lambda at: (at, 0, 0, 0)),
            pl.BlockSpec(one, lambda at: (jnp.minimum(at, 1), 0, 0, 0)),
            pl.BlockSpec(one, lambda at: (jnp.maximum(at - 2, 0), 0, 0, 0)),
        ]
        + [ANYWHERE] * (1 + len(after)),
        out_specs=pl.BlockSpec(
            one, lambda at: (jnp.where(at < 2, at, MEMBERS - 4 + at), 0, 0, 0)
        ),
        input_output_aliases={3: 0},
        compiler_params=pltpu.CompilerParams(vmem_limit_bytes=VMEM_LIMIT),
        cost_estimate=cost(3),
        name="whole_settle",
    )(near, below, above, summed, *after)


def gather_split_kernel(place, *refs):
    pieces, outs, sem = refs[:GROUP], refs[GROUP:-1], refs[-1]
    here = place[0] & (GROUP - 1)
    copies = []
    for away, piece in enumerate(pieces):
        start = (SHARE * (here ^ away) + CORES) * HEAD_DIM
        columns = pl.ds(pl.multiple_of(start, HEAD_DIM), HEAD_DIM)
        for index, out in enumerate(outs):
            copies.append((piece.at[index], out.at[:, columns]))
    copy_all(copies, sem)


def gather_split(place, pieces):
    return pl.pallas_call(
        gather_split_kernel,
        out_shape=[jax.ShapeDtypeStruct((BLOCK, HEADS * HEAD_DIM), jnp.bfloat16)] * 3,
        in_specs=[SCALARS] + [FAST] * GROUP,
        out_specs=[ANYWHERE] * 3,
        scratch_shapes=[pltpu.SemaphoreType.DMA((3 * GROUP,))],
        compiler_params=pltpu.CompilerParams(vmem_limit_bytes=VMEM_LIMIT),
        cost_estimate=cost(3),
        name="gather_split",
    )(place, *pieces)


def gather_kernel(columns, count, *refs):
    outs, sem = refs[-1 - count : -1], refs[-1]
    copies = []
    for at, head in enumerate(columns):
        for index in range(count):
            copies.append((refs[0].at[at, index], outs[index].at[:, head_columns(head)]))
    copy_all(copies, sem)


def gather(columns, pieces, so_far=()):
    count, kept = pieces.shape[1], len(so_far)
    return pl.pallas_call(
        functools.partial(gather_kernel, columns, count),
        out_shape=[jax.ShapeDtypeStruct((BLOCK, HEADS * HEAD_DIM), jnp.bfloat16)] * count,
        in_specs=[FAST] + [ANYWHERE] * kept,
        out_specs=[ANYWHERE] * count,
        scratch_shapes=[pltpu.SemaphoreType.DMA((count * len(columns),))],
        input_output_aliases={1 + at: at for at in range(kept)},
        compiler_params=pltpu.CompilerParams(vmem_limit_bytes=VMEM_LIMIT),
        cost_estimate=cost(3),
        name="gather",
    )(pieces, *so_far)


def shards(query_rows, key_rows, value_rows, out_grad, key_blocks, block_counts):
    chips = lax.axis_size("seq")
    chip = lax.axis_index("seq")
    core = lax.axis_index("head")
    place = jnp.stack([chip, core]).astype(jnp.int32)
    lists = key_blocks.reshape(-1)
    wide = [list(range(d, d + MEMBERS)) for d in range(0, CORES * chips, MEMBERS)]
    whole_heads = [SHARE * spot + at for spot in range(GROUP) for at in range(CORES)]

    def across(members):
        return [members[0]] + [
            lax.ppermute(members[away], "seq", [(c, c ^ away) for c in range(chips)])
            for away in range(1, GROUP)
        ]

    def regroup_wide(member):
        return lax.all_to_all(
            member, ("seq", "head"), split_axis=0, concat_axis=0, axis_index_groups=wide, tiled=True
        )

    def swap(member):
        return lax.ppermute(member, "head", [(0, 1), (1, 0)])

    def upward(member):
        return lax.ppermute(member, "seq", [(c, c + GROUP) for c in range(chips - GROUP)])

    def downward(member):
        return lax.ppermute(member, "seq", [(c + GROUP, c) for c in range(chips - GROUP)])

    def crosswise(member):
        pairs = [(2 * c + 1, 2 * (c + GROUP)) for c in range(chips - GROUP)]
        return lax.ppermute(member, ("seq", "head"), pairs + [(b, a) for a, b in pairs])

    sources = (key_rows, value_rows, query_rows, out_grad)
    split = across(pack_split(place, sources))
    keys, rows = pack(sources, whole_heads)
    keys = regroup_wide(keys)
    rows = regroup_wide(rows)
    ordered, low, high, cross = arrange(place, split, [])
    edges = [upward(high), downward(low), crosswise(cross)]
    queries, near, far, low, high, cross = split_grads(
        place, lists, block_counts, ordered, swap(ordered), edges, split, []
    )
    edges, far = [upward(high), downward(low), crosswise(cross)], swap(far)
    low, high = cut(
        place,
        keys,
        [lambda core: (0, 2, 2), lambda core: (MEMBERS - 2, 2, 2)],
        [],
    )
    whole_edges = [upward(high), downward(low)]
    split_done = split_settle(place, near, far, edges, queries, [])
    split_out = across(split_done)
    whole_queries, whole_sums, whole_near, low, high = whole_grads(
        place, lists, block_counts, keys, whole_edges, rows, []
    )
    below, above = upward(high), downward(low)
    whole_queries = regroup_wide(whole_queries)
    whole_sums = whole_settle(whole_near, below, above, whole_sums, [whole_queries])
    whole_out = regroup_wide(whole_sums)
    key_grad, value_grad, query_grad = gather_split(place, split_out)
    (query_grad,) = gather(whole_heads, whole_queries[:, None], (query_grad,))
    key_grad, value_grad = gather(whole_heads, whole_out, (key_grad, value_grad))
    return query_grad, key_grad, value_grad


def solution(mesh):
    rows = P(("seq", "head"), None)
    return jax.shard_map(
        shards,
        mesh=mesh,
        in_specs=(rows, rows, rows, rows, P(), P()),
        out_specs=(rows, rows, rows),
        check_vma=False,
    )
```

time: 208 us -> 185 us (0.89); the launches traced: 212 us -> 184 us
  blocking collectives: 41.8 us -> 0 us
  waiting for transfers between devices: 46.2 us -> 57.1 us
  starting transfers between devices: 45.8 us -> 52.2 us
  Pallas kernels: 68.8 us -> 64.6 us
  local copies, waits for them, and re-layouts: 5.21 us -> 8.41 us
    all_to_all x1 -> x0, blocking collectives: 41.8 us -> none  [regroup(): lax.all_to_all(member, 'seq', split_axis=0, concat_axis=0, axis_index_gro...]
    ppermute x0 -> x6, waiting for transfers between devices: none -> 16.8 us  [across(): lax.ppermute(members[away], 'seq', [(c, c ^ away) for c in range(chips)])]
    ppermute x0 -> x6, starting transfers between devices: none -> 8.03 us  [across(): lax.ppermute(members[away], 'seq', [(c, c ^ away) for c in range(chips)])]
    ppermute x3 -> x4, waiting for transfers between devices: 11.7 us -> 6.89 us  [downward(): lax.ppermute(member, 'seq', [(c + GROUP, c) for c in range(chips - GROUP)])]
    unnamed x27 -> x33, local copies, waits for them, and re-layouts: 3.12 us -> 7.71 us
    pallas_call x9 -> x11, Pallas kernels: 68.8 us -> 64.6 us  [the longest x1 22.1 us: whole_grads(): pl.pallas_call(functools.partial(whole_grads_kernel, len(after)), out_sha...]
    ppermute x3 -> x4, starting transfers between devices: 18.4 us -> 14.3 us  [upward(): lax.ppermute(member, 'seq', [(c, c + GROUP) for c in range(chips - GROUP)])]
    all_to_all x5 -> x4, waiting for transfers between devices: 28.5 us -> 31.2 us  [regroup_wide(): lax.all_to_all(member, ('seq', 'head'), split_axis=0, concat_axis=0, axis...]
  transfers between devices with their start and end apart: 17 -> 22, of which waited for: 8 -> 8; matrix products, arithmetic and copies ran while one was open for 2% -> 0% of each run, Pallas kernels for 27% -> 31%
where the time goes in v4:
time: 185 us; the launch traced here: 184 us
  Pallas kernels  64.6 us (35%)
  waiting for transfers between devices  57.1 us (31%)
  starting transfers between devices  52.2 us (28%)
  local copies, waits for them, and re-layouts  8.41 us (5%)
    all_to_all x4, waiting for transfers between devices, regroup_wide(): lax.all_to_all(member, ('seq', 'head'), split_axis=0, concat_axis=0, axis...  31.2 us
    pallas_call x1, Pallas kernels, whole_grads(): pl.pallas_call(functools.partial(whole_grads_kernel, len(after)), out_sha...  22.1 us
    all_to_all x4, starting transfers between devices, regroup_wide(): lax.all_to_all(member, ('seq', 'head'), split_axis=0, concat_axis=0, axis...  20.7 us
    ppermute x6, waiting for transfers between devices, across(): lax.ppermute(members[away], 'seq', [(c, c ^ away) for c in range(chips)])  16.8 us
    ppermute x4, starting transfers between devices, upward(): lax.ppermute(member, 'seq', [(c, c + GROUP) for c in range(chips - GROUP)])  14.3 us
    pallas_call x1, Pallas kernels, split_grads(): pl.pallas_call(functools.partial(split_grads_kernel, len(after)), out_sha...  12.4 us
    ppermute x6, starting transfers between devices, across(): lax.ppermute(members[away], 'seq', [(c, c ^ away) for c in range(chips)])  8.03 us
    unnamed x33, local copies, waits for them, and re-layouts  7.71 us
  transfers between devices with their start and end apart: 22, of which 8 were waited for; matrix products, arithmetic and copies ran while one was open for 0% of the time, Pallas kernels for 31%

profile of v4, /device:TPU:0, one launch (start us, length us, event | category | flops | bytes accessed | tf_op | source)
XLA Modules:
  0.0 184.1 jit_solution(6362252036502130414)
XLA Ops:
  1.3 3.8 %pack_split.1 = (bf16[4,512,128]{2,1,0:T(8,128)(2,1)}, bf16[4,512,128]{2,1,0:T(8,128)(2,1)}, bf16[4,512,128]{2,1,0:T(8,128)(2,1)}, bf16[4,512,128]{2,1,0:T(8,128)(2,1)}) custom-call(s32[2]{0:T(128)} %pad_add_fusion.place, bf16[512,1536]{1,0:T(8,128)(2,1)} %key_rows.1, bf16[512,1536]{1,0:T(8,128)(2,1)} %value_rows.1, bf16[512,1536]{1,0:T(8,128)(2,1)} %query_rows.1, ...), custom_call_target="tpu_custom_call" | custom-call | flops 13799999488 | bytes 36000000 | tf_op jit(solution)/shard_map/pack_split/pallas_call | solution.py:78
  5.1 3.0 %collective-permute-start.2 = (bf16[4,512,128]{2,1,0:T(8,128)(2,1)}, bf16[4,512,128]{2,1,0:T(8,128)(2,1)S(1)}, u32[]{:S(2)}, u32[]{:S(2)}) collective-permute-start(bf16[4,512,128]{2,1,0:T(8,128)(2,1)} %get-tuple-element.41), channel_id=1, source_target_pairs={{0,2},{2,0},{4,6},{6,4},{8,10},{10,8},{12,14},{14,12},{16,18},{18,... | collective-permute-start | bytes 1572872 | tf_op jit(solution)/shard_map/ppermute | solution.py:496
  8.1 1.5 collective-permute-start.3
  9.6 4.6 %pack.1 = (bf16[8,2,512,128]{3,2,1,0:T(8,128)(2,1)}, bf16[8,2,512,128]{3,2,1,0:T(8,128)(2,1)}) custom-call(bf16[512,1536]{1,0:T(8,128)(2,1)} %key_rows.1, bf16[512,1536]{1,0:T(8,128)(2,1)} %value_rows.1, bf16[512,1536]{1,0:T(8,128)(2,1)} %query_rows.1, bf16[512,1536]{1,0:T(8,128)(2,1)} %out_grad.1), custom_call_target="tpu_custom_call" | custom-call | flops 20700000256 | bytes 54000000 | tf_op jit(solution)/shard_map/pack/pallas_call | solution.py:102
  14.3 4.2 %all-to-all-start = ((bf16[8,2,512,128]{3,2,1,0:T(8,128)(2,1)}), bf16[8,2,512,128]{3,2,1,0:T(8,128)(2,1)S(1)}, u32[]{:S(2)}, u32[]{:S(2)}) async-start(bf16[8,2,512,128]{3,2,1,0:T(8,128)(2,1)} %get-tuple-element.35), calls=%async_computation | async-start | bytes 4194304 | tf_op jit(solution)/shard_map/all_to_all | solution.py:501
  18.4 2.6 %collective-permute-done.2.refs_1_.refs_6_ = bf16[4,512,128]{2,1,0:T(8,128)(2,1)S(1)} collective-permute-done((bf16[4,512,128]{2,1,0:T(8,128)(2,1)}, bf16[4,512,128]{2,1,0:T(8,128)(2,1)S(1)}, u32[]{:S(2)}, u32[]{:S(2)}) %collective-permute-start.2) | collective-permute-done | bytes 524320 | tf_op jit(solution)/shard_map/ppermute | solution.py:496
  21.1 12.5 %collective-permute-done.3.refs_2_.refs_7_ = bf16[4,512,128]{2,1,0:T(8,128)(2,1)S(1)} collective-permute-done((bf16[4,512,128]{2,1,0:T(8,128)(2,1)}, bf16[4,512,128]{2,1,0:T(8,128)(2,1)S(1)}, u32[]{:S(2)}, u32[]{:S(2)}) %collective-permute-start.3) | collective-permute-done | bytes 524320 | tf_op jit(solution)/shard_map/ppermute | solution.py:496
  34.3 3.2 %arrange.1 = (bf16[4,2,512,128]{3,2,1,0:T(8,128)(2,1)}, bf16[1,2,512,128]{3,2,1,0:T(8,128)(2,1)}, bf16[1,2,512,128]{3,2,1,0:T(8,128)(2,1)}, bf16[1,2,512,128]{3,2,1,0:T(8,128)(2,1)}) custom-call(s32[2]{0:T(128)} %pad_add_fusion.place, bf16[4,512,128]{2,1,0:T(8,128)(2,1)} %get-tuple-element.40.refs_0_.refs_5_, bf16[4,512,128]{2,1,0:T(8,128)(2,1)} %copy-done.6, ...), custom_call_target="tpu_custom_call" | custom-call | flops 8625000448 | bytes 22500000 | tf_op jit(solution)/shard_map/arrange/pallas_call | solution.py:134
  38.4 3.5 %collective-permute-start.6 = (bf16[1,2,512,128]{3,2,1,0:T(8,128)(2,1)}, bf16[1,2,512,128]{3,2,1,0:T(8,128)(2,1)S(1)}, u32[]{:S(2)}, u32[]{:S(2)}) collective-permute-start(bf16[1,2,512,128]{3,2,1,0:T(8,128)(2,1)} %get-tuple-element.45), channel_id=1, source_target_pairs={{0,8},{2,10},{4,12},{6,14},{8,16},{10,18},{12,20},{14,22},{16,24},... | collective-permute-start | bytes 786440 | tf_op jit(solution)/shard_map/ppermute | solution.py:509
  43.2 1.4 collective-permute-start.8
  44.6 10.8 %all-to-all-done.member.refs_0_ = bf16[8,2,512,128]{3,2,1,0:T(8,128)(2,1)S(1)} async-done(((bf16[8,2,512,128]{3,2,1,0:T(8,128)(2,1)}), bf16[8,2,512,128]{3,2,1,0:T(8,128)(2,1)S(1)}, u32[]{:S(2)}, u32[]{:S(2)}) %all-to-all-start) | async-done | bytes 2097184 | tf_op jit(solution)/shard_map/all_to_all | solution.py:501
  55.4 1.4 copy-done
  56.8 4.4 %all-to-all-start.1 = ((bf16[8,2,512,128]{3,2,1,0:T(8,128)(2,1)}), bf16[8,2,512,128]{3,2,1,0:T(8,128)(2,1)}, u32[]{:S(2)}, u32[]{:S(2)}) async-start(bf16[8,2,512,128]{3,2,1,0:T(8,128)(2,1)} %get-tuple-element.38), calls=%async_computation.1 | async-start | bytes 4194304 | tf_op jit(solution)/shard_map/all_to_all | solution.py:501
  61.2 2.9 %cut.1 = (bf16[2,2,512,128]{3,2,1,0:T(8,128)(2,1)}, bf16[2,2,512,128]{3,2,1,0:T(8,128)(2,1)}) custom-call(s32[2]{0:T(128)} %pad_add_fusion.place, bf16[8,2,512,128]{3,2,1,0:T(8,128)(2,1)} %copy-done), custom_call_target="tpu_custom_call" | custom-call | flops 5175000064 | bytes 13500000 | tf_op jit(solution)/shard_map/cut/pallas_call | solution.py:157
  64.0 3.5 %collective-permute-start = (bf16[2,2,512,128]{3,2,1,0:T(8,128)(2,1)}, bf16[2,2,512,128]{3,2,1,0:T(8,128)(2,1)S(1)}, u32[]{:S(2)}, u32[]{:S(2)}) collective-permute-start(bf16[2,2,512,128]{3,2,1,0:T(8,128)(2,1)} %get-tuple-element.36), channel_id=1, source_target_pairs={{0,8},{2,10},{4,12},{6,14},{8,16},{10,18},{12,20},{14,22},{16,24},... | collective-permute-start | bytes 1572872 | tf_op jit(solution)/shard_map/ppermute | solution.py:509
  69.9 12.4 %split_grads.1 = (bf16[4,512,128]{2,1,0:T(8,128)(2,1)}, f32[4,2,512,128]{3,2,1,0:T(8,128)}, bf16[4,2,512,128]{3,2,1,0:T(8,128)(2,1)}, bf16[1,2,512,128]{3,2,1,0:...) custom-call(s32[2]{0:T(128)} %pad_add_fusion.place, s32[96]{0:T(128)} %reshape.9.lists, ...), custom_call_target="tpu_custom_call" | custom-call | flops 44849999872 | bytes 117000000 | tf_op jit(solution)/shard_map/split_grads/pallas_call | solution.py:276
  83.5 4.4 %collective-permute-start.10 = (bf16[1,2,512,128]{3,2,1,0:T(8,128)(2,1)}, bf16[1,2,512,128]{3,2,1,0:T(8,128)(2,1)S(1)}, u32[]{:S(2)}, u32[]{:S(2)}) collective-permute-start(bf16[1,2,512,128]{3,2,1,0:T(8,128)(2,1)} %get-tuple-element.50), channel_id=1, source_target_pairs={{0,8},{2,10},{4,12},{6,14},{8,16},{10,18},{12,20},{14,22},{16,24},... | collective-permute-start | bytes 786440 | tf_op jit(solution)/shard_map/ppermute | solution.py:509
  89.2 1.4 collective-permute-start.12
  91.4 22.1 %whole_grads.1 = (bf16[8,512,128]{2,1,0:T(8,128)(2,1)}, bf16[8,2,512,128]{3,2,1,0:T(8,128)(2,1)}, f32[4,2,512,128]{3,2,1,0:T(8,128)}, bf16[2,2,512,128]{3,2,1,0:T(8,128)(2,1)}, bf16[2,2,512,128]{3,2,1,0:T(8,128)(2,1)}) custom-call(s32[2]{0:T(128)} %pad_add_fusion.place, s32[96]{0:T(128)} %reshape.9.lists, s32[32]{0:T(128)} %counts.3, ...), custom_call_target="tpu_custom_call" | custom-call | flops 75900002304 | bytes 198000000 | tf_op jit(solution)/shard_map/whole_grads/pallas_call | solution.py:348
  113.5 8.3 %all-to-all-start.2 = ((bf16[8,512,128]{2,1,0:T(8,128)(2,1)}), bf16[8,512,128]{2,1,0:T(8,128)(2,1)S(1)}, u32[]{:S(2)}, u32[]{:S(2)}) async-start(bf16[8,512,128]{2,1,0:T(8,128)(2,1)} %get-tuple-element.39), calls=%async_computation.2 | async-start | bytes 2097152 | tf_op jit(solution)/shard_map/all_to_all | solution.py:501
  121.9 2.9 %collective-permute-start.16 = (bf16[2,2,512,128]{3,2,1,0:T(8,128)(2,1)S(1)}, bf16[2,2,512,128]{3,2,1,0:T(8,128)(2,1)S(1)}, u32[]{:S(2)}, u32[]{:S(2)}) collective-permute-start(bf16[2,2,512,128]{3,2,1,0:T(8,128)(2,1)S(1)} %copy-done.11), channel_id=1, source_target_pairs={{0,8},{2,10},{4,12},{6,14},{8,16},{10,18},{12,20},{14,22},{16,24},... | collective-permute-start | bytes 1572872 | tf_op jit(solution)/shard_map/ppermute | solution.py:509
  127.1 3.8 %split_settle.1 = (bf16[3,512,128]{2,1,0:T(8,128)(2,1)}, bf16[3,512,128]{2,1,0:T(8,128)(2,1)}, bf16[3,512,128]{2,1,0:T(8,128)(2,1)}, bf16[3,512,128]{2,1,0:T(8,128)(2,1)}) custom-call(s32[2]{0:T(128)} %pad_add_fusion.place, f32[4,2,512,128]{3,2,1,0:T(8,128)} %get-tuple-element.48.near, bf16[4,2,512,128]{3,2,1,0:T(8,128)(2,1)} %copy-done.4, ...), custom_call_target="tpu_custom_call" | custom-call | flops 13799999488 | bytes 36000000 | tf_op jit(solution)/shard_map/split_settle/pallas_call | solution.py:390
  130.9 2.0 %collective-permute-start.13 = (bf16[3,512,128]{2,1,0:T(8,128)(2,1)}, bf16[3,512,128]{2,1,0:T(8,128)(2,1)S(1)}, u32[]{:S(2)}, u32[]{:S(2)}) collective-permute-start(bf16[3,512,128]{2,1,0:T(8,128)(2,1)} %get-tuple-element.55), channel_id=1, source_target_pairs={{0,2},{2,0},{4,6},{6,4},{8,10},{10,8},{12,14},{14,12},{16,18},{18,... | collective-permute-start | bytes 1179656 | tf_op jit(solution)/shard_map/ppermute | solution.py:496
  132.9 1.5 collective-permute-start.14
  134.4 2.1 %collective-permute-done.16.below = bf16[2,2,512,128]{3,2,1,0:T(8,128)(2,1)S(1)} collective-permute-done((bf16[2,2,512,128]{3,2,1,0:T(8,128)(2,1)S(1)}, bf16[2,2,512,128]{3,2,1,0:T(8,128)(2,1)S(1)}, u32[]{:S(2)}, u32[]{:S(2)}) %collective-permute-start.16) | collective-permute-done | bytes 524320 | tf_op jit(solution)/shard_map/ppermute | solution.py:509
  137.3 6.9 %collective-permute-done.17.above = bf16[2,2,512,128]{3,2,1,0:T(8,128)(2,1)} collective-permute-done((bf16[2,2,512,128]{3,2,1,0:T(8,128)(2,1)S(1)}, bf16[2,2,512,128]{3,2,1,0:T(8,128)(2,1)}, u32[]{:S(2)}, u32[]{:S(2)}) %collective-permute-start.17) | collective-permute-done | bytes 524320 | tf_op jit(solution)/shard_map/ppermute | solution.py:512
  145.2 3.8 %whole_settle.1 = bf16[8,2,512,128]{3,2,1,0:T(8,128)(2,1)} custom-call(f32[4,2,512,128]{3,2,1,0:T(8,128)} %get-tuple-element.59.near, bf16[2,2,512,128]{3,2,1,0:T(8,128)(2,1)} %copy-done.12, bf16[2,2,512,128]{3,2,1,0:T(8,128)(2,1)} %collective-permute-done.17.above, ...), custom_call_target="tpu_custom_call", output_to_operand_aliasing={{}: (3, {})} | custom-call | flops 10350000128 | bytes 27000000 | tf_op jit(solution)/shard_map/whole_settle/pallas_call | solution.py:416
  149.0 3.8 %all-to-all-start.3 = ((bf16[8,2,512,128]{3,2,1,0:T(8,128)(2,1)}), bf16[8,2,512,128]{3,2,1,0:T(8,128)(2,1)S(1)}, u32[]{:S(2)}, u32[]{:S(2)}) async-start(bf16[8,2,512,128]{3,2,1,0:T(8,128)(2,1)} %whole_settle.1), calls=%async_computation.3 | async-start | bytes 4194304 | tf_op jit(solution)/shard_map/all_to_all | solution.py:501
  154.2 2.6 %gather_split.1 = (bf16[512,1536]{1,0:T(8,128)(2,1)}, bf16[512,1536]{1,0:T(8,128)(2,1)}, bf16[512,1536]{1,0:T(8,128)(2,1)}) custom-call(s32[2]{0:T(128)} %pad_add_fusion.place, bf16[3,512,128]{2,1,0:T(8,128)(2,1)} %get-tuple-element.54.refs_0_, bf16[3,512,128]{2,1,0:T(8,128)(2,1)} %copy-done.13, bf16[3,512,128]{2,1,0:T(8,128)(2,1)} %collective-permute-done.14.refs_2_, ...), custom_call_target="tpu_custom_call" | custom-call | flops 10350000128 | bytes 27000000 | tf_op jit(solution)/shard_map/gather_split/pallas_call | solution.py:449
  156.8 2.3 %gather.2 = bf16[512,1536]{1,0:T(8,128)(2,1)} custom-call(bf16[8,1,512,128]{3,2,1,0:T(8,128)(2,1)} %bitcast.5, bf16[512,1536]{1,0:T(8,128)(2,1)} %get-tuple-element.58.refs_1_), custom_call_target="tpu_custom_call", output_to_operand_aliasing={{}: (1, {})} | custom-call | flops 10350000128 | bytes 27000000 | tf_op jit(solution)/shard_map/gather/pallas_call | solution.py:472
  159.1 20.4 %all-to-all-done.3.refs_0_ = bf16[8,2,512,128]{3,2,1,0:T(8,128)(2,1)S(1)} async-done(((bf16[8,2,512,128]{3,2,1,0:T(8,128)(2,1)}), bf16[8,2,512,128]{3,2,1,0:T(8,128)(2,1)S(1)}, u32[]{:S(2)}, u32[]{:S(2)}) %all-to-all-start.3) | async-done | bytes 2097184 | tf_op jit(solution)/shard_map/all_to_all | solution.py:501
  180.9 3.0 %gather.3 = (bf16[512,1536]{1,0:T(8,128)(2,1)}, bf16[512,1536]{1,0:T(8,128)(2,1)}) custom-call(bf16[8,2,512,128]{3,2,1,0:T(8,128)(2,1)} %copy-done.1, bf16[512,1536]{1,0:T(8,128)(2,1)} %get-tuple-element.63.refs_1_, bf16[512,1536]{1,0:T(8,128)(2,1)} %get-tuple-element.64.refs_2_), custom_call_target="tpu_custom_call", output_to_operand_aliasing={{0}: (1, {}), {1}: (2, {})} | custom-call | flops 10350000128 | bytes 27000000 | tf_op jit(solution)/shard_map/gather/pallas_call | solution.py:472
  (58 shorter events, 15.9 us)
Async XLA Ops:
  5.1 16.0 %collective-permute-start.2 = (bf16[4,512,128]{2,1,0:T(8,128)(2,1)}, bf16[4,512,128]{2,1,0:T(8,128)(2,1)S(1)}, u32[]{:S(2)}, u32[]{:S(2)}) collective-permute-start(bf16[4,512,128]{2,1,0:T(8,128)(2,1)} %get-tuple-element.41), channel_id=1, source_target_pairs={{0,2},{2,0},{4,6},{6,4},{8,10},{10,8},{12,14},{14,12},{16,18},{18,... | collective-permute-start | bytes 1572872 | tf_op jit(solution)/shard_map/ppermute | solution.py:496
  8.1 25.4 %collective-permute-start.3 = (bf16[4,512,128]{2,1,0:T(8,128)(2,1)}, bf16[4,512,128]{2,1,0:T(8,128)(2,1)S(1)}, u32[]{:S(2)}, u32[]{:S(2)}) collective-permute-start(bf16[4,512,128]{2,1,0:T(8,128)(2,1)} %get-tuple-element.42), channel_id=1, source_target_pairs={{0,4},{2,6},{4,0},{6,2},{8,12},{10,14},{12,8},{14,10},{16,20},{18,... | collective-permute-start | bytes 1572872 | tf_op jit(solution)/shard_map/ppermute | solution.py:496
  9.6 24.4 %collective-permute-start.4 = (bf16[4,512,128]{2,1,0:T(8,128)(2,1)}, bf16[4,512,128]{2,1,0:T(8,128)(2,1)}, u32[]{:S(2)}, u32[]{:S(2)}) collective-permute-start(bf16[4,512,128]{2,1,0:T(8,128)(2,1)} %get-tuple-element.43), channel_id=1, source_target_pairs={{0,6},{2,4},{4,2},{6,0},{8,14},{10,12},{12,10},{14,8},{16,22},{18,... | collective-permute-start | bytes 1572872 | tf_op jit(solution)/shard_map/ppermute | solution.py:496
  14.3 41.1 %all-to-all-start = ((bf16[8,2,512,128]{3,2,1,0:T(8,128)(2,1)}), bf16[8,2,512,128]{3,2,1,0:T(8,128)(2,1)S(1)}, u32[]{:S(2)}, u32[]{:S(2)}) async-start(bf16[8,2,512,128]{3,2,1,0:T(8,128)(2,1)} %get-tuple-element.35), calls=%async_computation | async-start | bytes 4194304 | tf_op jit(solution)/shard_map/all_to_all | solution.py:501
  21.1 12.9 %copy-start.6 = (bf16[4,512,128]{2,1,0:T(8,128)(2,1)}, bf16[4,512,128]{2,1,0:T(8,128)(2,1)S(1)}, u32[]{:S(2)}) copy-start(bf16[4,512,128]{2,1,0:T(8,128)(2,1)S(1)} %collective-permute-done.2.refs_1_.refs_6_) | copy-start | bytes 1572868
  34.3 3.3 %copy-start.3 = (s32[32,3]{0,1:T(4,128)S(1)}, s32[32,3]{0,1:T(4,128)}, u32[]{:S(2)}) copy-start(s32[32,3]{0,1:T(4,128)} %param.10) | copy-start | bytes 1156
  37.6 31.4 %collective-permute-start.5 = (bf16[4,2,512,128]{3,2,1,0:T(8,128)(2,1)}, bf16[4,2,512,128]{3,2,1,0:T(8,128)(2,1)S(1)}, u32[]{:S(2)}, u32[]{:S(2)}) collective-permute-start(bf16[4,2,512,128]{3,2,1,0:T(8,128)(2,1)} %get-tuple-element.44.refs_0_), channel_id=1, source_target_pairs={{0,1},{1,0},{2,3},{3,2},{4,5},{5,4},{6,7},{7,6},{8,9},{9,8},{10,11... | collective-permute-start | bytes 3145736 | tf_op jit(solution)/shard_map/ppermute | solution.py:506
  38.4 29.1 %collective-permute-start.6 = (bf16[1,2,512,128]{3,2,1,0:T(8,128)(2,1)}, bf16[1,2,512,128]{3,2,1,0:T(8,128)(2,1)S(1)}, u32[]{:S(2)}, u32[]{:S(2)}) collective-permute-start(bf16[1,2,512,128]{3,2,1,0:T(8,128)(2,1)} %get-tuple-element.45), channel_id=1, source_target_pairs={{0,8},{2,10},{4,12},{6,14},{8,16},{10,18},{12,20},{14,22},{16,24},... | collective-permute-start | bytes 786440 | tf_op jit(solution)/shard_map/ppermute | solution.py:509
  41.9 27.0 %collective-permute-start.7 = (bf16[1,2,512,128]{3,2,1,0:T(8,128)(2,1)}, bf16[1,2,512,128]{3,2,1,0:T(8,128)(2,1)}, u32[]{:S(2)}, u32[]{:S(2)}) collective-permute-start(bf16[1,2,512,128]{3,2,1,0:T(8,128)(2,1)} %get-tuple-element.46), channel_id=1, source_target_pairs={{8,0},{10,2},{12,4},{14,6},{16,8},{18,10},{20,12},{22,14},{24,16},... | collective-permute-start | bytes 786440 | tf_op jit(solution)/shard_map/ppermute | solution.py:512
  43.2 25.7 %collective-permute-start.8 = (bf16[1,2,512,128]{3,2,1,0:T(8,128)(2,1)}, bf16[1,2,512,128]{3,2,1,0:T(8,128)(2,1)}, u32[]{:S(2)}, u32[]{:S(2)}) collective-permute-start(bf16[1,2,512,128]{3,2,1,0:T(8,128)(2,1)} %get-tuple-element.47), channel_id=1, source_target_pairs={{1,8},{3,10},{5,12},{7,14},{9,16},{11,18},{13,20},{15,22},{17,24},... | collective-permute-start | bytes 786440 | tf_op jit(solution)/shard_map/ppermute | solution.py:516
  55.4 1.4 copy-start
  56.8 33.8 %all-to-all-start.1 = ((bf16[8,2,512,128]{3,2,1,0:T(8,128)(2,1)}), bf16[8,2,512,128]{3,2,1,0:T(8,128)(2,1)}, u32[]{:S(2)}, u32[]{:S(2)}) async-start(bf16[8,2,512,128]{3,2,1,0:T(8,128)(2,1)} %get-tuple-element.38), calls=%async_computation.1 | async-start | bytes 4194304 | tf_op jit(solution)/shard_map/all_to_all | solution.py:501
  64.0 25.2 %collective-permute-start = (bf16[2,2,512,128]{3,2,1,0:T(8,128)(2,1)}, bf16[2,2,512,128]{3,2,1,0:T(8,128)(2,1)S(1)}, u32[]{:S(2)}, u32[]{:S(2)}) collective-permute-start(bf16[2,2,512,128]{3,2,1,0:T(8,128)(2,1)} %get-tuple-element.36), channel_id=1, source_target_pairs={{0,8},{2,10},{4,12},{6,14},{8,16},{10,18},{12,20},{14,22},{16,24},... | collective-permute-start | bytes 1572872 | tf_op jit(solution)/shard_map/ppermute | solution.py:509
  67.6 1.3 copy-start.15
  67.6 23.0 %collective-permute-start.1 = (bf16[2,2,512,128]{3,2,1,0:T(8,128)(2,1)}, bf16[2,2,512,128]{3,2,1,0:T(8,128)(2,1)S(1)}, u32[]{:S(2)}, u32[]{:S(2)}) collective-permute-start(bf16[2,2,512,128]{3,2,1,0:T(8,128)(2,1)} %get-tuple-element.37), channel_id=1, source_target_pairs={{8,0},{10,2},{12,4},{14,6},{16,8},{18,10},{20,12},{22,14},{24,16},... | collective-permute-start | bytes 1572872 | tf_op jit(solution)/shard_map/ppermute | solution.py:512
  82.4 43.7 %collective-permute-start.9 = (bf16[4,2,512,128]{3,2,1,0:T(8,128)(2,1)}, bf16[4,2,512,128]{3,2,1,0:T(8,128)(2,1)S(1)}, u32[]{:S(2)}, u32[]{:S(2)}) collective-permute-start(bf16[4,2,512,128]{3,2,1,0:T(8,128)(2,1)} %get-tuple-element.49), channel_id=1, source_target_pairs={{0,1},{1,0},{2,3},{3,2},{4,5},{5,4},{6,7},{7,6},{8,9},{9,8},{10,11... | collective-permute-start | bytes 3145736 | tf_op jit(solution)/shard_map/ppermute | solution.py:506
  83.5 41.2 %collective-permute-start.10 = (bf16[1,2,512,128]{3,2,1,0:T(8,128)(2,1)}, bf16[1,2,512,128]{3,2,1,0:T(8,128)(2,1)S(1)}, u32[]{:S(2)}, u32[]{:S(2)}) collective-permute-start(bf16[1,2,512,128]{3,2,1,0:T(8,128)(2,1)} %get-tuple-element.50), channel_id=1, source_target_pairs={{0,8},{2,10},{4,12},{6,14},{8,16},{10,18},{12,20},{14,22},{16,24},... | collective-permute-start | bytes 786440 | tf_op jit(solution)/shard_map/ppermute | solution.py:509
  87.9 38.2 %collective-permute-start.11 = (bf16[1,2,512,128]{3,2,1,0:T(8,128)(2,1)}, bf16[1,2,512,128]{3,2,1,0:T(8,128)(2,1)}, u32[]{:S(2)}, u32[]{:S(2)}) collective-permute-start(bf16[1,2,512,128]{3,2,1,0:T(8,128)(2,1)} %get-tuple-element.51), channel_id=1, source_target_pairs={{8,0},{10,2},{12,4},{14,6},{16,8},{18,10},{20,12},{22,14},{24,16},... | collective-permute-start | bytes 786440 | tf_op jit(solution)/shard_map/ppermute | solution.py:512
  89.2 1.4 copy-start.8
  89.2 36.8 %collective-permute-start.12 = (bf16[1,2,512,128]{3,2,1,0:T(8,128)(2,1)}, bf16[1,2,512,128]{3,2,1,0:T(8,128)(2,1)}, u32[]{:S(2)}, u32[]{:S(2)}) collective-permute-start(bf16[1,2,512,128]{3,2,1,0:T(8,128)(2,1)} %get-tuple-element.52), channel_id=1, source_target_pairs={{1,8},{3,10},{5,12},{7,14},{9,16},{11,18},{13,20},{15,22},{17,24},... | collective-permute-start | bytes 786440 | tf_op jit(solution)/shard_map/ppermute | solution.py:516
  113.5 8.3 %copy-start.11 = (bf16[2,2,512,128]{3,2,1,0:T(8,128)(2,1)S(1)}, bf16[2,2,512,128]{3,2,1,0:T(8,128)(2,1)}, u32[]{:S(2)}) copy-start(bf16[2,2,512,128]{3,2,1,0:T(8,128)(2,1)} %get-tuple-element.60) | copy-start | bytes 1572868
  113.5 11.2 %copy-start.10 = (bf16[2,2,512,128]{3,2,1,0:T(8,128)(2,1)S(1)}, bf16[2,2,512,128]{3,2,1,0:T(8,128)(2,1)}, u32[]{:S(2)}) copy-start(bf16[2,2,512,128]{3,2,1,0:T(8,128)(2,1)} %get-tuple-element.61) | copy-start | bytes 1572868
  113.5 30.7 %all-to-all-start.2 = ((bf16[8,512,128]{2,1,0:T(8,128)(2,1)}), bf16[8,512,128]{2,1,0:T(8,128)(2,1)S(1)}, u32[]{:S(2)}, u32[]{:S(2)}) async-start(bf16[8,512,128]{2,1,0:T(8,128)(2,1)} %get-tuple-element.39), calls=%async_computation.2 | async-start | bytes 2097152 | tf_op jit(solution)/shard_map/all_to_all | solution.py:501
  121.9 14.7 %collective-permute-start.16 = (bf16[2,2,512,128]{3,2,1,0:T(8,128)(2,1)S(1)}, bf16[2,2,512,128]{3,2,1,0:T(8,128)(2,1)S(1)}, u32[]{:S(2)}, u32[]{:S(2)}) collective-permute-start(bf16[2,2,512,128]{3,2,1,0:T(8,128)(2,1)S(1)} %copy-done.11), channel_id=1, source_target_pairs={{0,8},{2,10},{4,12},{6,14},{8,16},{10,18},{12,20},{14,22},{16,24},... | collective-permute-start | bytes 1572872 | tf_op jit(solution)/shard_map/ppermute | solution.py:509
  124.7 1.4 copy-start.14
  124.8 19.4 %collective-permute-start.17 = (bf16[2,2,512,128]{3,2,1,0:T(8,128)(2,1)S(1)}, bf16[2,2,512,128]{3,2,1,0:T(8,128)(2,1)}, u32[]{:S(2)}, u32[]{:S(2)}) collective-permute-start(bf16[2,2,512,128]{3,2,1,0:T(8,128)(2,1)S(1)} %copy-done.10), channel_id=1, source_target_pairs={{8,0},{10,2},{12,4},{14,6},{16,8},{18,10},{20,12},{22,14},{24,16},... | collective-permute-start | bytes 1572872 | tf_op jit(solution)/shard_map/ppermute | solution.py:512
  130.9 22.0 %collective-permute-start.13 = (bf16[3,512,128]{2,1,0:T(8,128)(2,1)}, bf16[3,512,128]{2,1,0:T(8,128)(2,1)S(1)}, u32[]{:S(2)}, u32[]{:S(2)}) collective-permute-start(bf16[3,512,128]{2,1,0:T(8,128)(2,1)} %get-tuple-element.55), channel_id=1, source_target_pairs={{0,2},{2,0},{4,6},{6,4},{8,10},{10,8},{12,14},{14,12},{16,18},{18,... | collective-permute-start | bytes 1179656 | tf_op jit(solution)/shard_map/ppermute | solution.py:496
  132.9 20.0 %collective-permute-start.14 = (bf16[3,512,128]{2,1,0:T(8,128)(2,1)}, bf16[3,512,128]{2,1,0:T(8,128)(2,1)}, u32[]{:S(2)}, u32[]{:S(2)}) collective-permute-start(bf16[3,512,128]{2,1,0:T(8,128)(2,1)} %get-tuple-element.56), channel_id=1, source_target_pairs={{0,4},{2,6},{4,0},{6,2},{8,12},{10,14},{12,8},{14,10},{16,20},{18,... | collective-permute-start | bytes 1179656 | tf_op jit(solution)/shard_map/ppermute | solution.py:496
  134.4 19.9 %collective-permute-start.15 = (bf16[3,512,128]{2,1,0:T(8,128)(2,1)}, bf16[3,512,128]{2,1,0:T(8,128)(2,1)}, u32[]{:S(2)}, u32[]{:S(2)}) collective-permute-start(bf16[3,512,128]{2,1,0:T(8,128)(2,1)} %get-tuple-element.57), channel_id=1, source_target_pairs={{0,6},{2,4},{4,2},{6,0},{8,14},{10,12},{12,10},{14,8},{16,22},{18,... | collective-permute-start | bytes 1179656 | tf_op jit(solution)/shard_map/ppermute | solution.py:496
  149.0 30.5 %all-to-all-start.3 = ((bf16[8,2,512,128]{3,2,1,0:T(8,128)(2,1)}), bf16[8,2,512,128]{3,2,1,0:T(8,128)(2,1)S(1)}, u32[]{:S(2)}, u32[]{:S(2)}) async-start(bf16[8,2,512,128]{3,2,1,0:T(8,128)(2,1)} %whole_settle.1), calls=%async_computation.3 | async-start | bytes 4194304 | tf_op jit(solution)/shard_map/all_to_all | solution.py:501
  152.9 1.3 copy-start.13
  179.5 1.3 copy-start.1
  (6 other events, 5.3 us)
